TPU v7x, 512 devices: a whole 4x8x8 slice. The times are simulated.
512 devices in a mesh: cell: 128 (over y, z, core), img: 4 (over x).
Axes of the slice: x: 4, y: 8, z: 8, core: 2. Of those that a mesh axis runs over, the one named last changes fastest.
Arguments:
- proj: float32 [4, 6, 1048576], P('img', None, 'cell'), as said below
- sh_coeffs: float32 [48, 1048576], P(None, 'cell'), may hold values from -2 to 2
- positions: float32 [3, 1048576], P(None, 'cell'), may hold values from -2 to 2
- camera: float32 [4, 3], P('img'), as said below
- send_index: int32 [4, 524288], P('img', 'cell'), may hold values from 0 to 8191
- send_count: int32 [4, 16384], P('img', 'cell'), may hold values from 1 to 32, as said below
- tile_xy: int32 [4, 2, 512], P('img', None, 'cell'), may hold values from 0 to 31
- tile_list: int32 [4, 512, 256], P('img', 'cell'), may hold values from 0 to 4095, as said below
- tile_len: int32 [4, 512], P('img', 'cell'), may hold values from 1 to 256, as said below
- pixel_grad: float32 [4, 3, 131072], P('img', None, 'cell'), may hold values from -6 to 6
Outputs:
- grad_proj: float32 [4, 6, 1048576], P('img', None, 'cell')
- grad_sh: float32 [48, 1048576], P(None, ('cell', 'img'))
Inputs may be any that keep to these rules, and one draw needn't show every extreme that they name: `send_count`: for every image and owner, some renderer receives exactly 32 live slots from it. `tile_list`: an entry p * 32 + q of a tile's list always has q below send_count of owner p toward that tile's renderer. `tile_len`: every image has a tile with 256 live entries. `proj`: means lie in 0 to 4, the conic is positive definite with a and c from 0.2 to 13, opacity lies in 0.002 to 0.06. `camera`: camera heights lie in 6 to 10, other coordinates in -2 to 2.
All inputs are finite; a program needn't handle non-finite values.
Results may differ from a plain program's by a relative error of at most 0.0003.
Values sent between devices are 32-bit elements; how exact they have to be, the bound alone decides.
No kernel may reach another device: no remote copies, remote signals or barrier semaphores. Data moves between devices by JAX's collectives and lax.ppermute only.
A program may use at most 64 MiB of HBM per device.

v0:
```python
import jax
import jax.numpy as jnp
from jax import lax
from jax.sharding import PartitionSpec as P

SH_ZERO = 0.28209479177387814
SH_ONE = 0.4886025119029199
SH_TWO = (
    1.0925484305920792,
    -1.0925484305920792,
    0.31539156525252005,
    -1.0925484305920792,
    0.5462742152960396,
)
SH_THREE = (
    -0.5900435899266435,
    2.890611442640554,
    -0.4570457994644658,
    0.3731763325901154,
    -0.4570457994644658,
    1.445305721320277,
    -0.5900435899266435,
)


def sh_basis(positions, centre):
    offset = positions - centre[:, None]
    length = jnp.sqrt(jnp.sum(offset * offset, axis=0))
    xpos = offset[0] / length
    ypos = offset[1] / length
    zpos = offset[2] / length
    xsq = xpos * xpos
    ysq = ypos * ypos
    zsq = zpos * zpos
    terms = [
        jnp.full_like(xpos, SH_ZERO),
        -SH_ONE * ypos,
        SH_ONE * zpos,
        -SH_ONE * xpos,
        SH_TWO[0] * xpos * ypos,
        SH_TWO[1] * ypos * zpos,
        SH_TWO[2] * (2.0 * zsq - xsq - ysq),
        SH_TWO[3] * xpos * zpos,
        SH_TWO[4] * (xsq - ysq),
        SH_THREE[0] * ypos * (3.0 * xsq - ysq),
        SH_THREE[1] * xpos * ypos * zpos,
        SH_THREE[2] * ypos * (4.0 * zsq - xsq - ysq),
        SH_THREE[3] * zpos * (2.0 * zsq - 3.0 * xsq - 3.0 * ysq),
        SH_THREE[4] * xpos * (4.0 * zsq - xsq - ysq),
        SH_THREE[5] * zpos * (xsq - ysq),
        SH_THREE[6] * xpos * (xsq - 3.0 * ysq),
    ]
    return jnp.stack(terms, axis=0)


def shade(coeffs, basis):
    return (
        jnp.stack(
            [jnp.sum(coeffs[16 * chan : 16 * chan + 16] * basis, axis=0) for chan in range(3)],
            axis=0,
        )
        + 0.5
    )


def pixel_coords(tile_col, tile_row):
    local = jnp.arange(256, dtype=jnp.int32)
    upos = (tile_col.astype(jnp.float32) * 16.0 + (local % 16).astype(jnp.float32) + 0.5) / 128.0
    vpos = (tile_row.astype(jnp.float32) * 16.0 + (local // 16).astype(jnp.float32) + 0.5) / 128.0
    return (upos, vpos)


def render_tile(rows, livemask, upos, vpos):
    depth = rows.shape[1]
    delta_x = upos[:, None] - rows[0][None, :]
    delta_y = vpos[:, None] - rows[1][None, :]
    power = (
        -0.5 * (rows[2] * delta_x * delta_x + rows[4] * delta_y * delta_y)
        - rows[3] * delta_x * delta_y
    )
    alpha = rows[5] * jnp.exp(power) * livemask
    order = jnp.arange(depth, dtype=jnp.int32)
    upper = (order[:, None] < order[None, :]).astype(jnp.float32)
    log_trans = jnp.dot(
        jnp.log1p(-alpha),
        upper,
        precision=lax.Precision.HIGHEST,
        preferred_element_type=jnp.float32,
    )
    weight = alpha * jnp.exp(log_trans)
    return jnp.dot(
        rows[6:9], weight.T, precision=lax.Precision.HIGHEST, preferred_element_type=jnp.float32
    )


def tile_grad(rows, livemask, upos, vpos, cotangent):
    _, pullback = jax.vjp(lambda values: render_tile(values, livemask, upos, vpos), rows)
    return pullback(cotangent)[0]


def render_slots(rows, tile_xy, tile_list, tile_len, pixel_grad):
    tiles = tile_list.shape[1]
    depth = tile_list.shape[2]
    pixels = pixel_grad.shape[2] // tiles
    order = jnp.arange(depth, dtype=jnp.int32)

    def one_tile(tile):
        slots = tile_list[0, tile]
        gathered = rows[:, slots]
        livemask = (order < tile_len[0, tile]).astype(jnp.float32)
        upos, vpos = pixel_coords(tile_xy[0, 0, tile], tile_xy[0, 1, tile])
        cotangent = lax.dynamic_slice_in_dim(pixel_grad[0], tile * pixels, pixels, 1)
        return tile_grad(gathered, livemask, upos, vpos, cotangent)

    grads = lax.map(one_tile, jnp.arange(tiles, dtype=jnp.int32))
    flat = jnp.transpose(grads, (1, 0, 2)).reshape(9, tiles * depth)
    return jnp.zeros((9, rows.shape[1]), jnp.float32).at[:, tile_list[0].reshape(-1)].add(flat)


def on_device(
    proj,
    sh_coeffs,
    positions,
    camera,
    send_index,
    send_count,
    tile_xy,
    tile_list,
    tile_len,
    pixel_grad,
):
    peers = lax.axis_size("cell")
    slots = send_index.shape[1]
    width = slots // peers
    gauss = sh_coeffs.shape[1]
    slot_ids = jnp.arange(slots, dtype=jnp.int32)
    live = (slot_ids % width < jnp.repeat(send_count[0], width)).astype(jnp.float32)
    local = send_index[0]
    basis = sh_basis(positions, camera[0])
    rows = jnp.concatenate([proj[0], shade(sh_coeffs, basis)], axis=0)
    outgoing = rows[:, local] * live[None, :]
    received = lax.all_to_all(outgoing, "cell", split_axis=1, concat_axis=1, tiled=True)
    slot_grads = render_slots(received, tile_xy, tile_list, tile_len, pixel_grad)
    returned = lax.all_to_all(slot_grads, "cell", split_axis=1, concat_axis=1, tiled=True)
    summed = jnp.zeros((9, gauss), jnp.float32).at[:, local].add(returned * live[None, :])
    grad_rows = summed[:6]
    coeff_grad = (summed[6:9][:, None, :] * basis[None, :, :]).reshape(48, gauss)
    grad_sh = lax.psum_scatter(coeff_grad, "img", scatter_dimension=1, tiled=True)
    return (grad_rows[None], grad_sh)


def solution(mesh):
    return jax.shard_map(
        on_device,
        mesh=mesh,
        in_specs=(
            P("img", None, "cell"),
            P(None, "cell"),
            P(None, "cell"),
            P("img", None),
            P("img", "cell"),
            P("img", "cell"),
            P("img", None, "cell"),
            P("img", "cell", None),
            P("img", "cell"),
            P("img", None, "cell"),
        ),
        out_specs=(P("img", None, "cell"), P(None, ("cell", "img"))),
        check_vma=False,
    )
```

profile of v0, /device:TPU:8, one launch (start us, length us, event | category | flops | bytes accessed | tf_op | source)
XLA Modules:
  0.0 217.2 jit_solution(18237825300634950310)
XLA Ops:
  7.2 0.9 compare_select_fusion.1
  8.0 0.7 fusion.61
  8.8 1.1 multiply_reduce_fusion.4
  9.9 1.1 copy.56
  11.7 0.8 stack.10
  13.0 2.6 %copy.30 = f32[9,8192]{0,1:T(8,128)} copy(f32[9,8192]{1,0:T(8,128)S(1)} %pad_maximum_fusion) | data formatting | bytes 589824 | tf_op jit(solution)/shard_map/concatenate | solution.py:140
  15.6 16.3 %gather_fusion.1 = f32[4096,9]{1,0:T(8,128)} fusion(f32[9,8192]{0,1:T(8,128)} %copy.30, s32[4096]{0:T(1024)S(1)} %broadcast_clamp_fusion), kind=kCustom, calls=%fused_computation.1 | custom fusion | bytes 311296 | tf_op jit(solution)/shard_map/gather | solution.py:141
  31.9 2.4 %copy.31 = f32[9,128,32]{2,0,1:T(8,128)S(1)} copy(f32[9,128,32]{0,2,1:T(8,128)} %bitcast.101) | data formatting | bytes 294912 | tf_op jit(solution)/shard_map/gather | solution.py:141
  34.4 1.2 reshape.311
  35.6 17.4 %all-to-all-start = ((f32[128,1,288]{2,1,0:T(1,128)}), f32[128,1,288]{2,1,0:T(1,128)S(1)}, u32[]{:S(2)}, u32[]{:S(2)}) async-start(f32[128,1,288]{2,1,0:T(1,128)} %reshape.311), calls=%async_computation | async-start | bytes 393216 | tf_op jit(solution)/shard_map/all_to_all | solution.py:142
  53.0 13.3 %all-to-all-done = f32[128,1,288]{2,1,0:T(1,128)S(1)} async-done(((f32[128,1,288]{2,1,0:T(1,128)}), f32[128,1,288]{2,1,0:T(1,128)S(1)}, u32[]{:S(2)}, u32[]{:S(2)}) %all-to-all-start) | async-done | bytes 147488 | tf_op jit(solution)/shard_map/all_to_all | solution.py:142
  66.3 0.5 broadcast.400
  66.9 1.1 reduce.12
  68.2 2.2 %copy.41 = f32[9,128,32]{0,2,1:T(8,128)} copy(f32[9,128,32]{2,0,1:T(8,128)S(1)} %bitcast.97) | data formatting | bytes 294912
  70.4 48.6 %while.13 = (s32[]{:T(128)}, f32[4,9,256]{2,1,0:T(8,128)S(1)}, s32[4]{0:T(128)S(1)}, f32[1,3,1024]{2,0,1:T(1,128)}, s32[1,4,256]{2,1,0:T(4,128)S(1)}, /*index=5*...) while((s32[]{:T(128)}, f32[4,9,256]{2,1,0:T(8,128)S(1)}, ...), condition=%wide.region_11.12_spmd.clone, body=%wide.region_4.11_spmd.clone.sunk | while | flops 413421312 | bytes 1442121 | solution.py:115
  70.4 0.6 dynamic_slice.61
  73.6 0.6 constant_dynamic-slice_fusion.9
  74.1 0.6 compare_convert_fusion.2
  74.8 0.6 constant_dynamic-slice_fusion.8
  76.7 0.7 constant_dynamic-slice_fusion.10
  77.4 2.3 %gather_fusion = f32[256,9]{1,0:T(8,128)S(1)} fusion(f32[9,4096]{0,1:T(8,128)} %get-tuple-element.327, s32[1024]{0:T(1024)S(1)} %pad_clamp_fusion.2), kind=kCustom, calls=%fused_computation.clone.clone.1 | custom fusion | bytes 19456 | tf_op jit(solution)/shard_map/while/body/eval_jaxpr/gather | solution.py:109
  79.7 0.5 slice_reduce_fusion.7
  80.7 0.5 convolution_exponential_fusion.2
  81.2 0.8 fusion.85
  82.5 0.6 dynamic_slice.61
  85.7 0.6 constant_dynamic-slice_fusion.9
  86.3 0.6 compare_convert_fusion.2
  87.0 0.6 constant_dynamic-slice_fusion.8
  88.9 0.7 constant_dynamic-slice_fusion.10
  89.6 2.3 %gather_fusion = f32[256,9]{1,0:T(8,128)S(1)} fusion(f32[9,4096]{0,1:T(8,128)} %get-tuple-element.327, s32[1024]{0:T(1024)S(1)} %pad_clamp_fusion.2), kind=kCustom, calls=%fused_computation.clone.clone.1 | custom fusion | bytes 19456 | tf_op jit(solution)/shard_map/while/body/eval_jaxpr/gather | solution.py:109
  91.9 0.5 slice_reduce_fusion.7
  92.8 0.5 convolution_exponential_fusion.2
  93.4 0.8 fusion.85
  94.7 0.6 dynamic_slice.61
  97.9 0.6 constant_dynamic-slice_fusion.9
  98.4 0.6 compare_convert_fusion.2
  99.1 0.6 constant_dynamic-slice_fusion.8
  101.0 0.7 constant_dynamic-slice_fusion.10
  101.7 2.3 %gather_fusion = f32[256,9]{1,0:T(8,128)S(1)} fusion(f32[9,4096]{0,1:T(8,128)} %get-tuple-element.327, s32[1024]{0:T(1024)S(1)} %pad_clamp_fusion.2), kind=kCustom, calls=%fused_computation.clone.clone.1 | custom fusion | bytes 19456 | tf_op jit(solution)/shard_map/while/body/eval_jaxpr/gather | solution.py:109
  105.0 0.5 convolution_exponential_fusion.2
  105.5 0.8 fusion.85
  106.8 0.6 dynamic_slice.61
  110.0 0.6 constant_dynamic-slice_fusion.9
  110.6 0.6 compare_convert_fusion.2
  111.3 0.6 constant_dynamic-slice_fusion.8
  113.2 0.7 constant_dynamic-slice_fusion.10
  113.9 2.3 %gather_fusion = f32[256,9]{1,0:T(8,128)S(1)} fusion(f32[9,4096]{0,1:T(8,128)} %get-tuple-element.327, s32[1024]{0:T(1024)S(1)} %pad_clamp_fusion.2), kind=kCustom, calls=%fused_computation.clone.clone.1 | custom fusion | bytes 19456 | tf_op jit(solution)/shard_map/while/body/eval_jaxpr/gather | solution.py:109
  116.2 0.5 slice_reduce_fusion.7
  117.1 0.5 convolution_exponential_fusion.2
  117.7 0.8 fusion.85
  119.3 6.5 %scatter_custom_fusion = f32[9,4096]{0,1:T(8,128)S(1)} fusion(s32[1024]{0:T(1024)S(1)} %bitcast.123, f32[1024,9]{1,0:T(8,128)S(1)} %copy.35, f32[]{:T(128)} %constant.150.clone.1), kind=kCustom, calls=%fused_computation.95 | custom fusion | flops 9216 | bytes 147460 | tf_op jit(solution)/shard_map/scatter-add | solution.py:117
  125.8 1.8 copy.36
  127.7 2.3 %reshape.313 = f32[128,1,288]{2,1,0:T(1,128)} reshape(f32[128,9,32]{2,1,0:T(8,128)} %bitcast.98) | data formatting | bytes 294912
  130.0 6.5 %all-to-all-start.1 = ((f32[128,1,288]{2,1,0:T(1,128)}), f32[128,1,288]{2,1,0:T(1,128)S(1)}, u32[]{:S(2)}, u32[]{:S(2)}) async-start(f32[128,1,288]{2,1,0:T(1,128)} %reshape.313), calls=%async_computation.1 | async-start | bytes 393216 | tf_op jit(solution)/shard_map/all_to_all | solution.py:144
  137.0 12.9 %all-to-all-done.1 = f32[128,1,288]{2,1,0:T(1,128)S(1)} async-done(((f32[128,1,288]{2,1,0:T(1,128)}), f32[128,1,288]{2,1,0:T(1,128)S(1)}, u32[]{:S(2)}, u32[]{:S(2)}) %all-to-all-start.1) | async-done | bytes 147488 | tf_op jit(solution)/shard_map/all_to_all | solution.py:144
  149.9 1.1 reduce.13
  151.8 0.6 copy.38
  152.4 24.5 %scatter_custom_fusion.1 = f32[9,8192]{0,1:T(8,128)} fusion(s32[4096]{0:T(1024)S(1)} %bitcast.116, f32[4096,9]{1,0:T(8,128)S(1)} %copy.38, f32[]{:T(128)} %constant.150.clone.1), kind=kCustom, calls=%fused_computation.93 | custom fusion | flops 36864 | bytes 294916 | tf_op jit(solution)/shard_map/scatter-add | solution.py:145
  176.9 5.3 %slice.96 = f32[3,8192]{0,1:T(8,128)} slice(f32[9,8192]{0,1:T(8,128)} %scatter_custom_fusion.1), slice={[6:9], [0:8192]} | slice | bytes 196608 | tf_op jit(solution)/shard_map/slice | solution.py:147
  182.2 2.8 %copy.39 = f32[3,8192]{1,0:T(4,128)S(1)} copy(f32[3,8192]{0,1:T(8,128)} %slice.96) | data formatting | bytes 196608 | tf_op jit(solution)/shard_map/slice | solution.py:147
  185.1 1.3 broadcast_multiply_fusion
  186.4 4.4 %slice_bitcast_fusion = f32[1,6,8192]{1,2,0:T(8,128)} fusion(f32[9,8192]{0,1:T(8,128)} %scatter_custom_fusion.1), kind=kLoop, calls=%fused_computation.92 | loop fusion | bytes 393216 | tf_op jit(solution)/shard_map/broadcast_in_dim | solution.py:149
  190.9 3.5 %copy.40 = f32[1,6,8192]{2,0,1:T(1,128)} copy(f32[1,6,8192]{1,2,0:T(8,128)} %slice_bitcast_fusion) | data formatting | bytes 393216
  194.4 16.0 %reduce-scatter.2.cloned.1.call-done = f32[48,2048]{1,0:T(8,128)} async-done(((f32[48,8192]{1,0:T(8,128)}), f32[48,2048]{1,0:T(8,128)}) %reduce-scatter.2.cloned.1.call-update) | async-done | bytes 393232 | tf_op jit(solution)/shard_map/reduce_scatter | solution.py:148
  (72 shorter events, 7.3 us)
Async XLA Ops:
  7.2 5.3 %copy-start = (f32[48,8192]{1,0:T(8,128)S(1)}, f32[48,8192]{1,0:T(8,128)}, u32[]{:S(2)}) copy-start(f32[48,8192]{1,0:T(8,128)} %param.13) | copy-start | bytes 4718596
  34.3 18.7 %copy-start.2 = (s32[1,4,256]{2,1,0:T(4,128)S(1)}, s32[1,4,256]{2,1,0:T(4,128)}, u32[]{:S(2)}) copy-start(s32[1,4,256]{2,1,0:T(4,128)} %param.19) | copy-start | bytes 12292
  35.6 30.8 %all-to-all-start = ((f32[128,1,288]{2,1,0:T(1,128)}), f32[128,1,288]{2,1,0:T(1,128)S(1)}, u32[]{:S(2)}, u32[]{:S(2)}) async-start(f32[128,1,288]{2,1,0:T(1,128)} %reshape.311), calls=%async_computation | async-start | bytes 393216 | tf_op jit(solution)/shard_map/all_to_all | solution.py:142
  67.9 2.4 %copy-start.1 = (s32[1,2,4]{2,1,0:T(2,128)S(1)}, s32[1,2,4]{2,1,0:T(2,128)}, u32[]{:S(2)}) copy-start(s32[1,2,4]{2,1,0:T(2,128)} %param.18) | copy-start | bytes 100
  68.0 2.4 %copy-start.4 = (s32[1,4]{1,0:T(1,128)S(1)}, s32[1,4]{1,0:T(1,128)}, u32[]{:S(2)}) copy-start(s32[1,4]{1,0:T(1,128)} %param.20) | copy-start | bytes 52
  125.8 11.0 %copy-start.3 = (s32[1,128]{1,0:T(1,128)S(1)}, s32[1,128]{1,0:T(1,128)}, u32[]{:S(2)}) copy-start(s32[1,128]{1,0:T(1,128)} %param.17) | copy-start | bytes 1540
  130.0 19.9 %all-to-all-start.1 = ((f32[128,1,288]{2,1,0:T(1,128)}), f32[128,1,288]{2,1,0:T(1,128)S(1)}, u32[]{:S(2)}, u32[]{:S(2)}) async-start(f32[128,1,288]{2,1,0:T(1,128)} %reshape.313), calls=%async_computation.1 | async-start | bytes 393216 | tf_op jit(solution)/shard_map/all_to_all | solution.py:144
  136.5 73.8 %reduce-scatter.2.cloned.1.call-start = ((), (), s32[]{:S(2)}) async-start(), calls=%async_computation.3 | async-start | bytes 1966080 | tf_op jit(solution)/shard_map/reduce_scatter | solution.py:148
Sparse Core Ops, SparseCore 0:
  186.5 23.7 reduce-scatter.1
where the time goes:
time: 218 us; the launch traced here: 217 us
  local copies, waits for them, and re-layouts  70.4 us (32%)
  waiting for transfers between devices  42.3 us (19%)
  other arithmetic  41.5 us (19%)
  starting transfers between devices  24.2 us (11%)
  loops' own time  15.7 us (7%)
  between operations  14.3 us (7%)
  matrix products  8.81 us (4%)
    scatter-add x1, other arithmetic, on_device(): jnp.zeros((9, gauss), jnp.float32).at[:, local]  24.5 us
    gather x2, local copies, waits for them, and re-layouts, on_device(): outgoing = rows[:, local] * live[None, :]  18.7 us
    all_to_all x1, starting transfers between devices, on_device(): lax.all_to_all(outgoing, 'cell', split_axis=1, concat_axis=1, tiled=True)  17.4 us
    reduce_scatter x1, waiting for transfers between devices, on_device(): lax.psum_scatter(coeff_grad, 'img', scatter_dimension=1, tiled=True)  16 us
    another operation x1, loops' own time, render_slots(): grads = lax.map(one_tile, jnp.arange(tiles, dtype=jnp.int32))  15.7 us
    all_to_all x1, waiting for transfers between devices, on_device(): lax.all_to_all(outgoing, 'cell', split_axis=1, concat_axis=1, tiled=True)  13.3 us
    all_to_all x1, waiting for transfers between devices, on_device(): lax.all_to_all(slot_grads, 'cell', split_axis=1, concat_axis=1, tiled=True)  12.9 us
    unnamed x20, local copies, waits for them, and re-layouts  10.7 us
  transfers between devices with their start and end apart: 3, of which 3 were waited for; matrix products, arithmetic and copies ran while one was open for 4% of the time, Pallas kernels for 0%

commit v1 on v0

v1 whole, which is shorter than its diff:
```python
import functools

import jax
import jax.numpy as jnp
from jax import lax
from jax.experimental import pallas as pl
from jax.experimental.pallas import tpu as pltpu
from jax.sharding import PartitionSpec as P

SH_ZERO = 0.28209479177387814
SH_ONE = 0.4886025119029199
SH_TWO = (
    1.0925484305920792,
    -1.0925484305920792,
    0.31539156525252005,
    -1.0925484305920792,
    0.5462742152960396,
)
SH_THREE = (
    -0.5900435899266435,
    2.890611442640554,
    -0.4570457994644658,
    0.3731763325901154,
    -0.4570457994644658,
    1.445305721320277,
    -0.5900435899266435,
)

F32 = jnp.float32
BF16 = jnp.bfloat16
PEERS = 128
CAP = 32
COMPS = 9
TILES = 4
DEPTH = 256
LOW = 256
HIGH = 32
PACK = 56
NOTHING = -1.0e4

LINEAR = (
    (SH_ZERO, 0, 0, 0),
    (0, 0, -SH_ONE, 0),
    (0, 0, 0, SH_ONE),
    (0, -SH_ONE, 0, 0),
    (0, SH_TWO[0], 0, 0),
    (0, 0, SH_TWO[1], 0),
    (SH_TWO[2], 0, 0, 0),
    (0, SH_TWO[3], 0, 0),
    (SH_TWO[4], 0, 0, 0),
    (0, 0, SH_THREE[0], 0),
    (0, SH_THREE[1], 0, 0),
    (0, 0, SH_THREE[2], 0),
    (0, 0, 0, SH_THREE[3]),
    (0, SH_THREE[4], 0, 0),
    (0, 0, 0, SH_THREE[5]),
    (0, SH_THREE[6], 0, 0),
)
QUADRATIC = (
    (1, 0, 0, 0, 0, 0, 0),
    (1, 0, 0, 0, 0, 0, 0),
    (1, 0, 0, 0, 0, 0, 0),
    (1, 0, 0, 0, 0, 0, 0),
    (0, 1, 0, 0, 0, 0, 0),
    (0, 0, 1, 0, 0, 0, 0),
    (0, 0, 0, -1, -1, 2, 0),
    (0, 0, 1, 0, 0, 0, 0),
    (0, 0, 0, 1, -1, 0, 0),
    (0, 0, 0, 3, -1, 0, 0),
    (0, 0, 0, 0, 0, 0, 1),
    (0, 0, 0, -1, -1, 4, 0),
    (0, 0, 0, -3, -3, 2, 0),
    (0, 0, 0, -1, -1, 4, 0),
    (0, 0, 0, 1, -1, 0, 0),
    (0, 0, 0, 1, -3, 0, 0),
)


def dot(left, right):
    return lax.dot_general(left, right, (((1,), (0,)), ((), ())), preferred_element_type=F32)


def dot_t(left, right):
    return lax.dot_general(left, right, (((1,), (1,)), ((), ())), preferred_element_type=F32)


def iota(shape, axis):
    return lax.broadcasted_iota(jnp.int32, shape, axis)


def split(value, parts):
    out = []
    for _ in range(parts - 1):
        head = value.astype(BF16).astype(F32)
        out.append(head)
        value = value - head
    out.append(value.astype(BF16).astype(F32))
    return out


def column_consts(table, half):
    rows = iota((8, 128), 0)
    out = []
    for col in range(len(table[0])):
        vals = [float(table[8 * half + i][col]) for i in range(8)]
        if not any(vals):
            out.append(None)
            continue
        acc = jnp.zeros((8, 128), F32)
        for i, val in enumerate(vals):
            if val:
                acc = jnp.where(rows == i, val, acc)
        out.append(acc)
    return out


def form(consts, values):
    total = None
    for const, value in zip(consts, values):
        if const is None:
            continue
        term = const if value is None else const * value
        total = term if total is None else total + term
    return total


def basis_consts():
    return [(column_consts(LINEAR, half), column_consts(QUADRATIC, half)) for half in range(2)]


def basis_halves(consts, xoff, yoff, zoff):
    inv = lax.rsqrt(xoff * xoff + yoff * yoff + zoff * zoff)
    xpos, ypos, zpos = xoff * inv, yoff * inv, zoff * inv
    xsq, ysq, zsq, yz = xpos * xpos, ypos * ypos, zpos * zpos, ypos * zpos
    return [
        form(lin, (None, xpos, ypos, zpos)) * form(quad, (None, ypos, zpos, xsq, ysq, zsq, yz))
        for lin, quad in consts
    ]


def slot_index(idx_ref, cnt_ref, low_scr, high_scr):
    turned = jnp.transpose(idx_ref[...].astype(F32)).astype(jnp.int32)
    slots = jnp.concatenate([turned[32 * i : 32 * i + 32] for i in range(4)], axis=1)
    rows, cols = iota((PEERS, PEERS), 0), iota((PEERS, PEERS), 1)
    perm = (rows == 4 * (cols & 31) + (cols >> 5)).astype(F32).astype(BF16)
    counts = jnp.broadcast_to(cnt_ref[...], (8, PEERS)).astype(F32).astype(BF16)
    counts = dot(counts, perm)[0:1].astype(jnp.int32)
    live = iota((CAP, PEERS), 0) < counts
    low_scr[...] = slots & (LOW - 1)
    high_scr[...] = jnp.where(live, slots >> 8, -1)


def pair_row(ref, base, pair):
    first = ref[pl.ds(base + 2 * pair, 1), :]
    second = ref[pl.ds(base + 2 * pair + 1, 1), :]
    return jnp.concatenate([first, second], axis=1)


def owner_kernel(
    cam_ref, proj_ref, sh_ref, pos_ref, idx_ref, cnt_ref, out_ref, col_scr, low_scr, high_scr, rows_scr
):
    consts = basis_consts()
    camx, camy, camz = cam_ref[0, 0], cam_ref[0, 1], cam_ref[0, 2]

    def shade(chunk, carry):
        lanes = pl.ds(pl.multiple_of(chunk * 128, 128), 128)
        xoff = jnp.broadcast_to(pos_ref[0:1, lanes], (8, 128)) - camx
        yoff = jnp.broadcast_to(pos_ref[1:2, lanes], (8, 128)) - camy
        zoff = jnp.broadcast_to(pos_ref[2:3, lanes], (8, 128)) - camz
        first, second = basis_halves(consts, xoff, yoff, zoff)
        for chan in range(3):
            terms = sh_ref[16 * chan : 16 * chan + 8, lanes] * first
            terms = terms + sh_ref[16 * chan + 8 : 16 * chan + 16, lanes] * second
            colour = jnp.sum(terms, axis=0, keepdims=True) + 0.5
            col_scr[pl.ds(64 * chan + chunk, 1), :] = colour
        return carry

    lax.fori_loop(0, 64, shade, 0, unroll=4)
    slot_index(idx_ref, cnt_ref, low_scr, high_scr)

    even = jnp.concatenate(
        [proj_ref[pl.ds(0, 192, stride=2), :], col_scr[pl.ds(0, 96, stride=2), :]], axis=0
    )
    odd = jnp.concatenate(
        [proj_ref[pl.ds(1, 192, stride=2), :], col_scr[pl.ds(1, 96, stride=2), :]], axis=0
    )
    parts = [part.astype(BF16) for part in split(jnp.concatenate([even, odd], axis=1), 3)]
    low_iota = iota((LOW, 256), 0)
    high_iota = iota((HIGH, 256), 0)

    def gather(pair, carry):
        low, high = pair_row(low_scr, 0, pair), pair_row(high_scr, 0, pair)
        hot = jnp.where(low_iota == low, 1.0, 0.0).astype(BF16)
        wide = dot(parts[0], hot) + dot(parts[1], hot) + dot(parts[2], hot)
        mask = high_iota == high
        for comp in range(COMPS):
            row = jnp.sum(
                jnp.where(mask, wide[32 * comp : 32 * comp + 32], 0.0), axis=0, keepdims=True
            )
            rows_scr[pl.ds(32 * comp + 2 * pair, 1), :] = row[:, :128]
            rows_scr[pl.ds(32 * comp + 2 * pair + 1, 1), :] = row[:, 128:]
        return carry

    lax.fori_loop(0, CAP // 2, gather, 0, unroll=2)
    rows_scr[32 * COMPS :, :] = jnp.zeros((96, 128), F32)
    for k in range(3):
        turned = jnp.transpose(rows_scr[128 * k : 128 * k + 128, :])
        for i in range(4):
            out_ref[pl.ds(3 * i + k, 32, stride=12), :] = turned[32 * i : 32 * i + 32]


def render_kernel(xy_ref, len_ref, recv_ref, list_ref, grad_ref, out_ref, turn_scr):
    table = jnp.concatenate(
        [
            jnp.transpose(recv_ref[pl.ds(0, PEERS, stride=3), :]),
            jnp.transpose(recv_ref[pl.ds(1, PEERS, stride=3), :]),
            jnp.transpose(recv_ref[pl.ds(2, PEERS, stride=3), :])[0:32],
        ],
        axis=0,
    )
    table = [part.astype(BF16) for part in split(table, 3)]

    blank = jnp.zeros((2, 256), F32)
    blocks, heads, seconds = [], [], []
    for tile in range(TILES):
        grads = jnp.concatenate(
            [
                jnp.concatenate(
                    [grad_ref[8 * c + 2 * tile + h : 8 * c + 2 * tile + h + 1, :] for h in range(2)],
                    axis=1,
                )
                for c in range(3)
            ],
            axis=0,
        )
        g0, g1, g2 = split(grads, 3)
        blocks += [g0, g1, blank, g0, g2, blank, g0, g1, blank, jnp.zeros((8, 256), F32)]
        heads.append(g0)
        seconds.append(g1)
    turned = jnp.transpose(jnp.concatenate(blocks, axis=0)).astype(BF16)

    def powers(pixel, which):
        upos = ((pixel & 15).astype(F32) - 7.5) / 128.0
        vpos = ((pixel >> 4).astype(F32) - 7.5) / 128.0
        out = jnp.where(which == 0, 1.0, 0.0)
        out = jnp.where(which == 1, upos, out)
        out = jnp.where(which == 2, vpos, out)
        out = jnp.where(which == 3, upos * upos, out)
        out = jnp.where(which == 4, vpos * vpos, out)
        return jnp.where(which == 5, upos * vpos, out).astype(BF16)

    phi = powers(iota((256, 32), 0), iota((256, 32), 1) & 7)
    phi_rows = powers(iota((16, 256), 1), iota((16, 256), 0))
    before = (iota((DEPTH, DEPTH), 0) < iota((DEPTH, DEPTH), 1)).astype(F32).astype(BF16)
    after = (iota((DEPTH, DEPTH), 0) > iota((DEPTH, DEPTH), 1)).astype(F32).astype(BF16)
    peer_iota = iota((PEERS, DEPTH), 0)
    place_iota = iota((CAP, DEPTH), 0)
    order = iota((1, DEPTH), 1)
    total = jnp.zeros((PEERS, 384), F32)

    for tile in range(TILES):
        slots = list_ref[tile : tile + 1, :]
        hot = jnp.where(peer_iota == (slots >> 5), 1.0, 0.0).astype(BF16)
        place = place_iota == (slots & (CAP - 1))
        wide = dot(table[0], hot) + dot(table[1], hot) + dot(table[2], hot)
        vals = [
            jnp.sum(jnp.where(place, wide[32 * c : 32 * c + 32], 0.0), axis=0, keepdims=True)
            for c in range(COMPS)
        ]
        mean_x, mean_y, ca, cb, cc, opac = vals[:6]
        xrel = mean_x - (xy_ref[0, tile].astype(F32) * 16.0 + 8.0) / 128.0
        yrel = mean_y - (xy_ref[1, tile].astype(F32) * 16.0 + 8.0) / 128.0
        shown = opac > 0.0
        lead_x = ca * xrel + cb * yrel
        lead_y = cc * yrel + cb * xrel
        const = -0.5 * (xrel * lead_x + yrel * lead_y) + jnp.log(jnp.where(shown, opac, 1.0))
        const = jnp.where(shown & (order < len_ref[0, tile]), const, NOTHING)
        coef = jnp.concatenate(
            [const, lead_x, lead_y, -0.5 * ca, -0.5 * cc, -cb, jnp.zeros((2, DEPTH), F32)], axis=0
        )
        coef = jnp.concatenate(split(coef, 3) + [jnp.zeros((8, DEPTH), F32)], axis=0).astype(BF16)
        alpha = jnp.exp(dot(phi, coef))
        rest = 1.0 - alpha
        logs = jnp.log(rest)
        l0 = logs.astype(BF16)
        l1 = (logs - l0.astype(F32)).astype(BF16)
        weight = alpha * jnp.exp(dot(l0, before) + dot(l1, before))

        k0, k1, k2 = split(jnp.concatenate(vals[6:9], axis=0), 3)
        right = [k0, k0, blank, k1, k0, blank, k2, k1, blank, jnp.zeros((8, DEPTH), F32)]
        right = jnp.concatenate(right, axis=0)
        pad = [jnp.zeros((32 * n, DEPTH), F32) for n in (tile, TILES - 1 - tile) ]
        pieces = ([pad[0]] if tile else []) + [right] + ([pad[1]] if tile < TILES - 1 else [])
        right = jnp.concatenate(pieces, axis=0).astype(BF16)
        flow = dot(turned, right) * weight
        s0 = flow.astype(BF16)
        s1 = (flow - s0.astype(F32)).astype(BF16)
        behind = dot(s0, after) + dot(s1, after)
        power = flow - behind * (alpha / rest)
        p0 = power.astype(BF16)
        p1 = (power - p0.astype(F32)).astype(BF16)
        moments = dot(phi_rows, p0) + dot(phi_rows, p1)
        w0 = weight.astype(BF16)
        w1 = (weight - w0.astype(F32)).astype(BF16)
        zero5 = jnp.zeros((5, 256), F32)
        sides = jnp.concatenate([heads[tile], zero5, seconds[tile], zero5], axis=0).astype(BF16)
        colours = dot(sides, w0)
        colours = colours[0:8] + colours[8:16] + dot(sides, w1)[0:8]

        m0, mu, mv, muu, mvv, muv = [moments[i : i + 1] for i in range(6)]
        grads = [
            ca * mu + cb * mv - lead_x * m0,
            cc * mv + cb * mu - lead_y * m0,
            -0.5 * (muu - 2.0 * xrel * mu + xrel * xrel * m0),
            -(muv - yrel * mu - xrel * mv + xrel * yrel * m0),
            -0.5 * (mvv - 2.0 * yrel * mv + yrel * yrel * m0),
            jnp.where(shown, m0 / jnp.where(shown, opac, 1.0), 0.0),
        ] + [colours[i : i + 1] for i in range(3)]
        fill = jnp.zeros((96, DEPTH), F32)
        heads_tails = [split(grad, 2) for grad in grads]
        for part in range(2):
            wide = jnp.concatenate(
                [jnp.where(place, both[part], 0.0) for both in heads_tails] + [fill], axis=0
            ).astype(BF16)
            total = total + dot_t(hot, wide)
    for k in range(3):
        out_ref[pl.ds(k, PEERS, stride=3), :] = total[:, 128 * k : 128 * k + 128]


def scatter_kernel(
    cam_ref, back_ref, idx_ref, cnt_ref, out_ref, col_ref, low_scr, high_scr, rows_scr, acc_scr
):
    slot_index(idx_ref, cnt_ref, low_scr, high_scr)
    for k in range(3):
        block = jnp.concatenate(
            [back_ref[pl.ds(3 * i + k, 32, stride=12), :] for i in range(4)], axis=0
        )
        rows_scr[128 * k : 128 * k + 128, :] = jnp.transpose(block)
    low_iota = iota((LOW, 256), 0)
    high_iota = iota((HIGH, 256), 0)
    acc_scr[...] = jnp.zeros(acc_scr.shape, F32)

    def scatter(step, carry):
        hots, heads, tails = [], [], []
        for sub in range(4):
            pair = 4 * step + sub
            low, high = pair_row(low_scr, 0, pair), pair_row(high_scr, 0, pair)
            hots.append(jnp.where(low_iota == low, 1.0, 0.0).astype(BF16))
            mask = high_iota == high
            both = [split(pair_row(rows_scr, 32 * comp, pair), 2) for comp in range(COMPS)]
            heads.append(
                jnp.concatenate([jnp.where(mask, b[0], 0.0) for b in both], axis=0).astype(BF16)
            )
            tails.append(
                jnp.concatenate([jnp.where(mask, b[1], 0.0) for b in both], axis=0).astype(BF16)
            )
        hot = jnp.concatenate(hots, axis=1)
        acc_scr[...] += dot_t(jnp.concatenate(heads, axis=1), hot) + dot_t(
            jnp.concatenate(tails, axis=1), hot
        )
        return carry

    lax.fori_loop(0, 4, scatter, 0)
    for par in range(2):
        out_ref[pl.ds(par, 192, stride=2), :] = acc_scr[0:192, 128 * par : 128 * par + 128]
        for share in range(4):
            for chan in range(3):
                first = 192 + 32 * chan + 8 * share
                col_ref[pl.ds(PACK * share + 16 * chan + par, 8, stride=2), :] = acc_scr[
                    first : first + 8, 128 * par : 128 * par + 128
                ]
    lanes = iota((8, 128), 1)
    row = jnp.where(lanes == 0, cam_ref[0, 0], 0.0)
    row = jnp.where(lanes == 1, cam_ref[0, 1], row)
    row = jnp.where(lanes == 2, cam_ref[0, 2], row)
    for share in range(4):
        col_ref[PACK * share + 48 : PACK * share + 56, :] = row


def coeff_kernel(share_ref, col_ref, pos_ref, out_ref):
    consts = basis_consts()
    share = share_ref[0]
    cams = []
    for image in range(4):
        row = col_ref[PACK * image + 48 : PACK * image + 56, :]
        cams.append([jnp.broadcast_to(row[:, i : i + 1], (8, 128)) for i in range(3)])

    def chunk(step, carry):
        lanes = pl.ds(pl.multiple_of(share * 2048 + step * 128, 128), 128)
        place = [jnp.broadcast_to(pos_ref[i : i + 1, lanes], (8, 128)) for i in range(3)]
        totals = [[None, None] for _ in range(3)]
        for image in range(4):
            cam = cams[image]
            halves = basis_halves(
                consts, place[0] - cam[0], place[1] - cam[1], place[2] - cam[2]
            )
            for chan in range(3):
                grad = jnp.broadcast_to(
                    col_ref[pl.ds(PACK * image + 16 * chan + step, 1), :], (8, 128)
                )
                for half in range(2):
                    term = grad * halves[half]
                    old = totals[chan][half]
                    totals[chan][half] = term if old is None else old + term
        here = pl.ds(pl.multiple_of(step * 128, 128), 128)
        for chan in range(3):
            for half in range(2):
                out_ref[16 * chan + 8 * half : 16 * chan + 8 * half + 8, here] = totals[chan][half]
        return carry

    lax.fori_loop(0, 16, chunk, 0, unroll=2)


VMEM = pl.BlockSpec(memory_space=pltpu.VMEM)
SMEM = pl.BlockSpec(memory_space=pltpu.SMEM)
PARAMS = pltpu.CompilerParams(vmem_limit_bytes=40 * 1024 * 1024)


def shape(*dims):
    return jax.ShapeDtypeStruct(dims, F32)


def owner(camera, proj, coeffs, positions, index, count):
    return pl.pallas_call(
        owner_kernel,
        out_shape=shape(384, 128),
        in_specs=[SMEM] + [VMEM] * 5,
        out_specs=VMEM,
        scratch_shapes=[
            pltpu.VMEM((192, 128), F32),
            pltpu.VMEM((CAP, PEERS), jnp.int32),
            pltpu.VMEM((CAP, PEERS), jnp.int32),
            pltpu.VMEM((384, 128), F32),
        ],
        compiler_params=PARAMS,
        name="owner_rows",
    )(camera, proj, coeffs, positions, index, count)


def render(tile_xy, tile_len, received, tile_list, pixel_grad):
    return pl.pallas_call(
        render_kernel,
        out_shape=shape(384, 128),
        in_specs=[SMEM] * 2 + [VMEM] * 3,
        out_specs=VMEM,
        scratch_shapes=[pltpu.VMEM((128, 256), F32)],
        compiler_params=PARAMS,
        name="render_tiles",
    )(tile_xy, tile_len, received, tile_list, pixel_grad)


def scatter(camera, returned, index, count):
    return pl.pallas_call(
        scatter_kernel,
        out_shape=(shape(384, 128), shape(4 * PACK, 128)),
        in_specs=[SMEM] + [VMEM] * 3,
        out_specs=(VMEM, VMEM),
        scratch_shapes=[
            pltpu.VMEM((CAP, PEERS), jnp.int32),
            pltpu.VMEM((CAP, PEERS), jnp.int32),
            pltpu.VMEM((384, 128), F32),
            pltpu.VMEM((32 * COMPS, LOW), F32),
        ],
        compiler_params=PARAMS,
        name="owner_sums",
    )(camera, returned, index, count)


def coefficients(share, colours, positions):
    return pl.pallas_call(
        coeff_kernel,
        out_shape=shape(48, 2048),
        in_specs=[SMEM] + [VMEM] * 2,
        out_specs=VMEM,
        compiler_params=PARAMS,
        name="coeff_grads",
    )(share, colours, positions)


def exchange(rows, axis, peers):
    sent = rows.reshape(peers, 1, -1)
    got = lax.all_to_all(sent, axis, split_axis=0, concat_axis=0, tiled=True)
    return got.reshape(rows.shape)


def on_device(
    proj,
    sh_coeffs,
    positions,
    camera,
    send_index,
    send_count,
    tile_xy,
    tile_list,
    tile_len,
    pixel_grad,
):
    index = send_index.reshape(CAP, PEERS)
    outgoing = owner(
        camera, proj.reshape(384, 128), sh_coeffs, positions, index, send_count
    )
    received = exchange(outgoing, "cell", PEERS)
    slot_grads = render(
        tile_xy[0], tile_len, received, tile_list[0], pixel_grad.reshape(24, 128)
    )
    returned = exchange(slot_grads, "cell", PEERS)
    grad_rows, colours = scatter(camera, returned, index, send_count)
    colours = exchange(colours, "img", 4)
    share = lax.axis_index("img").astype(jnp.int32).reshape(1)
    grad_sh = coefficients(share, colours, positions)
    return (grad_rows.reshape(proj.shape), grad_sh)


def solution(mesh):
    return jax.shard_map(
        on_device,
        mesh=mesh,
        in_specs=(
            P("img", None, "cell"),
            P(None, "cell"),
            P(None, "cell"),
            P("img", None),
            P("img", "cell"),
            P("img", "cell"),
            P("img", None, "cell"),
            P("img", "cell", None),
            P("img", "cell"),
            P("img", None, "cell"),
        ),
        out_specs=(P("img", None, "cell"), P(None, ("cell", "img"))),
        check_vma=False,
    )
```

time: 218 us -> 82.4 us (0.38)
  local copies, waits for them, and re-layouts: 70.4 us -> 5.29 us
  blocking collectives: 0 us -> 49.8 us
  other arithmetic: 41.5 us -> 0 us
  waiting for transfers between devices: 42.3 us -> 5.89 us
  starting transfers between devices: 24.2 us -> 4.3 us
  Pallas kernels: 0 us -> 16 us
  loops' own time: 15.7 us -> 0 us
  between operations: 14.3 us -> 0.69 us
  matrix products: 8.81 us -> 0 us
    all_to_all x0 -> x2, blocking collectives: none -> 49.8 us  [exchange(): got = lax.all_to_all(sent, axis, split_axis=0, concat_axis=0, tiled=True)]
    scatter-add x2 -> x0, other arithmetic: 31 us -> none  [the longest x1 24.5 us: on_device(): jnp.zeros((9, gauss), jnp.float32).at[:, local]]
    gather x6 -> x0, local copies, waits for them, and re-layouts: 27.9 us -> none  [the longest x2 18.7 us: on_device(): outgoing = rows[:, local] * live[None, :]]
    all_to_all x2 -> x1, waiting for transfers between devices: 26.2 us -> 5.89 us  [exchange(): got = lax.all_to_all(sent, axis, split_axis=0, concat_axis=0, tiled=True)]
    all_to_all x2 -> x1, starting transfers between devices: 23.9 us -> 4.3 us  [exchange(): got = lax.all_to_all(sent, axis, split_axis=0, concat_axis=0, tiled=True)]
    pallas_call x0 -> x4, Pallas kernels: none -> 16 us  [the longest x1 5.87 us: render(): pl.pallas_call(render_kernel, out_shape=shape(384, 128), in_specs=[SMEM]...]
    reduce_scatter x1 -> x0, waiting for transfers between devices: 16 us -> none  [on_device(): lax.psum_scatter(coeff_grad, 'img', scatter_dimension=1, tiled=True)]
    another operation x1 -> x0, loops' own time: 15.7 us -> none  [render_slots(): grads = lax.map(one_tile, jnp.arange(tiles, dtype=jnp.int32))]
  transfers between devices with their start and end apart: 3 -> 1, of which waited for: 3 -> 1; matrix products, arithmetic and copies ran while one was open for 4% -> 0% of each run, Pallas kernels for 0% -> 0%
where the time goes in v1:
time: 82.4 us; the launch traced here: 82 us
  blocking collectives  49.8 us (60%)
  Pallas kernels  16 us (19%)
  waiting for transfers between devices  5.89 us (7%)
  local copies, waits for them, and re-layouts  5.29 us (6%)
  starting transfers between devices  4.3 us (5%)
    all_to_all x2, blocking collectives, exchange(): got = lax.all_to_all(sent, axis, split_axis=0, concat_axis=0, tiled=True)  49.8 us
    all_to_all x1, waiting for transfers between devices, exchange(): got = lax.all_to_all(sent, axis, split_axis=0, concat_axis=0, tiled=True)  5.89 us
    pallas_call x1, Pallas kernels, render(): pl.pallas_call(render_kernel, out_shape=shape(384, 128), in_specs=[SMEM]...  5.87 us
    unnamed x24, local copies, waits for them, and re-layouts  5.29 us
    pallas_call x1, Pallas kernels, owner(): pl.pallas_call(owner_kernel, out_shape=shape(384, 128), in_specs=[SMEM] +...  5.13 us
    all_to_all x1, starting transfers between devices, exchange(): got = lax.all_to_all(sent, axis, split_axis=0, concat_axis=0, tiled=True)  4.3 us
    pallas_call x1, Pallas kernels, scatter(): pl.pallas_call(scatter_kernel, out_shape=(shape(384, 128), shape(4 * PACK...  3.61 us
  transfers between devices with their start and end apart: 1, of which 1 were waited for; matrix products, arithmetic and copies ran while one was open for 0% of the time, Pallas kernels for 0%

profile of v1, /device:TPU:8, one launch (start us, length us, event | category | flops | bytes accessed | tf_op | source)
XLA Modules:
  0.0 82.0 jit_solution(544053653508637823)
XLA Ops:
  0.6 0.0 copy-start.11
  0.6 0.0 copy-start.10
  0.7 0.0 copy-start
  0.7 1.4 %copy-done = f32[48,8192]{1,0:T(8,128)S(1)} copy-done((f32[48,8192]{1,0:T(8,128)S(1)}, f32[48,8192]{1,0:T(8,128)}, u32[]{:S(2)}) %copy-start) | copy-done | bytes 1572888
  2.1 0.0 copy-start.1
  2.1 0.9 %copy-done.1 = f32[3,8192]{1,0:T(4,128)S(1)} copy-done((f32[3,8192]{1,0:T(4,128)S(1)}, f32[3,8192]{1,0:T(4,128)}, u32[]{:S(2)}) %copy-start.1) | copy-done | bytes 98328
  3.0 0.0 copy-start.3
  3.0 0.9 %copy-done.3 = f32[1,6,8192]{2,0,1:T(1,128)S(1)} copy-done((f32[1,6,8192]{2,0,1:T(1,128)S(1)}, f32[1,6,8192]{2,0,1:T(1,128)}, u32[]{:S(2)}) %copy-start.3) | copy-done | bytes 196632
  3.9 0.0 copy-start.4
  3.9 0.7 copy-done.4
  4.6 0.0 copy-start.7
  4.6 0.7 copy-done.7
  5.3 0.0 copy-start.9
  5.3 0.7 copy-done.9
  5.9 0.0 copy-start.5
  5.9 0.0 copy-start.6
  5.9 0.0 copy-start.8
  5.9 0.0 copy-start.2
  5.9 5.1 %owner_rows.1 = f32[384,128]{1,0:T(8,128)S(1)} custom-call(f32[1,3]{1,0:T(1,128)S(1)} %copy-done.7, f32[384,128]{1,0:T(8,128)S(1)} %bitcast.18, f32[48,8192]{1,0:T(8,128)S(1)} %copy-done, f32[3,8192]{1,0:T(4,128)S(1)} %copy-done.1, s32[32,128]{1,0:T(8,128)S(1)} %bitcast.19, s32[1,128]{1,0:T(1,128)S(1)} %copy-done.9), custom_call_target="tpu_custom_call" | custom-call | tf_op jit(solution)/shard_map/owner_rows/pallas_call | solution.py:424
  11.1 30.5 %all_to_all.15 = f32[128,1,384]{2,1,0:T(1,128)S(1)} all-to-all(f32[128,1,384]{2,1,0:T(1,128)S(1)} %bitcast.16), channel_id=1, replica_groups=mesh['cell'=128,'img'=4] {'cell'}, dimensions={0} | all-to-all | bytes 393216 | tf_op jit(solution)/shard_map/all_to_all | solution.py:482
  41.6 0.0 copy-done.11
  41.6 0.0 copy-done.10
  41.6 0.0 copy-done.5
  41.6 0.0 copy-done.6
  41.6 5.9 %render_tiles.1 = f32[384,128]{1,0:T(8,128)S(1)} custom-call(s32[2,4]{1,0:T(2,128)S(1)} %bitcast.23, s32[1,4]{1,0:T(1,128)S(1)} %copy-done.11, f32[384,128]{1,0:T(8,128)S(1)} %bitcast.14, s32[4,256]{1,0:T(4,128)S(1)} %bitcast.22, f32[24,128]{1,0:T(8,128)S(1)} %bitcast.21), custom_call_target="tpu_custom_call" | custom-call | tf_op jit(solution)/shard_map/render_tiles/pallas_call | solution.py:441
  47.5 19.3 %all_to_all.16 = f32[128,1,384]{2,1,0:T(1,128)S(1)} all-to-all(f32[128,1,384]{2,1,0:T(1,128)S(1)} %bitcast.15), channel_id=1, replica_groups=mesh['cell'=128,'img'=4] {'cell'}, dimensions={0} | all-to-all | bytes 393216 | tf_op jit(solution)/shard_map/all_to_all | solution.py:482
  66.8 0.0 copy-done.8
  66.8 3.6 %owner_sums.1 = (f32[384,128]{1,0:T(8,128)}, f32[224,128]{1,0:T(8,128)}) custom-call(f32[1,3]{1,0:T(1,128)S(1)} %copy-done.8, f32[384,128]{1,0:T(8,128)S(1)} %bitcast.13, s32[32,128]{1,0:T(8,128)S(1)} %bitcast.20, s32[1,128]{1,0:T(1,128)S(1)} %copy-done.9), custom_call_target="tpu_custom_call" | custom-call | tf_op jit(solution)/shard_map/owner_sums/pallas_call | solution.py:453
  70.4 4.3 %all-to-all-start.2 = ((f32[4,1,7168]{2,1,0:T(1,128)}), f32[4,1,7168]{2,1,0:T(1,128)S(1)}, u32[]{:S(2)}, u32[]{:S(2)}) async-start(f32[4,1,7168]{2,1,0:T(1,128)} %bitcast.11), calls=%async_computation.2 | async-start | bytes 229376 | tf_op jit(solution)/shard_map/all_to_all | solution.py:482
  74.7 5.9 %all-to-all-done.2 = f32[4,1,7168]{2,1,0:T(1,128)S(1)} async-done(((f32[4,1,7168]{2,1,0:T(1,128)}), f32[4,1,7168]{2,1,0:T(1,128)S(1)}, u32[]{:S(2)}, u32[]{:S(2)}) %all-to-all-start.2) | async-done | bytes 114720 | tf_op jit(solution)/shard_map/all_to_all | solution.py:482
  80.6 0.0 copy-done.2
  80.6 1.4 %coeff_grads.1 = f32[48,2048]{1,0:T(8,128)} custom-call(s32[1]{0:T(128)} %bitcast.10.share_ref, f32[224,128]{1,0:T(8,128)S(1)} %bitcast.17, f32[3,8192]{1,0:T(4,128)S(1)} %copy-done.2), custom_call_target="tpu_custom_call" | custom-call | tf_op jit(solution)/shard_map/coeff_grads/pallas_call | solution.py:470
Async XLA Ops:
  0.6 41.0 %copy-start.11 = (s32[1,4]{1,0:T(1,128)S(1)}, s32[1,4]{1,0:T(1,128)}, u32[]{:S(2)}) copy-start(s32[1,4]{1,0:T(1,128)} %len_ref.1) | copy-start | bytes 52
  0.6 41.0 %copy-start.10 = (s32[1,2,4]{2,1,0:T(2,128)S(1)}, s32[1,2,4]{2,1,0:T(2,128)}, u32[]{:S(2)}) copy-start(s32[1,2,4]{2,1,0:T(2,128)} %param.16) | copy-start | bytes 100
  0.7 1.4 %copy-start = (f32[48,8192]{1,0:T(8,128)S(1)}, f32[48,8192]{1,0:T(8,128)}, u32[]{:S(2)}) copy-start(f32[48,8192]{1,0:T(8,128)} %sh_ref.1) | copy-start | bytes 4718596
  2.1 0.9 %copy-start.1 = (f32[3,8192]{1,0:T(4,128)S(1)}, f32[3,8192]{1,0:T(4,128)}, u32[]{:S(2)}) copy-start(f32[3,8192]{1,0:T(4,128)} %pos_ref.3) | copy-start | bytes 294916
  3.0 0.9 %copy-start.3 = (f32[1,6,8192]{2,0,1:T(1,128)S(1)}, f32[1,6,8192]{2,0,1:T(1,128)}, u32[]{:S(2)}) copy-start(f32[1,6,8192]{2,0,1:T(1,128)} %param.10) | copy-start | bytes 589828
  3.9 0.7 copy-start.4
  4.6 0.7 copy-start.7
  5.3 0.7 copy-start.9
  5.9 35.7 %copy-start.5 = (f32[1,3,1024]{2,0,1:T(1,128)S(1)}, f32[1,3,1024]{2,0,1:T(1,128)}, u32[]{:S(2)}) copy-start(f32[1,3,1024]{2,0,1:T(1,128)} %param.19) | copy-start | bytes 36868
  5.9 35.7 %copy-start.6 = (s32[1,4,256]{2,1,0:T(4,128)S(1)}, s32[1,4,256]{2,1,0:T(4,128)}, u32[]{:S(2)}) copy-start(s32[1,4,256]{2,1,0:T(4,128)} %param.17) | copy-start | bytes 12292
  5.9 60.8 %copy-start.8 = (f32[1,3]{1,0:T(1,128)S(1)}, f32[1,3]{1,0:T(1,128)}, u32[]{:S(2)}) copy-start(f32[1,3]{1,0:T(1,128)} %cam_ref.3) | copy-start | bytes 40
  5.9 74.6 %copy-start.2 = (f32[3,8192]{1,0:T(4,128)S(1)}, f32[3,8192]{1,0:T(4,128)}, u32[]{:S(2)}) copy-start(f32[3,8192]{1,0:T(4,128)} %pos_ref.3) | copy-start | bytes 294916
  70.4 10.2 %all-to-all-start.2 = ((f32[4,1,7168]{2,1,0:T(1,128)}), f32[4,1,7168]{2,1,0:T(1,128)S(1)}, u32[]{:S(2)}, u32[]{:S(2)}) async-start(f32[4,1,7168]{2,1,0:T(1,128)} %bitcast.11), calls=%async_computation.2 | async-start | bytes 229376 | tf_op jit(solution)/shard_map/all_to_all | solution.py:482

commit v2 on v1

v2 whole, which is shorter than its diff:
```python
import functools

import jax
import jax.numpy as jnp
from jax import lax
from jax.experimental import pallas as pl
from jax.experimental.pallas import tpu as pltpu
from jax.sharding import PartitionSpec as P

SH_ZERO = 0.28209479177387814
SH_ONE = 0.4886025119029199
SH_TWO = (
    1.0925484305920792,
    -1.0925484305920792,
    0.31539156525252005,
    -1.0925484305920792,
    0.5462742152960396,
)
SH_THREE = (
    -0.5900435899266435,
    2.890611442640554,
    -0.4570457994644658,
    0.3731763325901154,
    -0.4570457994644658,
    1.445305721320277,
    -0.5900435899266435,
)

F32 = jnp.float32
BF16 = jnp.bfloat16
PEERS = 128
CAP = 32
COMPS = 9
TILES = 4
DEPTH = 256
LOW = 256
HIGH = 32
PACK = 56
NOTHING = -1.0e4

LINEAR = (
    (SH_ZERO, 0, 0, 0),
    (0, 0, -SH_ONE, 0),
    (0, 0, 0, SH_ONE),
    (0, -SH_ONE, 0, 0),
    (0, SH_TWO[0], 0, 0),
    (0, 0, SH_TWO[1], 0),
    (SH_TWO[2], 0, 0, 0),
    (0, SH_TWO[3], 0, 0),
    (SH_TWO[4], 0, 0, 0),
    (0, 0, SH_THREE[0], 0),
    (0, SH_THREE[1], 0, 0),
    (0, 0, SH_THREE[2], 0),
    (0, 0, 0, SH_THREE[3]),
    (0, SH_THREE[4], 0, 0),
    (0, 0, 0, SH_THREE[5]),
    (0, SH_THREE[6], 0, 0),
)
QUADRATIC = (
    (1, 0, 0, 0, 0, 0, 0),
    (1, 0, 0, 0, 0, 0, 0),
    (1, 0, 0, 0, 0, 0, 0),
    (1, 0, 0, 0, 0, 0, 0),
    (0, 1, 0, 0, 0, 0, 0),
    (0, 0, 1, 0, 0, 0, 0),
    (0, 0, 0, -1, -1, 2, 0),
    (0, 0, 1, 0, 0, 0, 0),
    (0, 0, 0, 1, -1, 0, 0),
    (0, 0, 0, 3, -1, 0, 0),
    (0, 0, 0, 0, 0, 0, 1),
    (0, 0, 0, -1, -1, 4, 0),
    (0, 0, 0, -3, -3, 2, 0),
    (0, 0, 0, -1, -1, 4, 0),
    (0, 0, 0, 1, -1, 0, 0),
    (0, 0, 0, 1, -3, 0, 0),
)


def dot(left, right):
    return lax.dot_general(left, right, (((1,), (0,)), ((), ())), preferred_element_type=F32)


def dot_t(left, right):
    return lax.dot_general(left, right, (((1,), (1,)), ((), ())), preferred_element_type=F32)


def iota(shape, axis):
    return lax.broadcasted_iota(jnp.int32, shape, axis)


def split(value, parts):
    out = []
    for _ in range(parts - 1):
        head = value.astype(BF16).astype(F32)
        out.append(head)
        value = value - head
    out.append(value.astype(BF16).astype(F32))
    return out


def column_consts(table, half):
    rows = iota((8, 128), 0)
    out = []
    for col in range(len(table[0])):
        vals = [float(table[8 * half + i][col]) for i in range(8)]
        if not any(vals):
            out.append(None)
            continue
        acc = jnp.zeros((8, 128), F32)
        for i, val in enumerate(vals):
            if val:
                acc = jnp.where(rows == i, val, acc)
        out.append(acc)
    return out


def form(consts, values):
    total = None
    for const, value in zip(consts, values):
        if const is None:
            continue
        term = const if value is None else const * value
        total = term if total is None else total + term
    return total


def basis_consts():
    return [(column_consts(LINEAR, half), column_consts(QUADRATIC, half)) for half in range(2)]


def basis_halves(consts, xoff, yoff, zoff):
    inv = lax.rsqrt(xoff * xoff + yoff * yoff + zoff * zoff)
    xpos, ypos, zpos = xoff * inv, yoff * inv, zoff * inv
    xsq, ysq, zsq, yz = xpos * xpos, ypos * ypos, zpos * zpos, ypos * zpos
    return [
        form(lin, (None, xpos, ypos, zpos)) * form(quad, (None, ypos, zpos, xsq, ysq, zsq, yz))
        for lin, quad in consts
    ]


def slot_index(idx_ref, cnt_ref, low_scr, high_scr):
    turned = jnp.transpose(idx_ref[...].astype(F32)).astype(jnp.int32)
    slots = jnp.concatenate([turned[32 * i : 32 * i + 32] for i in range(4)], axis=1)
    rows, cols = iota((PEERS, PEERS), 0), iota((PEERS, PEERS), 1)
    perm = (rows == 4 * (cols & 31) + (cols >> 5)).astype(F32).astype(BF16)
    counts = jnp.broadcast_to(cnt_ref[...], (8, PEERS)).astype(F32).astype(BF16)
    counts = dot(counts, perm)[0:1].astype(jnp.int32)
    live = iota((CAP, PEERS), 0) < counts
    low_scr[...] = slots & (LOW - 1)
    high_scr[...] = jnp.where(live, slots >> 8, -1)


def pair_row(ref, base, pair):
    first = ref[pl.ds(base + 2 * pair, 1), :]
    second = ref[pl.ds(base + 2 * pair + 1, 1), :]
    return jnp.concatenate([first, second], axis=1)


def owner_kernel(
    cam_hbm,
    proj_hbm,
    sh_hbm,
    pos_hbm,
    idx_hbm,
    cnt_hbm,
    out_ref,
    cam_ref,
    proj_ref,
    sh_ref,
    pos_ref,
    idx_ref,
    cnt_ref,
    col_scr,
    low_scr,
    high_scr,
    rows_scr,
    sems,
):
    copies = [
        pltpu.make_async_copy(src, dst, sems.at[i])
        for i, (src, dst) in enumerate(
            (
                (idx_hbm, idx_ref),
                (cnt_hbm, cnt_ref),
                (cam_hbm, cam_ref),
                (pos_hbm, pos_ref),
                (sh_hbm, sh_ref),
                (proj_hbm, proj_ref),
            )
        )
    ]
    for copy in copies:
        copy.start()
    consts = basis_consts()
    for copy in copies[:2]:
        copy.wait()
    slot_index(idx_ref, cnt_ref, low_scr, high_scr)
    for copy in copies[2:5]:
        copy.wait()
    cam = [jnp.broadcast_to(cam_ref[0:1, i : i + 1], (8, 128)) for i in range(3)]

    def shade(chunk, carry):
        lanes = pl.ds(pl.multiple_of(chunk * 128, 128), 128)
        offs = [jnp.broadcast_to(pos_ref[i : i + 1, lanes], (8, 128)) - cam[i] for i in range(3)]
        first, second = basis_halves(consts, *offs)
        for chan in range(3):
            terms = sh_ref[16 * chan : 16 * chan + 8, lanes] * first
            terms = terms + sh_ref[16 * chan + 8 : 16 * chan + 16, lanes] * second
            colour = jnp.sum(terms, axis=0, keepdims=True) + 0.5
            col_scr[pl.ds(64 * chan + chunk, 1), :] = colour
        return carry

    lax.fori_loop(0, 64, shade, 0, unroll=16)
    copies[5].wait()

    even = jnp.concatenate(
        [proj_ref[pl.ds(0, 192, stride=2), :], col_scr[pl.ds(0, 96, stride=2), :]], axis=0
    )
    odd = jnp.concatenate(
        [proj_ref[pl.ds(1, 192, stride=2), :], col_scr[pl.ds(1, 96, stride=2), :]], axis=0
    )
    parts = [part.astype(BF16) for part in split(jnp.concatenate([even, odd], axis=1), 3)]
    low_iota = iota((LOW, 256), 0)
    high_iota = iota((HIGH, 256), 0)

    for pair in range(CAP // 2):
        low, high = pair_row(low_scr, 0, pair), pair_row(high_scr, 0, pair)
        hot = jnp.where(low_iota == low, 1.0, 0.0).astype(BF16)
        wide = dot(parts[0], hot) + dot(parts[1], hot) + dot(parts[2], hot)
        mask = high_iota == high
        for comp in range(COMPS):
            row = jnp.sum(
                jnp.where(mask, wide[32 * comp : 32 * comp + 32], 0.0), axis=0, keepdims=True
            )
            rows_scr[32 * comp + 2 * pair : 32 * comp + 2 * pair + 1, :] = row[:, :128]
            rows_scr[32 * comp + 2 * pair + 1 : 32 * comp + 2 * pair + 2, :] = row[:, 128:]

    rows_scr[32 * COMPS :, :] = jnp.zeros((96, 128), F32)
    for k in range(3):
        turned = jnp.transpose(rows_scr[128 * k : 128 * k + 128, :])
        for i in range(4):
            out_ref[pl.ds(3 * i + k, 32, stride=12), :] = turned[32 * i : 32 * i + 32]


def render_kernel(
    xy_ref, len_ref, recv_ref, list_ref, grad_ref, out_ref, table_scr, coef_scr, right_scr, sums_scr
):
    for k in range(3):
        table_scr[128 * k : 128 * k + 128, :] = jnp.transpose(
            recv_ref[pl.ds(k, PEERS, stride=3), :]
        )

    slots = jnp.concatenate(
        [list_ref[t : t + 1, 128 * h : 128 * h + 128] for t in range(TILES) for h in range(2)],
        axis=0,
    )
    peer, place = slots >> 5, slots & (CAP - 1)
    row_iota = iota((8, 128), 0)

    def by_tile(ref, row):
        out = jnp.zeros((8, 128), jnp.int32)
        for t in range(TILES):
            out = jnp.where(
                row_iota >> 1 == t, jnp.broadcast_to(ref[row : row + 1, t : t + 1], (8, 128)), out
            )
        return out

    centre_x = (by_tile(xy_ref, 0).astype(F32) * 16.0 + 8.0) / 128.0
    centre_y = (by_tile(xy_ref, 1).astype(F32) * 16.0 + 8.0) / 128.0
    inside = (row_iota & 1) * 128 + iota((8, 128), 1) < by_tile(len_ref, 0)

    vals = [jnp.zeros((8, 128), F32) for _ in range(COMPS)]
    for q in range(CAP):
        mine = place == q
        for c in range(COMPS):
            row = jnp.broadcast_to(table_scr[32 * c + q : 32 * c + q + 1, :], (8, 128))
            vals[c] = jnp.where(mine, jnp.take_along_axis(row, peer, axis=1), vals[c])

    mean_x, mean_y, ca, cb, cc, opac = vals[:6]
    xrel, yrel = mean_x - centre_x, mean_y - centre_y
    shown = opac > 0.0
    lead_x = ca * xrel + cb * yrel
    lead_y = cc * yrel + cb * xrel
    const = -0.5 * (xrel * lead_x + yrel * lead_y) + jnp.log(jnp.where(shown, opac, 1.0))
    const = jnp.where(shown & inside, const, NOTHING)
    zero = jnp.zeros((8, 128), F32)
    coef = [split(v, 3) for v in (const, lead_x, lead_y, -0.5 * ca, -0.5 * cc, -cb, zero, zero)]
    for part in range(3):
        for i in range(8):
            at = 64 * part + 8 * i
            coef_scr[at : at + 8, :] = coef[i][part]
    coef_scr[192:256, :] = jnp.zeros((64, 128), F32)
    tint = [split(v, 3) for v in vals[6:9]]
    for block, (one, two) in enumerate(((0, 0), (1, 0), (2, 1))):
        for c in range(3):
            right_scr[64 * block + 8 * c : 64 * block + 8 * c + 8, :] = tint[c][one]
            right_scr[64 * block + 24 + 8 * c : 64 * block + 32 + 8 * c, :] = tint[c][two]
        right_scr[64 * block + 48 : 64 * block + 64, :] = jnp.zeros((16, 128), F32)
    right_scr[192:256, :] = jnp.zeros((64, 128), F32)

    blank = jnp.zeros((2, 256), F32)
    blocks, sides = [], []
    for tile in range(TILES):
        grads = jnp.concatenate(
            [
                jnp.concatenate(
                    [grad_ref[8 * c + 2 * tile + h : 8 * c + 2 * tile + h + 1, :] for h in range(2)],
                    axis=1,
                )
                for c in range(3)
            ],
            axis=0,
        )
        g0, g1, g2 = split(grads, 3)
        blocks += [g0, g1, blank, g0, g2, blank, g0, g1, blank, jnp.zeros((8, 256), F32)]
        zero5 = jnp.zeros((5, 256), F32)
        sides.append(jnp.concatenate([g0, zero5, g1, zero5], axis=0).astype(BF16))
    turned = jnp.transpose(jnp.concatenate(blocks, axis=0)).astype(BF16)

    pixel, which = iota((256, 32), 0), iota((256, 32), 1) & 7
    upos = ((pixel & 15).astype(F32) - 7.5) / 128.0
    vpos = ((pixel >> 4).astype(F32) - 7.5) / 128.0
    phi = jnp.where(which == 0, 1.0, 0.0)
    phi = jnp.where(which == 1, upos, phi)
    phi = jnp.where(which == 2, vpos, phi)
    phi = jnp.where(which == 3, upos * upos, phi)
    phi = jnp.where(which == 4, vpos * vpos, phi)
    phi = jnp.where(which == 5, upos * vpos, phi).astype(BF16)
    column = (iota((16, DEPTH), 0).astype(F32) - 7.5) / 128.0
    before = (iota((DEPTH, DEPTH), 0) < iota((DEPTH, DEPTH), 1)).astype(F32).astype(BF16)
    after = (iota((DEPTH, DEPTH), 0) > iota((DEPTH, DEPTH), 1)).astype(F32).astype(BF16)

    def both(ref, tile):
        return jnp.concatenate(
            [ref[pl.ds(2 * tile + h, 32, stride=8), :] for h in range(2)], axis=1
        ).astype(BF16)

    for tile in range(TILES):
        alpha = jnp.exp(dot(phi, both(coef_scr, tile)))
        logs = jnp.log(1.0 - alpha)
        l0 = logs.astype(BF16)
        l1 = (logs - l0.astype(F32)).astype(BF16)
        weight = alpha * jnp.exp(dot(l0, before) + dot(l1, before))
        flow = dot(turned[:, 32 * tile : 32 * tile + 32], both(right_scr, tile)) * weight
        s0 = flow.astype(BF16)
        s1 = (flow - s0.astype(F32)).astype(BF16)
        behind = dot(s0, after) + dot(s1, after)
        power = flow - behind * (alpha * jnp.exp(-logs))
        w0 = weight.astype(BF16)
        w1 = (weight - w0.astype(F32)).astype(BF16)
        colours = dot(sides[tile], w0)
        colours = colours[0:8] + colours[8:16] + dot(sides[tile], w1)[0:8]

        plain = linear = square = None
        for i in range(8):
            vpos = (7.5 - i) / 128.0
            top, bottom = power[16 * i : 16 * i + 16], power[240 - 16 * i : 256 - 16 * i]
            total, slope = top + bottom, (bottom - top) * vpos
            curve = total * (vpos * vpos)
            plain = total if plain is None else plain + total
            linear = slope if linear is None else linear + slope
            square = curve if square is None else square + curve
        sums = [
            plain,
            plain * column,
            linear,
            plain * (column * column),
            square,
            linear * column,
        ]
        rows = [jnp.sum(v, axis=0, keepdims=True) for v in sums]
        rows += [colours[i : i + 1] for i in range(3)]
        for i, row in enumerate(rows):
            for h in range(2):
                sums_scr[8 * i + 2 * tile + h : 8 * i + 2 * tile + h + 1, :] = row[
                    :, 128 * h : 128 * h + 128
                ]

    m0, mu, mv, muu, mvv, muv, red, green, blue = [sums_scr[8 * i : 8 * i + 8, :] for i in range(9)]
    grads = [
        ca * mu + cb * mv - lead_x * m0,
        cc * mv + cb * mu - lead_y * m0,
        -0.5 * (muu - 2.0 * xrel * mu + xrel * xrel * m0),
        -(muv - yrel * mu - xrel * mv + xrel * yrel * m0),
        -0.5 * (mvv - 2.0 * yrel * mv + yrel * yrel * m0),
        jnp.where(shown, m0 / jnp.where(shown, opac, 1.0), 0.0),
        red,
        green,
        blue,
    ]
    grads = [split(grad, 2) for grad in grads]
    peer_iota, place_iota = iota((PEERS, 128), 0), iota((CAP, 128), 0)
    hots, wides = [], []
    for r in range(8):
        hots.append(jnp.where(peer_iota == peer[r : r + 1], 1.0, 0.0).astype(BF16))
        mine = place_iota == place[r : r + 1]
        wides.append(
            jnp.concatenate(
                [
                    jnp.where(mine, grads[c][part][r : r + 1], 0.0)
                    for part in range(2)
                    for c in range(COMPS)
                ],
                axis=0,
            ).astype(BF16)
        )
    total = dot_t(jnp.concatenate(wides, axis=1), jnp.concatenate(hots, axis=1))
    total = total[: 32 * COMPS] + total[32 * COMPS :]
    total = jnp.concatenate([total, jnp.zeros((96, 128), F32)], axis=0)
    for k in range(3):
        out_ref[pl.ds(k, PEERS, stride=3), :] = jnp.transpose(total[128 * k : 128 * k + 128])


def sum_slots(comps, back_ref, idx_ref, cnt_ref, low_scr, high_scr, rows_scr):
    slot_index(idx_ref, cnt_ref, low_scr, high_scr)
    for k in sorted({comp // 4 for comp in comps}):
        block = jnp.concatenate(
            [back_ref[pl.ds(3 * i + k, 32, stride=12), :] for i in range(4)], axis=0
        )
        rows_scr[128 * k : 128 * k + 128, :] = jnp.transpose(block)
    low_iota = iota((LOW, 256), 0)
    high_iota = iota((HIGH, 256), 0)
    hots, wides = [], []
    for pair in range(CAP // 2):
        low, high = pair_row(low_scr, 0, pair), pair_row(high_scr, 0, pair)
        hots.append(jnp.where(low_iota == low, 1.0, 0.0).astype(BF16))
        mask = high_iota == high
        both = [split(pair_row(rows_scr, 32 * comp, pair), 2) for comp in comps]
        wides.append(
            jnp.concatenate(
                [jnp.where(mask, b[part], 0.0) for part in range(2) for b in both], axis=0
            ).astype(BF16)
        )
    total = None
    for i in range(0, CAP // 2, 4):
        term = dot_t(
            jnp.concatenate(wides[i : i + 4], axis=1), jnp.concatenate(hots[i : i + 4], axis=1)
        )
        total = term if total is None else total + term
    size = 32 * len(comps)
    return total[:size] + total[size:]


def colour_sum_kernel(cam_ref, back_ref, idx_ref, cnt_ref, col_ref, low_scr, high_scr, rows_scr):
    total = sum_slots((6, 7, 8), back_ref, idx_ref, cnt_ref, low_scr, high_scr, rows_scr)
    for par in range(2):
        for share in range(4):
            for chan in range(3):
                first = 32 * chan + 8 * share
                col_ref[pl.ds(PACK * share + 16 * chan + par, 8, stride=2), :] = total[
                    first : first + 8, 128 * par : 128 * par + 128
                ]
    lanes = iota((8, 128), 1)
    row = jnp.zeros((8, 128), F32)
    for i in range(3):
        row = jnp.where(lanes == i, jnp.broadcast_to(cam_ref[0:1, i : i + 1], (8, 128)), row)
    for share in range(4):
        col_ref[PACK * share + 48 : PACK * share + 56, :] = row


def row_sum_kernel(back_ref, idx_ref, cnt_ref, out_ref, low_scr, high_scr, rows_scr):
    total = sum_slots(range(6), back_ref, idx_ref, cnt_ref, low_scr, high_scr, rows_scr)
    for par in range(2):
        out_ref[pl.ds(par, 192, stride=2), :] = total[:, 128 * par : 128 * par + 128]


def coeff_kernel(share_ref, col_ref, pos_ref, out_ref):
    consts = basis_consts()
    share = share_ref[0]
    cams = []
    for image in range(4):
        row = col_ref[PACK * image + 48 : PACK * image + 56, :]
        cams.append([jnp.broadcast_to(row[:, i : i + 1], (8, 128)) for i in range(3)])

    def chunk(step, carry):
        lanes = pl.ds(pl.multiple_of(share * 2048 + step * 128, 128), 128)
        place = [jnp.broadcast_to(pos_ref[i : i + 1, lanes], (8, 128)) for i in range(3)]
        totals = [[None, None] for _ in range(3)]
        for image in range(4):
            cam = cams[image]
            halves = basis_halves(
                consts, place[0] - cam[0], place[1] - cam[1], place[2] - cam[2]
            )
            for chan in range(3):
                grad = jnp.broadcast_to(
                    col_ref[pl.ds(PACK * image + 16 * chan + step, 1), :], (8, 128)
                )
                for half in range(2):
                    term = grad * halves[half]
                    old = totals[chan][half]
                    totals[chan][half] = term if old is None else old + term
        here = pl.ds(pl.multiple_of(step * 128, 128), 128)
        for chan in range(3):
            for half in range(2):
                out_ref[16 * chan + 8 * half : 16 * chan + 8 * half + 8, here] = totals[chan][half]
        return carry

    lax.fori_loop(0, 16, chunk, 0, unroll=2)


VMEM = pl.BlockSpec(memory_space=pltpu.VMEM)
SMEM = pl.BlockSpec(memory_space=pltpu.SMEM)
HBM = pl.BlockSpec(memory_space=pltpu.HBM)
PARAMS = pltpu.CompilerParams(vmem_limit_bytes=40 * 1024 * 1024)


def shape(*dims):
    return jax.ShapeDtypeStruct(dims, F32)


def in_hbm(array):
    return pltpu.with_memory_space_constraint(array, pltpu.HBM)


def owner(camera, proj, coeffs, positions, index, count):
    return pl.pallas_call(
        owner_kernel,
        out_shape=shape(384, 128),
        in_specs=[HBM] * 6,
        out_specs=VMEM,
        scratch_shapes=[
            pltpu.VMEM((1, 3), F32),
            pltpu.VMEM((384, 128), F32),
            pltpu.VMEM((48, 8192), F32),
            pltpu.VMEM((3, 8192), F32),
            pltpu.VMEM((CAP, PEERS), jnp.int32),
            pltpu.VMEM((1, PEERS), jnp.int32),
            pltpu.VMEM((192, 128), F32),
            pltpu.VMEM((CAP, PEERS), jnp.int32),
            pltpu.VMEM((CAP, PEERS), jnp.int32),
            pltpu.VMEM((384, 128), F32),
            pltpu.SemaphoreType.DMA((6,)),
        ],
        compiler_params=PARAMS,
        name="owner_rows",
    )(*[in_hbm(x) for x in (camera, proj, coeffs, positions, index, count)])


def render(tile_xy, tile_len, received, tile_list, pixel_grad):
    return pl.pallas_call(
        render_kernel,
        out_shape=shape(384, 128),
        in_specs=[VMEM] * 5,
        out_specs=VMEM,
        scratch_shapes=[
            pltpu.VMEM((384, 128), F32),
            pltpu.VMEM((256, 128), F32),
            pltpu.VMEM((256, 128), F32),
            pltpu.VMEM((72, 128), F32),
        ],
        compiler_params=PARAMS,
        name="render_tiles",
    )(tile_xy, tile_len, received, tile_list, pixel_grad)


SLOT_SCRATCH = (
    pltpu.VMEM((CAP, PEERS), jnp.int32),
    pltpu.VMEM((CAP, PEERS), jnp.int32),
    pltpu.VMEM((384, 128), F32),
)


def sum_colours(camera, returned, index, count):
    return pl.pallas_call(
        colour_sum_kernel,
        out_shape=shape(4 * PACK, 128),
        in_specs=[VMEM] * 4,
        out_specs=VMEM,
        scratch_shapes=SLOT_SCRATCH,
        compiler_params=PARAMS,
        name="colour_sums",
    )(camera, returned, index, count)


def sum_rows(returned, index, count):
    return pl.pallas_call(
        row_sum_kernel,
        out_shape=shape(384, 128),
        in_specs=[VMEM] * 3,
        out_specs=VMEM,
        scratch_shapes=SLOT_SCRATCH,
        compiler_params=PARAMS,
        cost_estimate=pl.CostEstimate(
            flops=2 * 384 * 256 * 4096, bytes_accessed=400_000, transcendentals=0
        ),
        name="row_sums",
    )(returned, index, count)


def coefficients(share, colours, positions):
    return pl.pallas_call(
        coeff_kernel,
        out_shape=shape(48, 2048),
        in_specs=[SMEM] + [VMEM] * 2,
        out_specs=VMEM,
        compiler_params=PARAMS,
        name="coeff_grads",
    )(share, colours, positions)


def exchange(rows, axis, peers):
    sent = rows.reshape(peers, 1, -1)
    got = lax.all_to_all(sent, axis, split_axis=0, concat_axis=0, tiled=True)
    return got.reshape(rows.shape)


def on_device(
    proj,
    sh_coeffs,
    positions,
    camera,
    send_index,
    send_count,
    tile_xy,
    tile_list,
    tile_len,
    pixel_grad,
):
    index = send_index.reshape(CAP, PEERS)
    outgoing = owner(
        camera, proj.reshape(384, 128), sh_coeffs, positions, index, send_count
    )
    received = exchange(outgoing, "cell", PEERS)
    slot_grads = render(
        tile_xy[0], tile_len, received, tile_list[0], pixel_grad.reshape(24, 128)
    )
    returned = exchange(slot_grads, "cell", PEERS)
    colours = exchange(sum_colours(camera, returned, index, send_count), "img", 4)
    grad_rows = sum_rows(returned, index, send_count)
    share = lax.axis_index("img").astype(jnp.int32).reshape(1)
    grad_sh = coefficients(share, colours, positions)
    return (grad_rows.reshape(proj.shape), grad_sh)


def solution(mesh):
    return jax.shard_map(
        on_device,
        mesh=mesh,
        in_specs=(
            P("img", None, "cell"),
            P(None, "cell"),
            P(None, "cell"),
            P("img", None),
            P("img", "cell"),
            P("img", "cell"),
            P("img", None, "cell"),
            P("img", "cell", None),
            P("img", "cell"),
            P("img", None, "cell"),
        ),
        out_specs=(P("img", None, "cell"), P(None, ("cell", "img"))),
        check_vma=False,
    )
```

time: 82.4 us -> 72.1 us (0.87)
  local copies, waits for them, and re-layouts: 5.29 us -> 0.03 us
  Pallas kernels: 16 us -> 12.9 us
  waiting for transfers between devices: 5.89 us -> 3.99 us
    unnamed x24 -> x16, local copies, waits for them, and re-layouts: 5.29 us -> 0.03 us
    pallas_call x3 -> x4, Pallas kernels: 14.6 us -> 11.5 us  [the longest x1 4.73 us: owner(): pl.pallas_call(owner_kernel, out_shape=shape(384, 128), in_specs=[HBM] *...]
    all_to_all x1, waiting for transfers between devices: 5.89 us -> 3.99 us  [exchange(): got = lax.all_to_all(sent, axis, split_axis=0, concat_axis=0, tiled=True)]
  transfers between devices with their start and end apart: 1 -> 1, of which waited for: 1 -> 1; matrix products, arithmetic and copies ran while one was open for 0% -> 0% of each run, Pallas kernels for 0% -> 3%
where the time goes in v2:
time: 72.1 us; the launch traced here: 71.8 us
  blocking collectives  49.8 us (69%)
  Pallas kernels  12.9 us (18%)
  starting transfers between devices  4.43 us (6%)
  waiting for transfers between devices  3.99 us (6%)
    all_to_all x2, blocking collectives, exchange(): got = lax.all_to_all(sent, axis, split_axis=0, concat_axis=0, tiled=True)  49.8 us
    pallas_call x1, Pallas kernels, owner(): pl.pallas_call(owner_kernel, out_shape=shape(384, 128), in_specs=[HBM] *...  4.73 us
    all_to_all x1, starting transfers between devices, exchange(): got = lax.all_to_all(sent, axis, split_axis=0, concat_axis=0, tiled=True)  4.43 us
    all_to_all x1, waiting for transfers between devices, exchange(): got = lax.all_to_all(sent, axis, split_axis=0, concat_axis=0, tiled=True)  3.99 us
    pallas_call x1, Pallas kernels, render(): pl.pallas_call(render_kernel, out_shape=shape(384, 128), in_specs=[VMEM]...  3.16 us
    pallas_call x1, Pallas kernels, sum_rows(): pl.pallas_call(row_sum_kernel, out_shape=shape(384, 128), in_specs=[VMEM]...  1.89 us
    pallas_call x1, Pallas kernels, sum_colours(): pl.pallas_call(colour_sum_kernel, out_shape=shape(4 * PACK, 128), in_spec...  1.67 us
  transfers between devices with their start and end apart: 1, of which 1 were waited for; matrix products, arithmetic and copies ran while one was open for 0% of the time, Pallas kernels for 3%

profile of v2, /device:TPU:8, one launch (start us, length us, event | category | flops | bytes accessed | tf_op | source)
XLA Modules:
  0.0 71.8 jit_solution(7494684981754492300)
XLA Ops:
  0.6 0.0 copy-start.2
  0.6 0.0 copy-start.7
  0.7 0.0 copy-start.3
  0.7 0.0 copy-start.6
  0.7 0.0 copy-start.1
  0.7 0.0 copy-start.4
  0.7 0.0 copy-start.5
  0.7 4.7 %owner_rows.1 = f32[384,128]{1,0:T(8,128)S(1)} custom-call(f32[1,3]{1,0:T(1,128)} %cam_ref.1, f32[384,128]{1,0:T(8,128)} %bitcast.25, f32[48,8192]{1,0:T(8,128)} %sh_hbm.1, f32[3,8192]{1,0:T(4,128)} %pos_ref.1, s32[32,128]{1,0:T(8,128)} %bitcast.19, s32[1,128]{1,0:T(1,128)} %cnt_ref.3), custom_call_target="tpu_custom_call" | custom-call | tf_op jit(solution)/shard_map/owner_rows/pallas_call | solution.py:516
  5.4 30.5 %all_to_all.15 = f32[128,1,384]{2,1,0:T(1,128)S(1)} all-to-all(f32[128,1,384]{2,1,0:T(1,128)S(1)} %bitcast.17), channel_id=1, replica_groups=mesh['cell'=128,'img'=4] {'cell'}, dimensions={0} | all-to-all | bytes 393216 | tf_op jit(solution)/shard_map/all_to_all | solution.py:603
  36.0 0.0 copy-done.2
  36.0 0.0 copy-done.7
  36.0 0.0 copy-done.3
  36.0 0.0 copy-done.6
  36.0 3.2 %render_tiles.1 = f32[384,128]{1,0:T(8,128)S(1)} custom-call(s32[2,4]{1,0:T(2,128)S(1)} %bitcast.24, s32[1,4]{1,0:T(1,128)S(1)} %copy-done.7, f32[384,128]{1,0:T(8,128)S(1)} %bitcast.15, s32[4,256]{1,0:T(4,128)S(1)} %bitcast.23, f32[24,128]{1,0:T(8,128)S(1)} %bitcast.22), custom_call_target="tpu_custom_call" | custom-call | tf_op jit(solution)/shard_map/render_tiles/pallas_call | solution.py:540
  39.2 19.3 %all_to_all.16 = f32[128,1,384]{2,1,0:T(1,128)S(1)} all-to-all(f32[128,1,384]{2,1,0:T(1,128)S(1)} %bitcast.16), channel_id=1, replica_groups=mesh['cell'=128,'img'=4] {'cell'}, dimensions={0} | all-to-all | bytes 393216 | tf_op jit(solution)/shard_map/all_to_all | solution.py:603
  58.4 0.0 copy-done.1
  58.4 0.0 copy-done.4
  58.4 0.0 copy-done.5
  58.4 1.7 %colour_sums.1 = f32[224,128]{1,0:T(8,128)} custom-call(f32[1,3]{1,0:T(1,128)S(1)} %copy-done.4, f32[384,128]{1,0:T(8,128)S(1)} %bitcast.13, s32[32,128]{1,0:T(8,128)S(1)} %bitcast.20, s32[1,128]{1,0:T(1,128)S(1)} %copy-done.5), custom_call_target="tpu_custom_call" | custom-call | tf_op jit(solution)/shard_map/colour_sums/pallas_call | solution.py:564
  60.1 0.0 copy-start
  60.1 4.4 %all-to-all-start.2 = ((f32[4,1,7168]{2,1,0:T(1,128)}), f32[4,1,7168]{2,1,0:T(1,128)S(1)}, u32[]{:S(2)}, u32[]{:S(2)}) async-start(f32[4,1,7168]{2,1,0:T(1,128)} %bitcast.11), calls=%async_computation.2 | async-start | bytes 229376 | tf_op jit(solution)/shard_map/all_to_all | solution.py:603
  64.5 1.9 %row_sums.1 = f32[384,128]{1,0:T(8,128)} custom-call(f32[384,128]{1,0:T(8,128)S(1)} %bitcast.14, s32[32,128]{1,0:T(8,128)S(1)} %bitcast.21, s32[1,128]{1,0:T(1,128)S(1)} %copy-done.5), custom_call_target="tpu_custom_call" | custom-call | flops 805306368 | bytes 400000 | tf_op jit(solution)/shard_map/row_sums/pallas_call | solution.py:576
  66.4 4.0 %all-to-all-done.2 = f32[4,1,7168]{2,1,0:T(1,128)S(1)} async-done(((f32[4,1,7168]{2,1,0:T(1,128)}), f32[4,1,7168]{2,1,0:T(1,128)S(1)}, u32[]{:S(2)}, u32[]{:S(2)}) %all-to-all-start.2) | async-done | bytes 114720 | tf_op jit(solution)/shard_map/all_to_all | solution.py:603
  70.4 0.0 copy-done
  70.4 1.4 %coeff_grads.1 = f32[48,2048]{1,0:T(8,128)} custom-call(s32[1]{0:T(128)} %bitcast.10.share_ref, f32[224,128]{1,0:T(8,128)S(1)} %bitcast.18, f32[3,8192]{1,0:T(4,128)S(1)} %copy-done), custom_call_target="tpu_custom_call" | custom-call | tf_op jit(solution)/shard_map/coeff_grads/pallas_call | solution.py:591
Async XLA Ops:
  0.6 35.3 %copy-start.2 = (f32[1,3,1024]{2,0,1:T(1,128)S(1)}, f32[1,3,1024]{2,0,1:T(1,128)}, u32[]{:S(2)}) copy-start(f32[1,3,1024]{2,0,1:T(1,128)} %param.19) | copy-start | bytes 36868
  0.6 35.3 %copy-start.7 = (s32[1,4]{1,0:T(1,128)S(1)}, s32[1,4]{1,0:T(1,128)}, u32[]{:S(2)}) copy-start(s32[1,4]{1,0:T(1,128)} %len_ref.1) | copy-start | bytes 52
  0.7 35.3 %copy-start.3 = (s32[1,4,256]{2,1,0:T(4,128)S(1)}, s32[1,4,256]{2,1,0:T(4,128)}, u32[]{:S(2)}) copy-start(s32[1,4,256]{2,1,0:T(4,128)} %param.17) | copy-start | bytes 12292
  0.7 35.3 %copy-start.6 = (s32[1,2,4]{2,1,0:T(2,128)S(1)}, s32[1,2,4]{2,1,0:T(2,128)}, u32[]{:S(2)}) copy-start(s32[1,2,4]{2,1,0:T(2,128)} %param.16) | copy-start | bytes 100
  0.7 57.8 %copy-start.1 = (s32[1,4096]{1,0:T(1,128)S(1)}, s32[1,4096]{1,0:T(1,128)}, u32[]{:S(2)}) copy-start(s32[1,4096]{1,0:T(1,128)} %param.14) | copy-start | bytes 49156
  0.7 57.7 %copy-start.4 = (f32[1,3]{1,0:T(1,128)S(1)}, f32[1,3]{1,0:T(1,128)}, u32[]{:S(2)}) copy-start(f32[1,3]{1,0:T(1,128)} %cam_ref.1) | copy-start | bytes 40
  0.7 57.7 %copy-start.5 = (s32[1,128]{1,0:T(1,128)S(1)}, s32[1,128]{1,0:T(1,128)}, u32[]{:S(2)}) copy-start(s32[1,128]{1,0:T(1,128)} %cnt_ref.3) | copy-start | bytes 1540
  60.1 10.3 %copy-start = (f32[3,8192]{1,0:T(4,128)S(1)}, f32[3,8192]{1,0:T(4,128)}, u32[]{:S(2)}) copy-start(f32[3,8192]{1,0:T(4,128)} %pos_ref.1) | copy-start | bytes 294916
  60.1 10.3 %all-to-all-start.2 = ((f32[4,1,7168]{2,1,0:T(1,128)}), f32[4,1,7168]{2,1,0:T(1,128)S(1)}, u32[]{:S(2)}, u32[]{:S(2)}) async-start(f32[4,1,7168]{2,1,0:T(1,128)} %bitcast.11), calls=%async_computation.2 | async-start | bytes 229376 | tf_op jit(solution)/shard_map/all_to_all | solution.py:603

commit v3 on v2

--- a/solution.py
+++ b/solution.py
@@ -37,6 +37,8 @@
 HIGH = 32
 PACK = 56
 NOTHING = -1.0e4
+EARLY = 6
+ALONE = 3
 
 LINEAR = (
     (SH_ZERO, 0, 0, 0),
@@ -84,6 +86,16 @@
     return lax.dot_general(left, right, (((1,), (1,)), ((), ())), preferred_element_type=F32)
 
 
+def one_hot(rows, index):
+    same = rows.astype(jnp.int16) == index.astype(jnp.int16)
+    return jnp.where(same, jnp.ones((), BF16), jnp.zeros((), BF16))
+
+
+def stacked(first, second, right):
+    both = dot(jnp.concatenate([first, second], axis=0), right)
+    return both[: first.shape[0]] + both[first.shape[0] :]
+
+
 def iota(shape, axis):
     return lax.broadcasted_iota(jnp.int32, shape, axis)
 
@@ -164,6 +176,8 @@
     idx_hbm,
     cnt_hbm,
     out_ref,
+    high_scr,
+    hot_ref,
     cam_ref,
     proj_ref,
     sh_ref,
@@ -172,7 +186,6 @@
     cnt_ref,
     col_scr,
     low_scr,
-    high_scr,
     rows_scr,
     sems,
 ):
@@ -182,10 +195,10 @@
             (
                 (idx_hbm, idx_ref),
                 (cnt_hbm, cnt_ref),
+                (proj_hbm, proj_ref),
                 (cam_hbm, cam_ref),
                 (pos_hbm, pos_ref),
                 (sh_hbm, sh_ref),
-                (proj_hbm, proj_ref),
             )
         )
     ]
@@ -195,45 +208,72 @@
     for copy in copies[:2]:
         copy.wait()
     slot_index(idx_ref, cnt_ref, low_scr, high_scr)
-    for copy in copies[2:5]:
-        copy.wait()
-    cam = [jnp.broadcast_to(cam_ref[0:1, i : i + 1], (8, 128)) for i in range(3)]
-
-    def shade(chunk, carry):
-        lanes = pl.ds(pl.multiple_of(chunk * 128, 128), 128)
+    low_iota = iota((LOW, 256), 0)
+    high_iota = iota((HIGH, 256), 0)
+
+    def table(ref, comps):
+        return jnp.concatenate(
+            [ref[pl.ds(par, 32 * comps, stride=2), :] for par in range(2)], axis=1
+        )
+
+    def pick(wide, mask, base, comps, pair):
+        for comp in range(comps):
+            row = jnp.sum(
+                jnp.where(mask, wide[32 * comp : 32 * comp + 32], 0.0), axis=0, keepdims=True
+            )
+            at = 32 * (base + comp) + 2 * pair
+            rows_scr[at : at + 1, :] = row[:, :128]
+            rows_scr[at + 1 : at + 2, :] = row[:, 128:]
+
+    def shade(chunk):
+        lanes = slice(128 * chunk, 128 * chunk + 128)
         offs = [jnp.broadcast_to(pos_ref[i : i + 1, lanes], (8, 128)) - cam[i] for i in range(3)]
         first, second = basis_halves(consts, *offs)
         for chan in range(3):
             terms = sh_ref[16 * chan : 16 * chan + 8, lanes] * first
             terms = terms + sh_ref[16 * chan + 8 : 16 * chan + 16, lanes] * second
             colour = jnp.sum(terms, axis=0, keepdims=True) + 0.5
-            col_scr[pl.ds(64 * chan + chunk, 1), :] = colour
-        return carry
-
-    lax.fori_loop(0, 64, shade, 0, unroll=16)
-    copies[5].wait()
-
-    even = jnp.concatenate(
-        [proj_ref[pl.ds(0, 192, stride=2), :], col_scr[pl.ds(0, 96, stride=2), :]], axis=0
-    )
-    odd = jnp.concatenate(
-        [proj_ref[pl.ds(1, 192, stride=2), :], col_scr[pl.ds(1, 96, stride=2), :]], axis=0
-    )
-    parts = [part.astype(BF16) for part in split(jnp.concatenate([even, odd], axis=1), 3)]
-    low_iota = iota((LOW, 256), 0)
-    high_iota = iota((HIGH, 256), 0)
-
-    for pair in range(CAP // 2):
-        low, high = pair_row(low_scr, 0, pair), pair_row(high_scr, 0, pair)
-        hot = jnp.where(low_iota == low, 1.0, 0.0).astype(BF16)
-        wide = dot(parts[0], hot) + dot(parts[1], hot) + dot(parts[2], hot)
-        mask = high_iota == high
-        for comp in range(COMPS):
-            row = jnp.sum(
-                jnp.where(mask, wide[32 * comp : 32 * comp + 32], 0.0), axis=0, keepdims=True
-            )
-            rows_scr[32 * comp + 2 * pair : 32 * comp + 2 * pair + 1, :] = row[:, :128]
-            rows_scr[32 * comp + 2 * pair + 1 : 32 * comp + 2 * pair + 2, :] = row[:, 128:]
+            at = 64 * chan + chunk
+            col_scr[at : at + 1, :] = colour
+
+    def hots(pair):
+        hot = one_hot(low_iota, pair_row(low_scr, 0, pair))
+        hot_ref[:, 256 * pair : 256 * pair + 256] = hot
+        return hot
+
+    def mask(pair):
+        return high_iota == pair_row(high_scr, 0, pair)
+
+    copies[2].wait()
+    rows = split(table(proj_ref, 6), 3)
+    rows = jnp.concatenate([rows[0], rows[1], rows[2][:160]], axis=0).astype(BF16)
+
+    def sum_rows(wide):
+        exact = wide[:160] + wide[192:352] + wide[384:544]
+        return jnp.concatenate([exact, wide[160:192] + wide[352:384]], axis=0)
+
+    cam, chunk = None, 0
+    for pair in range(EARLY):
+        hot = hots(pair)
+        pick(sum_rows(dot(rows, hot)), mask(pair), 0, 6, pair)
+        if pair == ALONE - 1:
+            for copy in copies[3:]:
+                copy.wait()
+            cam = [jnp.broadcast_to(cam_ref[0:1, i : i + 1], (8, 128)) for i in range(3)]
+        if pair >= ALONE:
+            for _ in range(-(-64 // (EARLY - ALONE))):
+                if chunk < 64:
+                    shade(chunk)
+                    chunk += 1
+    tints = jnp.concatenate(split(table(col_scr, 3), 2), axis=0).astype(BF16)
+    everything = jnp.concatenate([rows, tints], axis=0)
+    for pair in range(EARLY, CAP // 2):
+        wide = dot(everything, hots(pair))
+        pick(sum_rows(wide), mask(pair), 0, 6, pair)
+        pick(wide[544:640] + wide[640:736], mask(pair), 6, 3, pair)
+    for pair in range(EARLY):
+        wide = dot(tints, hot_ref[:, 256 * pair : 256 * pair + 256])
+        pick(wide[:96] + wide[96:], mask(pair), 6, 3, pair)
 
     rows_scr[32 * COMPS :, :] = jnp.zeros((96, 128), F32)
     for k in range(3):
@@ -340,11 +380,11 @@
         logs = jnp.log(1.0 - alpha)
         l0 = logs.astype(BF16)
         l1 = (logs - l0.astype(F32)).astype(BF16)
-        weight = alpha * jnp.exp(dot(l0, before) + dot(l1, before))
+        weight = alpha * jnp.exp(stacked(l0, l1, before))
         flow = dot(turned[:, 32 * tile : 32 * tile + 32], both(right_scr, tile)) * weight
         s0 = flow.astype(BF16)
         s1 = (flow - s0.astype(F32)).astype(BF16)
-        behind = dot(s0, after) + dot(s1, after)
+        behind = stacked(s0, s1, after)
         power = flow - behind * (alpha * jnp.exp(-logs))
         w0 = weight.astype(BF16)
         w1 = (weight - w0.astype(F32)).astype(BF16)
@@ -411,38 +451,34 @@
         out_ref[pl.ds(k, PEERS, stride=3), :] = jnp.transpose(total[128 * k : 128 * k + 128])
 
 
-def sum_slots(comps, back_ref, idx_ref, cnt_ref, low_scr, high_scr, rows_scr):
-    slot_index(idx_ref, cnt_ref, low_scr, high_scr)
+def sum_slots(comps, back_ref, high_ref, hot_ref, rows_scr):
     for k in sorted({comp // 4 for comp in comps}):
         block = jnp.concatenate(
             [back_ref[pl.ds(3 * i + k, 32, stride=12), :] for i in range(4)], axis=0
         )
         rows_scr[128 * k : 128 * k + 128, :] = jnp.transpose(block)
-    low_iota = iota((LOW, 256), 0)
     high_iota = iota((HIGH, 256), 0)
-    hots, wides = [], []
-    for pair in range(CAP // 2):
-        low, high = pair_row(low_scr, 0, pair), pair_row(high_scr, 0, pair)
-        hots.append(jnp.where(low_iota == low, 1.0, 0.0).astype(BF16))
-        mask = high_iota == high
-        both = [split(pair_row(rows_scr, 32 * comp, pair), 2) for comp in comps]
-        wides.append(
-            jnp.concatenate(
-                [jnp.where(mask, b[part], 0.0) for part in range(2) for b in both], axis=0
-            ).astype(BF16)
-        )
     total = None
-    for i in range(0, CAP // 2, 4):
+    for step in range(4):
+        wides = []
+        for pair in range(4 * step, 4 * step + 4):
+            mask = high_iota == pair_row(high_ref, 0, pair)
+            both = [split(pair_row(rows_scr, 32 * comp, pair), 2) for comp in comps]
+            wides.append(
+                jnp.concatenate(
+                    [jnp.where(mask, b[part], 0.0) for part in range(2) for b in both], axis=0
+                ).astype(BF16)
+            )
         term = dot_t(
-            jnp.concatenate(wides[i : i + 4], axis=1), jnp.concatenate(hots[i : i + 4], axis=1)
+            jnp.concatenate(wides, axis=1), hot_ref[:, 1024 * step : 1024 * step + 1024]
         )
         total = term if total is None else total + term
     size = 32 * len(comps)
     return total[:size] + total[size:]
 
 
-def colour_sum_kernel(cam_ref, back_ref, idx_ref, cnt_ref, col_ref, low_scr, high_scr, rows_scr):
-    total = sum_slots((6, 7, 8), back_ref, idx_ref, cnt_ref, low_scr, high_scr, rows_scr)
+def colour_sum_kernel(cam_ref, back_ref, high_ref, hot_ref, col_ref, rows_scr):
+    total = sum_slots((6, 7, 8), back_ref, high_ref, hot_ref, rows_scr)
     for par in range(2):
         for share in range(4):
             for chan in range(3):
@@ -458,8 +494,8 @@
         col_ref[PACK * share + 48 : PACK * share + 56, :] = row
 
 
-def row_sum_kernel(back_ref, idx_ref, cnt_ref, out_ref, low_scr, high_scr, rows_scr):
-    total = sum_slots(range(6), back_ref, idx_ref, cnt_ref, low_scr, high_scr, rows_scr)
+def row_sum_kernel(back_ref, high_ref, hot_ref, out_ref, rows_scr):
+    total = sum_slots(range(6), back_ref, high_ref, hot_ref, rows_scr)
     for par in range(2):
         out_ref[pl.ds(par, 192, stride=2), :] = total[:, 128 * par : 128 * par + 128]
 
@@ -495,7 +531,7 @@
                 out_ref[16 * chan + 8 * half : 16 * chan + 8 * half + 8, here] = totals[chan][half]
         return carry
 
-    lax.fori_loop(0, 16, chunk, 0, unroll=2)
+    lax.fori_loop(0, 16, chunk, 0, unroll=16)
 
 
 VMEM = pl.BlockSpec(memory_space=pltpu.VMEM)
@@ -515,9 +551,13 @@
 def owner(camera, proj, coeffs, positions, index, count):
     return pl.pallas_call(
         owner_kernel,
-        out_shape=shape(384, 128),
+        out_shape=(
+            shape(384, 128),
+            jax.ShapeDtypeStruct((CAP, PEERS), jnp.int32),
+            jax.ShapeDtypeStruct((LOW, CAP * PEERS), BF16),
+        ),
         in_specs=[HBM] * 6,
-        out_specs=VMEM,
+        out_specs=[VMEM] * 3,
         scratch_shapes=[
             pltpu.VMEM((1, 3), F32),
             pltpu.VMEM((384, 128), F32),
@@ -526,7 +566,6 @@
             pltpu.VMEM((CAP, PEERS), jnp.int32),
             pltpu.VMEM((1, PEERS), jnp.int32),
             pltpu.VMEM((192, 128), F32),
-            pltpu.VMEM((CAP, PEERS), jnp.int32),
             pltpu.VMEM((CAP, PEERS), jnp.int32),
             pltpu.VMEM((384, 128), F32),
             pltpu.SemaphoreType.DMA((6,)),
@@ -553,38 +592,31 @@
     )(tile_xy, tile_len, received, tile_list, pixel_grad)
 
 
-SLOT_SCRATCH = (
-    pltpu.VMEM((CAP, PEERS), jnp.int32),
-    pltpu.VMEM((CAP, PEERS), jnp.int32),
-    pltpu.VMEM((384, 128), F32),
-)
-
-
-def sum_colours(camera, returned, index, count):
+def sum_colours(camera, returned, high, low_hot):
     return pl.pallas_call(
         colour_sum_kernel,
         out_shape=shape(4 * PACK, 128),
         in_specs=[VMEM] * 4,
         out_specs=VMEM,
-        scratch_shapes=SLOT_SCRATCH,
+        scratch_shapes=[pltpu.VMEM((384, 128), F32)],
         compiler_params=PARAMS,
         name="colour_sums",
-    )(camera, returned, index, count)
-
-
-def sum_rows(returned, index, count):
+    )(camera, returned, high, low_hot)
+
+
+def sum_rows(returned, high, low_hot):
     return pl.pallas_call(
         row_sum_kernel,
         out_shape=shape(384, 128),
         in_specs=[VMEM] * 3,
         out_specs=VMEM,
-        scratch_shapes=SLOT_SCRATCH,
+        scratch_shapes=[pltpu.VMEM((384, 128), F32)],
         compiler_params=PARAMS,
         cost_estimate=pl.CostEstimate(
             flops=2 * 384 * 256 * 4096, bytes_accessed=400_000, transcendentals=0
         ),
         name="row_sums",
-    )(returned, index, count)
+    )(returned, high, low_hot)
 
 
 def coefficients(share, colours, positions):
@@ -617,7 +649,7 @@
     pixel_grad,
 ):
     index = send_index.reshape(CAP, PEERS)
-    outgoing = owner(
+    outgoing, high, low_hot = owner(
         camera, proj.reshape(384, 128), sh_coeffs, positions, index, send_count
     )
     received = exchange(outgoing, "cell", PEERS)
@@ -625,8 +657,8 @@
         tile_xy[0], tile_len, received, tile_list[0], pixel_grad.reshape(24, 128)
     )
     returned = exchange(slot_grads, "cell", PEERS)
-    colours = exchange(sum_colours(camera, returned, index, send_count), "img", 4)
-    grad_rows = sum_rows(returned, index, send_count)
+    colours = exchange(sum_colours(camera, returned, high, low_hot), "img", 4)
+    grad_rows = sum_rows(returned, high, low_hot)
     share = lax.axis_index("img").astype(jnp.int32).reshape(1)
     grad_sh = coefficients(share, colours, positions)
     return (grad_rows.reshape(proj.shape), grad_sh)

time: 72.1 us -> 71.1 us (0.986)
  Pallas kernels: 12.9 us -> 11.6 us
  transfers between devices with their start and end apart: 1 -> 1, of which waited for: 1 -> 1; matrix products, arithmetic and copies ran while one was open for 0% -> 0% of each run, Pallas kernels for 3% -> 2%
where the time goes in v3:
time: 71.1 us; the launch traced here: 70.8 us
  blocking collectives  49.8 us (70%)
  Pallas kernels  11.6 us (16%)
  starting transfers between devices  4.42 us (6%)
  waiting for transfers between devices  4.18 us (6%)
    all_to_all x2, blocking collectives, exchange(): got = lax.all_to_all(sent, axis, split_axis=0, concat_axis=0, tiled=True)  49.8 us
    all_to_all x1, starting transfers between devices, exchange(): got = lax.all_to_all(sent, axis, split_axis=0, concat_axis=0, tiled=True)  4.42 us
    all_to_all x1, waiting for transfers between devices, exchange(): got = lax.all_to_all(sent, axis, split_axis=0, concat_axis=0, tiled=True)  4.18 us
    pallas_call x1, Pallas kernels, owner(): pl.pallas_call(owner_kernel, out_shape=(shape(384, 128), jax.ShapeDtypeSt...  4.01 us
    pallas_call x1, Pallas kernels, render(): pl.pallas_call(render_kernel, out_shape=shape(384, 128), in_specs=[VMEM]...  3.06 us
    pallas_call x1, Pallas kernels, sum_rows(): pl.pallas_call(row_sum_kernel, out_shape=shape(384, 128), in_specs=[VMEM]...  1.71 us
    pallas_call x1, Pallas kernels, sum_colours(): pl.pallas_call(colour_sum_kernel, out_shape=shape(4 * PACK, 128), in_spec...  1.52 us
  transfers between devices with their start and end apart: 1, of which 1 were waited for; matrix products, arithmetic and copies ran while one was open for 0% of the time, Pallas kernels for 2%

profile of v3, /device:TPU:8, one launch (start us, length us, event | category | flops | bytes accessed | tf_op | source)
XLA Modules:
  0.0 70.8 jit_solution(7533629513772675244)
XLA Ops:
  0.6 0.0 copy-start.3
  0.6 0.0 copy-start.1
  0.7 0.0 copy-start.5
  0.7 0.0 copy-start.2
  0.7 0.0 copy-start.4
  0.7 4.0 %owner_rows.1 = (f32[384,128]{1,0:T(8,128)S(1)}, s32[32,128]{1,0:T(8,128)S(1)}, bf16[256,4096]{1,0:T(8,128)(2,1)S(1)}) custom-call(f32[1,3]{1,0:T(1,128)} %cam_ref.1, f32[384,128]{1,0:T(8,128)} %bitcast.22, f32[48,8192]{1,0:T(8,128)} %sh_hbm.1, f32[3,8192]{1,0:T(4,128)} %pos_ref.1, s32[32,128]{1,0:T(8,128)} %bitcast.23, s32[1,128]{1,0:T(1,128)} %cnt_hbm.1), custom_call_target="tpu_custom_call" | custom-call | tf_op jit(solution)/shard_map/owner_rows/pallas_call | solution.py:552
  4.7 30.5 %all_to_all.15 = f32[128,1,384]{2,1,0:T(1,128)S(1)} all-to-all(f32[128,1,384]{2,1,0:T(1,128)S(1)} %bitcast.18), channel_id=1, replica_groups=mesh['cell'=128,'img'=4] {'cell'}, dimensions={0} | all-to-all | bytes 393216 | tf_op jit(solution)/shard_map/all_to_all | solution.py:635
  35.2 0.0 copy-done.1
  35.2 0.0 copy-done.5
  35.3 0.0 copy-done.2
  35.3 0.0 copy-done.4
  35.3 3.1 %render_tiles.1 = f32[384,128]{1,0:T(8,128)S(1)} custom-call(s32[2,4]{1,0:T(2,128)S(1)} %bitcast.21, s32[1,4]{1,0:T(1,128)S(1)} %copy-done.5, f32[384,128]{1,0:T(8,128)S(1)} %bitcast.13, s32[4,256]{1,0:T(4,128)S(1)} %bitcast.20, f32[24,128]{1,0:T(8,128)S(1)} %bitcast.19), custom_call_target="tpu_custom_call" | custom-call | tf_op jit(solution)/shard_map/render_tiles/pallas_call | solution.py:579
  38.3 19.3 %all_to_all.16 = f32[128,1,384]{2,1,0:T(1,128)S(1)} all-to-all(f32[128,1,384]{2,1,0:T(1,128)S(1)} %bitcast.14), channel_id=1, replica_groups=mesh['cell'=128,'img'=4] {'cell'}, dimensions={0} | all-to-all | bytes 393216 | tf_op jit(solution)/shard_map/all_to_all | solution.py:635
  57.6 0.0 copy-done.3
  57.6 1.5 %colour_sums.1 = f32[224,128]{1,0:T(8,128)} custom-call(f32[1,3]{1,0:T(1,128)S(1)} %copy-done.3, f32[384,128]{1,0:T(8,128)S(1)} %bitcast.15, s32[32,128]{1,0:T(8,128)S(1)} %get-tuple-element.6.high_ref, bf16[256,4096]{1,0:T(8,128)(2,1)S(1)} %get-tuple-element.7.hot_ref), custom_call_target="tpu_custom_call" | custom-call | tf_op jit(solution)/shard_map/colour_sums/pallas_call | solution.py:596
  59.1 0.0 copy-start
  59.1 4.4 %all-to-all-start.2 = ((f32[4,1,7168]{2,1,0:T(1,128)}), f32[4,1,7168]{2,1,0:T(1,128)S(1)}, u32[]{:S(2)}, u32[]{:S(2)}) async-start(f32[4,1,7168]{2,1,0:T(1,128)} %bitcast.11), calls=%async_computation.2 | async-start | bytes 229376 | tf_op jit(solution)/shard_map/all_to_all | solution.py:635
  63.5 1.7 %row_sums.1 = f32[384,128]{1,0:T(8,128)} custom-call(f32[384,128]{1,0:T(8,128)S(1)} %bitcast.16, s32[32,128]{1,0:T(8,128)S(1)} %get-tuple-element.6.high_ref, bf16[256,4096]{1,0:T(8,128)(2,1)S(1)} %get-tuple-element.7.hot_ref), custom_call_target="tpu_custom_call" | custom-call | flops 805306368 | bytes 400000 | tf_op jit(solution)/shard_map/row_sums/pallas_call | solution.py:608
  65.3 4.2 %all-to-all-done.2 = f32[4,1,7168]{2,1,0:T(1,128)S(1)} async-done(((f32[4,1,7168]{2,1,0:T(1,128)}), f32[4,1,7168]{2,1,0:T(1,128)S(1)}, u32[]{:S(2)}, u32[]{:S(2)}) %all-to-all-start.2) | async-done | bytes 114720 | tf_op jit(solution)/shard_map/all_to_all | solution.py:635
  69.4 0.0 copy-done
  69.4 1.3 %coeff_grads.1 = f32[48,2048]{1,0:T(8,128)} custom-call(s32[1]{0:T(128)} %bitcast.10.share_ref, f32[224,128]{1,0:T(8,128)S(1)} %bitcast.17, f32[3,8192]{1,0:T(4,128)S(1)} %copy-done), custom_call_target="tpu_custom_call" | custom-call | tf_op jit(solution)/shard_map/coeff_grads/pallas_call | solution.py:623
Async XLA Ops:
  0.6 57.0 %copy-start.3 = (f32[1,3]{1,0:T(1,128)S(1)}, f32[1,3]{1,0:T(1,128)}, u32[]{:S(2)}) copy-start(f32[1,3]{1,0:T(1,128)} %cam_ref.1) | copy-start | bytes 40
  0.6 34.6 %copy-start.1 = (f32[1,3,1024]{2,0,1:T(1,128)S(1)}, f32[1,3,1024]{2,0,1:T(1,128)}, u32[]{:S(2)}) copy-start(f32[1,3,1024]{2,0,1:T(1,128)} %param.19) | copy-start | bytes 36868
  0.7 34.6 %copy-start.5 = (s32[1,4]{1,0:T(1,128)S(1)}, s32[1,4]{1,0:T(1,128)}, u32[]{:S(2)}) copy-start(s32[1,4]{1,0:T(1,128)} %len_ref.1) | copy-start | bytes 52
  0.7 34.6 %copy-start.2 = (s32[1,4,256]{2,1,0:T(4,128)S(1)}, s32[1,4,256]{2,1,0:T(4,128)}, u32[]{:S(2)}) copy-start(s32[1,4,256]{2,1,0:T(4,128)} %param.17) | copy-start | bytes 12292
  0.7 34.6 %copy-start.4 = (s32[1,2,4]{2,1,0:T(2,128)S(1)}, s32[1,2,4]{2,1,0:T(2,128)}, u32[]{:S(2)}) copy-start(s32[1,2,4]{2,1,0:T(2,128)} %param.16) | copy-start | bytes 100
  59.1 10.3 %copy-start = (f32[3,8192]{1,0:T(4,128)S(1)}, f32[3,8192]{1,0:T(4,128)}, u32[]{:S(2)}) copy-start(f32[3,8192]{1,0:T(4,128)} %pos_ref.1) | copy-start | bytes 294916
  59.1 10.3 %all-to-all-start.2 = ((f32[4,1,7168]{2,1,0:T(1,128)}), f32[4,1,7168]{2,1,0:T(1,128)S(1)}, u32[]{:S(2)}, u32[]{:S(2)}) async-start(f32[4,1,7168]{2,1,0:T(1,128)} %bitcast.11), calls=%async_computation.2 | async-start | bytes 229376 | tf_op jit(solution)/shard_map/all_to_all | solution.py:635

commit v4 on v3

--- a/solution.py
+++ b/solution.py
@@ -37,6 +37,7 @@
 HIGH = 32
 PACK = 56
 NOTHING = -1.0e4
+LOG2E = 1.4426950408889634
 EARLY = 6
 ALONE = 3
 
@@ -165,6 +166,12 @@
 def pair_row(ref, base, pair):
     first = ref[pl.ds(base + 2 * pair, 1), :]
     second = ref[pl.ds(base + 2 * pair + 1, 1), :]
+    return jnp.concatenate([first, second], axis=1)
+
+
+def returned_row(ref, base, pair):
+    first = ref[pl.ds(base + pair, 1), :]
+    second = ref[pl.ds(base + CAP // 2 + pair, 1), :]
     return jnp.concatenate([first, second], axis=1)
 
 
@@ -323,13 +330,8 @@
     lead_y = cc * yrel + cb * xrel
     const = -0.5 * (xrel * lead_x + yrel * lead_y) + jnp.log(jnp.where(shown, opac, 1.0))
     const = jnp.where(shown & inside, const, NOTHING)
-    zero = jnp.zeros((8, 128), F32)
-    coef = [split(v, 3) for v in (const, lead_x, lead_y, -0.5 * ca, -0.5 * cc, -cb, zero, zero)]
-    for part in range(3):
-        for i in range(8):
-            at = 64 * part + 8 * i
-            coef_scr[at : at + 8, :] = coef[i][part]
-    coef_scr[192:256, :] = jnp.zeros((64, 128), F32)
+    for i, value in enumerate((const, lead_x, lead_y, -0.5 * ca, -0.5 * cc, -cb)):
+        coef_scr[8 * i : 8 * i + 8, :] = LOG2E * value
     tint = [split(v, 3) for v in vals[6:9]]
     for block, (one, two) in enumerate(((0, 0), (1, 0), (2, 1))):
         for c in range(3):
@@ -357,15 +359,6 @@
         sides.append(jnp.concatenate([g0, zero5, g1, zero5], axis=0).astype(BF16))
     turned = jnp.transpose(jnp.concatenate(blocks, axis=0)).astype(BF16)
 
-    pixel, which = iota((256, 32), 0), iota((256, 32), 1) & 7
-    upos = ((pixel & 15).astype(F32) - 7.5) / 128.0
-    vpos = ((pixel >> 4).astype(F32) - 7.5) / 128.0
-    phi = jnp.where(which == 0, 1.0, 0.0)
-    phi = jnp.where(which == 1, upos, phi)
-    phi = jnp.where(which == 2, vpos, phi)
-    phi = jnp.where(which == 3, upos * upos, phi)
-    phi = jnp.where(which == 4, vpos * vpos, phi)
-    phi = jnp.where(which == 5, upos * vpos, phi).astype(BF16)
     column = (iota((16, DEPTH), 0).astype(F32) - 7.5) / 128.0
     before = (iota((DEPTH, DEPTH), 0) < iota((DEPTH, DEPTH), 1)).astype(F32).astype(BF16)
     after = (iota((DEPTH, DEPTH), 0) > iota((DEPTH, DEPTH), 1)).astype(F32).astype(BF16)
@@ -375,17 +368,40 @@
             [ref[pl.ds(2 * tile + h, 32, stride=8), :] for h in range(2)], axis=1
         ).astype(BF16)
 
-    for tile in range(TILES):
-        alpha = jnp.exp(dot(phi, both(coef_scr, tile)))
+    side = [column[8 * g : 8 * g + 8, :128] for g in range(2)]
+
+    def exponents(tile):
+        halves = []
+        for h in range(2):
+            at = 2 * tile + h
+            rows = [
+                jnp.broadcast_to(coef_scr[8 * i + at : 8 * i + at + 1, :], (8, 128))
+                for i in range(6)
+            ]
+            along = [rows[0] + u * (rows[1] + u * rows[3]) for u in side]
+            across = [rows[2] + u * rows[5] for u in side]
+            blocks = []
+            for i in range(16):
+                vpos = (i - 7.5) / 128.0
+                bend = vpos * rows[4]
+                blocks += [along[g] + vpos * (across[g] + bend) for g in range(2)]
+            halves.append(jnp.concatenate(blocks, axis=0))
+        return jnp.concatenate(halves, axis=1)
+
+    def front(tile):
+        alpha = jnp.exp2(exponents(tile))
         logs = jnp.log(1.0 - alpha)
         l0 = logs.astype(BF16)
-        l1 = (logs - l0.astype(F32)).astype(BF16)
+        return alpha, logs, l0, (logs - l0.astype(F32)).astype(BF16)
+
+    def middle(tile, alpha, logs, l0, l1):
         weight = alpha * jnp.exp(stacked(l0, l1, before))
         flow = dot(turned[:, 32 * tile : 32 * tile + 32], both(right_scr, tile)) * weight
         s0 = flow.astype(BF16)
-        s1 = (flow - s0.astype(F32)).astype(BF16)
-        behind = stacked(s0, s1, after)
-        power = flow - behind * (alpha * jnp.exp(-logs))
+        return weight, flow, s0, (flow - s0.astype(F32)).astype(BF16)
+
+    def back(tile, alpha, logs, weight, flow, s0, s1):
+        power = flow - stacked(s0, s1, after) * (alpha * jnp.exp(-logs))
         w0 = weight.astype(BF16)
         w1 = (weight - w0.astype(F32)).astype(BF16)
         colours = dot(sides[tile], w0)
@@ -416,6 +432,13 @@
                     :, 128 * h : 128 * h + 128
                 ]
 
+    for first in range(0, TILES, 2):
+        group = (first, first + 1)
+        fronts = [front(tile) for tile in group]
+        middles = [middle(tile, *fronts[tile - first]) for tile in group]
+        for tile in group:
+            back(tile, *fronts[tile - first][:2], *middles[tile - first])
+
     m0, mu, mv, muu, mvv, muv, red, green, blue = [sums_scr[8 * i : 8 * i + 8, :] for i in range(9)]
     grads = [
         ca * mu + cb * mv - lead_x * m0,
@@ -429,11 +452,12 @@
         blue,
     ]
     grads = [split(grad, 2) for grad in grads]
-    peer_iota, place_iota = iota((PEERS, 128), 0), iota((CAP, 128), 0)
+    column_iota, place_iota = iota((2 * PEERS, 128), 0), iota((CAP // 2, 128), 0)
+    column_of, row_of = peer + PEERS * (place & 1), place >> 1
     hots, wides = [], []
     for r in range(8):
-        hots.append(jnp.where(peer_iota == peer[r : r + 1], 1.0, 0.0).astype(BF16))
-        mine = place_iota == place[r : r + 1]
+        hots.append(one_hot(column_iota, column_of[r : r + 1]))
+        mine = place_iota == row_of[r : r + 1]
         wides.append(
             jnp.concatenate(
                 [
@@ -445,8 +469,17 @@
             ).astype(BF16)
         )
     total = dot_t(jnp.concatenate(wides, axis=1), jnp.concatenate(hots, axis=1))
-    total = total[: 32 * COMPS] + total[32 * COMPS :]
-    total = jnp.concatenate([total, jnp.zeros((96, 128), F32)], axis=0)
+    half = 16 * COMPS
+    total = total[:half] + total[half:]
+    total = jnp.concatenate(
+        [
+            total[16 * c : 16 * c + 16, PEERS * bit : PEERS * bit + PEERS]
+            for c in range(COMPS)
+            for bit in range(2)
+        ]
+        + [jnp.zeros((96, 128), F32)],
+        axis=0,
+    )
     for k in range(3):
         out_ref[pl.ds(k, PEERS, stride=3), :] = jnp.transpose(total[128 * k : 128 * k + 128])
 
@@ -463,7 +496,7 @@
         wides = []
         for pair in range(4 * step, 4 * step + 4):
             mask = high_iota == pair_row(high_ref, 0, pair)
-            both = [split(pair_row(rows_scr, 32 * comp, pair), 2) for comp in comps]
+            both = [split(returned_row(rows_scr, 32 * comp, pair), 2) for comp in comps]
             wides.append(
                 jnp.concatenate(
                     [jnp.where(mask, b[part], 0.0) for part in range(2) for b in both], axis=0
@@ -583,7 +616,7 @@
         out_specs=VMEM,
         scratch_shapes=[
             pltpu.VMEM((384, 128), F32),
-            pltpu.VMEM((256, 128), F32),
+            pltpu.VMEM((48, 128), F32),
             pltpu.VMEM((256, 128), F32),
             pltpu.VMEM((72, 128), F32),
         ],

time: 71.1 us -> 70.4 us (level)
  no operation moved by 1% of the time
where the time goes in v4:
time: 70.4 us; the launch traced here: 70.1 us
  blocking collectives  49.8 us (71%)
  Pallas kernels  11 us (16%)
  starting transfers between devices  4.42 us (6%)
  waiting for transfers between devices  4.18 us (6%)
  between operations  0.71 us (1%)
    all_to_all x2, blocking collectives, exchange(): got = lax.all_to_all(sent, axis, split_axis=0, concat_axis=0, tiled=True)  49.8 us
    all_to_all x1, starting transfers between devices, exchange(): got = lax.all_to_all(sent, axis, split_axis=0, concat_axis=0, tiled=True)  4.42 us
    all_to_all x1, waiting for transfers between devices, exchange(): got = lax.all_to_all(sent, axis, split_axis=0, concat_axis=0, tiled=True)  4.18 us
    pallas_call x1, Pallas kernels, owner(): pl.pallas_call(owner_kernel, out_shape=(shape(384, 128), jax.ShapeDtypeSt...  4.01 us
    pallas_call x1, Pallas kernels, render(): pl.pallas_call(render_kernel, out_shape=shape(384, 128), in_specs=[VMEM]...  2.41 us
    pallas_call x1, Pallas kernels, sum_rows(): pl.pallas_call(row_sum_kernel, out_shape=shape(384, 128), in_specs=[VMEM]...  1.71 us
    pallas_call x1, Pallas kernels, sum_colours(): pl.pallas_call(colour_sum_kernel, out_shape=shape(4 * PACK, 128), in_spec...  1.53 us
  transfers between devices with their start and end apart: 1, of which 1 were waited for; matrix products, arithmetic and copies ran while one was open for 0% of the time, Pallas kernels for 2%

profile of v4, /device:TPU:8, one launch (start us, length us, event | category | flops | bytes accessed | tf_op | source)
XLA Modules:
  0.0 70.1 jit_solution(14335366829356713256)
XLA Ops:
  0.6 0.0 copy-start.3
  0.6 0.0 copy-start.1
  0.7 0.0 copy-start.5
  0.7 0.0 copy-start.2
  0.7 0.0 copy-start.4
  0.7 4.0 %owner_rows.1 = (f32[384,128]{1,0:T(8,128)S(1)}, s32[32,128]{1,0:T(8,128)S(1)}, bf16[256,4096]{1,0:T(8,128)(2,1)S(1)}) custom-call(f32[1,3]{1,0:T(1,128)} %cam_ref.1, f32[384,128]{1,0:T(8,128)} %bitcast.22, f32[48,8192]{1,0:T(8,128)} %sh_hbm.1, f32[3,8192]{1,0:T(4,128)} %pos_ref.1, s32[32,128]{1,0:T(8,128)} %bitcast.23, s32[1,128]{1,0:T(1,128)} %cnt_hbm.1), custom_call_target="tpu_custom_call" | custom-call | tf_op jit(solution)/shard_map/owner_rows/pallas_call | solution.py:585
  4.7 30.5 %all_to_all.15 = f32[128,1,384]{2,1,0:T(1,128)S(1)} all-to-all(f32[128,1,384]{2,1,0:T(1,128)S(1)} %bitcast.18), channel_id=1, replica_groups=mesh['cell'=128,'img'=4] {'cell'}, dimensions={0} | all-to-all | bytes 393216 | tf_op jit(solution)/shard_map/all_to_all | solution.py:668
  35.2 0.0 copy-done.1
  35.2 0.0 copy-done.5
  35.3 0.0 copy-done.2
  35.3 0.0 copy-done.4
  35.3 2.4 %render_tiles.1 = f32[384,128]{1,0:T(8,128)S(1)} custom-call(s32[2,4]{1,0:T(2,128)S(1)} %bitcast.21, s32[1,4]{1,0:T(1,128)S(1)} %copy-done.5, f32[384,128]{1,0:T(8,128)S(1)} %bitcast.13, s32[4,256]{1,0:T(4,128)S(1)} %bitcast.20, f32[24,128]{1,0:T(8,128)S(1)} %bitcast.19), custom_call_target="tpu_custom_call" | custom-call | tf_op jit(solution)/shard_map/render_tiles/pallas_call | solution.py:612
  37.7 19.3 %all_to_all.16 = f32[128,1,384]{2,1,0:T(1,128)S(1)} all-to-all(f32[128,1,384]{2,1,0:T(1,128)S(1)} %bitcast.14), channel_id=1, replica_groups=mesh['cell'=128,'img'=4] {'cell'}, dimensions={0} | all-to-all | bytes 393216 | tf_op jit(solution)/shard_map/all_to_all | solution.py:668
  56.9 0.0 copy-done.3
  56.9 1.5 %colour_sums.1 = f32[224,128]{1,0:T(8,128)} custom-call(f32[1,3]{1,0:T(1,128)S(1)} %copy-done.3, f32[384,128]{1,0:T(8,128)S(1)} %bitcast.15, s32[32,128]{1,0:T(8,128)S(1)} %get-tuple-element.6.high_ref, bf16[256,4096]{1,0:T(8,128)(2,1)S(1)} %get-tuple-element.7.hot_ref), custom_call_target="tpu_custom_call" | custom-call | tf_op jit(solution)/shard_map/colour_sums/pallas_call | solution.py:629
  58.5 0.0 copy-start
  58.5 4.4 %all-to-all-start.2 = ((f32[4,1,7168]{2,1,0:T(1,128)}), f32[4,1,7168]{2,1,0:T(1,128)S(1)}, u32[]{:S(2)}, u32[]{:S(2)}) async-start(f32[4,1,7168]{2,1,0:T(1,128)} %bitcast.11), calls=%async_computation.2 | async-start | bytes 229376 | tf_op jit(solution)/shard_map/all_to_all | solution.py:668
  62.9 1.7 %row_sums.1 = f32[384,128]{1,0:T(8,128)} custom-call(f32[384,128]{1,0:T(8,128)S(1)} %bitcast.16, s32[32,128]{1,0:T(8,128)S(1)} %get-tuple-element.6.high_ref, bf16[256,4096]{1,0:T(8,128)(2,1)S(1)} %get-tuple-element.7.hot_ref), custom_call_target="tpu_custom_call" | custom-call | flops 805306368 | bytes 400000 | tf_op jit(solution)/shard_map/row_sums/pallas_call | solution.py:641
  64.6 4.2 %all-to-all-done.2 = f32[4,1,7168]{2,1,0:T(1,128)S(1)} async-done(((f32[4,1,7168]{2,1,0:T(1,128)}), f32[4,1,7168]{2,1,0:T(1,128)S(1)}, u32[]{:S(2)}, u32[]{:S(2)}) %all-to-all-start.2) | async-done | bytes 114720 | tf_op jit(solution)/shard_map/all_to_all | solution.py:668
  68.8 0.0 copy-done
  68.8 1.3 %coeff_grads.1 = f32[48,2048]{1,0:T(8,128)} custom-call(s32[1]{0:T(128)} %bitcast.10.share_ref, f32[224,128]{1,0:T(8,128)S(1)} %bitcast.17, f32[3,8192]{1,0:T(4,128)S(1)} %copy-done), custom_call_target="tpu_custom_call" | custom-call | tf_op jit(solution)/shard_map/coeff_grads/pallas_call | solution.py:656
Async XLA Ops:
  0.6 56.3 %copy-start.3 = (f32[1,3]{1,0:T(1,128)S(1)}, f32[1,3]{1,0:T(1,128)}, u32[]{:S(2)}) copy-start(f32[1,3]{1,0:T(1,128)} %cam_ref.1) | copy-start | bytes 40
  0.6 34.6 %copy-start.1 = (f32[1,3,1024]{2,0,1:T(1,128)S(1)}, f32[1,3,1024]{2,0,1:T(1,128)}, u32[]{:S(2)}) copy-start(f32[1,3,1024]{2,0,1:T(1,128)} %param.19) | copy-start | bytes 36868
  0.7 34.6 %copy-start.5 = (s32[1,4]{1,0:T(1,128)S(1)}, s32[1,4]{1,0:T(1,128)}, u32[]{:S(2)}) copy-start(s32[1,4]{1,0:T(1,128)} %len_ref.1) | copy-start | bytes 52
  0.7 34.6 %copy-start.2 = (s32[1,4,256]{2,1,0:T(4,128)S(1)}, s32[1,4,256]{2,1,0:T(4,128)}, u32[]{:S(2)}) copy-start(s32[1,4,256]{2,1,0:T(4,128)} %param.17) | copy-start | bytes 12292
  0.7 34.6 %copy-start.4 = (s32[1,2,4]{2,1,0:T(2,128)S(1)}, s32[1,2,4]{2,1,0:T(2,128)}, u32[]{:S(2)}) copy-start(s32[1,2,4]{2,1,0:T(2,128)} %param.16) | copy-start | bytes 100
  58.5 10.3 %copy-start = (f32[3,8192]{1,0:T(4,128)S(1)}, f32[3,8192]{1,0:T(4,128)}, u32[]{:S(2)}) copy-start(f32[3,8192]{1,0:T(4,128)} %pos_ref.1) | copy-start | bytes 294916
  58.5 10.3 %all-to-all-start.2 = ((f32[4,1,7168]{2,1,0:T(1,128)}), f32[4,1,7168]{2,1,0:T(1,128)S(1)}, u32[]{:S(2)}, u32[]{:S(2)}) async-start(f32[4,1,7168]{2,1,0:T(1,128)} %bitcast.11), calls=%async_computation.2 | async-start | bytes 229376 | tf_op jit(solution)/shard_map/all_to_all | solution.py:668

commit v5 on v4

--- a/solution.py
+++ b/solution.py
@@ -205,7 +205,8 @@
                 (proj_hbm, proj_ref),
                 (cam_hbm, cam_ref),
                 (pos_hbm, pos_ref),
-                (sh_hbm, sh_ref),
+                (sh_hbm.at[:, pl.ds(0, 4096)], sh_ref.at[:, pl.ds(0, 4096)]),
+                (sh_hbm.at[:, pl.ds(4096, 4096)], sh_ref.at[:, pl.ds(4096, 4096)]),
             )
         )
     ]
@@ -264,11 +265,13 @@
         hot = hots(pair)
         pick(sum_rows(dot(rows, hot)), mask(pair), 0, 6, pair)
         if pair == ALONE - 1:
-            for copy in copies[3:]:
+            for copy in copies[3:6]:
                 copy.wait()
             cam = [jnp.broadcast_to(cam_ref[0:1, i : i + 1], (8, 128)) for i in range(3)]
         if pair >= ALONE:
             for _ in range(-(-64 // (EARLY - ALONE))):
+                if chunk == 32:
+                    copies[6].wait()
                 if chunk < 64:
                     shade(chunk)
                     chunk += 1
@@ -510,12 +513,13 @@
     return total[:size] + total[size:]
 
 
-def colour_sum_kernel(cam_ref, back_ref, high_ref, hot_ref, col_ref, rows_scr):
-    total = sum_slots((6, 7, 8), back_ref, high_ref, hot_ref, rows_scr)
+def sum_kernel(cam_ref, back_ref, high_ref, hot_ref, out_ref, col_ref, rows_scr):
+    total = sum_slots(range(COMPS), back_ref, high_ref, hot_ref, rows_scr)
     for par in range(2):
+        out_ref[pl.ds(par, 192, stride=2), :] = total[:192, 128 * par : 128 * par + 128]
         for share in range(4):
             for chan in range(3):
-                first = 32 * chan + 8 * share
+                first = 192 + 32 * chan + 8 * share
                 col_ref[pl.ds(PACK * share + 16 * chan + par, 8, stride=2), :] = total[
                     first : first + 8, 128 * par : 128 * par + 128
                 ]
@@ -524,24 +528,22 @@
     for i in range(3):
         row = jnp.where(lanes == i, jnp.broadcast_to(cam_ref[0:1, i : i + 1], (8, 128)), row)
     for share in range(4):
-        col_ref[PACK * share + 48 : PACK * share + 56, :] = row
-
-
-def row_sum_kernel(back_ref, high_ref, hot_ref, out_ref, rows_scr):
-    total = sum_slots(range(6), back_ref, high_ref, hot_ref, rows_scr)
-    for par in range(2):
-        out_ref[pl.ds(par, 192, stride=2), :] = total[:, 128 * par : 128 * par + 128]
-
-
-def coeff_kernel(share_ref, col_ref, pos_ref, out_ref):
+        col_ref[PACK * share + 48 : PACK * share + 56, :] = jnp.where(
+            lanes == 3, float(share), row
+        )
+
+
+def coeff_kernel(col_ref, pos_ref, rows_ref, out_hbm, rows_hbm, out_scr, sems):
+    keep = pltpu.make_async_copy(rows_ref, rows_hbm, sems.at[2])
+    keep.start()
     consts = basis_consts()
-    share = share_ref[0]
+    share = jnp.max(col_ref[48:49, 3:4]).astype(jnp.int32)
     cams = []
     for image in range(4):
         row = col_ref[PACK * image + 48 : PACK * image + 56, :]
         cams.append([jnp.broadcast_to(row[:, i : i + 1], (8, 128)) for i in range(3)])
 
-    def chunk(step, carry):
+    def chunk(step):
         lanes = pl.ds(pl.multiple_of(share * 2048 + step * 128, 128), 128)
         place = [jnp.broadcast_to(pos_ref[i : i + 1, lanes], (8, 128)) for i in range(3)]
         totals = [[None, None] for _ in range(3)]
@@ -551,24 +553,32 @@
                 consts, place[0] - cam[0], place[1] - cam[1], place[2] - cam[2]
             )
             for chan in range(3):
-                grad = jnp.broadcast_to(
-                    col_ref[pl.ds(PACK * image + 16 * chan + step, 1), :], (8, 128)
-                )
+                at = PACK * image + 16 * chan + step
+                grad = jnp.broadcast_to(col_ref[at : at + 1, :], (8, 128))
                 for half in range(2):
                     term = grad * halves[half]
                     old = totals[chan][half]
                     totals[chan][half] = term if old is None else old + term
-        here = pl.ds(pl.multiple_of(step * 128, 128), 128)
         for chan in range(3):
             for half in range(2):
-                out_ref[16 * chan + 8 * half : 16 * chan + 8 * half + 8, here] = totals[chan][half]
-        return carry
-
-    lax.fori_loop(0, 16, chunk, 0, unroll=16)
+                at = 16 * chan + 8 * half
+                out_scr[at : at + 8, 128 * step : 128 * step + 128] = totals[chan][half]
+
+    copies = []
+    for half in range(2):
+        for step in range(8 * half, 8 * half + 8):
+            chunk(step)
+        lanes = pl.ds(1024 * half, 1024)
+        copies.append(
+            pltpu.make_async_copy(out_scr.at[:, lanes], out_hbm.at[:, lanes], sems.at[half])
+        )
+        copies[-1].start()
+    keep.wait()
+    for copy in copies:
+        copy.wait()
 
 
 VMEM = pl.BlockSpec(memory_space=pltpu.VMEM)
-SMEM = pl.BlockSpec(memory_space=pltpu.SMEM)
 HBM = pl.BlockSpec(memory_space=pltpu.HBM)
 PARAMS = pltpu.CompilerParams(vmem_limit_bytes=40 * 1024 * 1024)
 
@@ -601,7 +611,7 @@
             pltpu.VMEM((192, 128), F32),
             pltpu.VMEM((CAP, PEERS), jnp.int32),
             pltpu.VMEM((384, 128), F32),
-            pltpu.SemaphoreType.DMA((6,)),
+            pltpu.SemaphoreType.DMA((7,)),
         ],
         compiler_params=PARAMS,
         name="owner_rows",
@@ -625,42 +635,28 @@
     )(tile_xy, tile_len, received, tile_list, pixel_grad)
 
 
-def sum_colours(camera, returned, high, low_hot):
+def sum_returned(camera, returned, high, low_hot):
     return pl.pallas_call(
-        colour_sum_kernel,
-        out_shape=shape(4 * PACK, 128),
+        sum_kernel,
+        out_shape=(shape(384, 128), shape(4 * PACK, 128)),
         in_specs=[VMEM] * 4,
-        out_specs=VMEM,
+        out_specs=[VMEM] * 2,
         scratch_shapes=[pltpu.VMEM((384, 128), F32)],
         compiler_params=PARAMS,
-        name="colour_sums",
+        name="owner_sums",
     )(camera, returned, high, low_hot)
 
 
-def sum_rows(returned, high, low_hot):
-    return pl.pallas_call(
-        row_sum_kernel,
-        out_shape=shape(384, 128),
-        in_specs=[VMEM] * 3,
-        out_specs=VMEM,
-        scratch_shapes=[pltpu.VMEM((384, 128), F32)],
-        compiler_params=PARAMS,
-        cost_estimate=pl.CostEstimate(
-            flops=2 * 384 * 256 * 4096, bytes_accessed=400_000, transcendentals=0
-        ),
-        name="row_sums",
-    )(returned, high, low_hot)
-
-
-def coefficients(share, colours, positions):
+def coefficients(colours, positions, rows):
     return pl.pallas_call(
         coeff_kernel,
-        out_shape=shape(48, 2048),
-        in_specs=[SMEM] + [VMEM] * 2,
-        out_specs=VMEM,
+        out_shape=(shape(48, 2048), shape(384, 128)),
+        in_specs=[VMEM] * 3,
+        out_specs=[HBM] * 2,
+        scratch_shapes=[pltpu.VMEM((48, 2048), F32), pltpu.SemaphoreType.DMA((3,))],
         compiler_params=PARAMS,
         name="coeff_grads",
-    )(share, colours, positions)
+    )(colours, positions, rows)
 
 
 def exchange(rows, axis, peers):
@@ -690,10 +686,9 @@
         tile_xy[0], tile_len, received, tile_list[0], pixel_grad.reshape(24, 128)
     )
     returned = exchange(slot_grads, "cell", PEERS)
-    colours = exchange(sum_colours(camera, returned, high, low_hot), "img", 4)
-    grad_rows = sum_rows(returned, high, low_hot)
-    share = lax.axis_index("img").astype(jnp.int32).reshape(1)
-    grad_sh = coefficients(share, colours, positions)
+    grad_rows, colours = sum_returned(camera, returned, high, low_hot)
+    colours = exchange(colours, "img", 4)
+    grad_sh, grad_rows = coefficients(colours, positions, grad_rows)
     return (grad_rows.reshape(proj.shape), grad_sh)
 
 

time: 70.4 us -> 69.9 us (level)
  blocking collectives: 49.8 us -> 59.9 us
  starting transfers between devices: 4.42 us -> 0 us
  waiting for transfers between devices: 4.18 us -> 0 us
  Pallas kernels: 11 us -> 9.04 us
    all_to_all x2 -> x3, blocking collectives: 49.8 us -> 59.9 us  [exchange(): got = lax.all_to_all(sent, axis, split_axis=0, concat_axis=0, tiled=True)]
    all_to_all x1 -> x0, starting transfers between devices: 4.42 us -> none  [exchange(): got = lax.all_to_all(sent, axis, split_axis=0, concat_axis=0, tiled=True)]
    all_to_all x1 -> x0, waiting for transfers between devices: 4.18 us -> none  [exchange(): got = lax.all_to_all(sent, axis, split_axis=0, concat_axis=0, tiled=True)]
    pallas_call x3 -> x2, Pallas kernels: 4.55 us -> 2.78 us  [the longest x1 1.46 us: sum_returned(): pl.pallas_call(sum_kernel, out_shape=(shape(384, 128), shape(4 * PACK, 12...]
  transfers between devices with their start and end apart: 1 -> 0, of which waited for: 1 -> 0; matrix products, arithmetic and copies ran while one was open for 0% -> 0% of each run, Pallas kernels for 2% -> 0%
where the time goes in v5:
time: 69.9 us; the launch traced here: 69.7 us
  blocking collectives  59.9 us (86%)
  Pallas kernels  9.04 us (13%)
  between operations  0.72 us (1%)
    all_to_all x3, blocking collectives, exchange(): got = lax.all_to_all(sent, axis, split_axis=0, concat_axis=0, tiled=True)  59.9 us
    pallas_call x1, Pallas kernels, owner(): pl.pallas_call(owner_kernel, out_shape=(shape(384, 128), jax.ShapeDtypeSt...  3.86 us
    pallas_call x1, Pallas kernels, render(): pl.pallas_call(render_kernel, out_shape=shape(384, 128), in_specs=[VMEM]...  2.41 us
    pallas_call x1, Pallas kernels, sum_returned(): pl.pallas_call(sum_kernel, out_shape=(shape(384, 128), shape(4 * PACK, 12...  1.46 us

profile of v5, /device:TPU:8, one launch (start us, length us, event | category | flops | bytes accessed | tf_op | source)
XLA Modules:
  0.0 69.7 jit_solution(10123747698217292900)
XLA Ops:
  0.6 0.0 copy-start.3
  0.6 0.0 copy-start.1
  0.7 0.0 copy-start.5
  0.7 0.0 copy-start.2
  0.7 0.0 copy-start.4
  0.7 3.9 %owner_rows.1 = (f32[384,128]{1,0:T(8,128)S(1)}, s32[32,128]{1,0:T(8,128)S(1)}, bf16[256,4096]{1,0:T(8,128)(2,1)S(1)}) custom-call(f32[1,3]{1,0:T(1,128)} %cam_ref.1, f32[384,128]{1,0:T(8,128)} %bitcast.21, f32[48,8192]{1,0:T(8,128)} %sh_hbm.1, f32[3,8192]{1,0:T(4,128)} %pos_ref.1, s32[32,128]{1,0:T(8,128)} %bitcast.22, s32[1,128]{1,0:T(1,128)} %cnt_hbm.1), custom_call_target="tpu_custom_call" | custom-call | tf_op jit(solution)/shard_map/owner_rows/pallas_call | solution.py:595
  4.5 0.0 copy-start
  4.6 30.7 %all_to_all.15 = f32[128,1,384]{2,1,0:T(1,128)S(1)} all-to-all(f32[128,1,384]{2,1,0:T(1,128)S(1)} %bitcast.16), channel_id=1, replica_groups=mesh['cell'=128,'img'=4] {'cell'}, dimensions={0} | all-to-all | bytes 393216 | tf_op jit(solution)/shard_map/all_to_all | solution.py:664
  35.2 0.0 copy-done.1
  35.2 0.0 copy-done.5
  35.2 0.0 copy-done.2
  35.2 0.0 copy-done.4
  35.3 2.4 %render_tiles.1 = f32[384,128]{1,0:T(8,128)S(1)} custom-call(s32[2,4]{1,0:T(2,128)S(1)} %bitcast.20, s32[1,4]{1,0:T(1,128)S(1)} %copy-done.5, f32[384,128]{1,0:T(8,128)S(1)} %bitcast.13, s32[4,256]{1,0:T(4,128)S(1)} %bitcast.19, f32[24,128]{1,0:T(8,128)S(1)} %bitcast.18), custom_call_target="tpu_custom_call" | custom-call | tf_op jit(solution)/shard_map/render_tiles/pallas_call | solution.py:622
  37.7 19.3 %all_to_all.16 = f32[128,1,384]{2,1,0:T(1,128)S(1)} all-to-all(f32[128,1,384]{2,1,0:T(1,128)S(1)} %bitcast.14), channel_id=1, replica_groups=mesh['cell'=128,'img'=4] {'cell'}, dimensions={0} | all-to-all | bytes 393216 | tf_op jit(solution)/shard_map/all_to_all | solution.py:664
  56.9 0.0 copy-done.3
  56.9 1.5 %owner_sums.1 = (f32[384,128]{1,0:T(8,128)S(1)}, f32[224,128]{1,0:T(8,128)S(1)}) custom-call(f32[1,3]{1,0:T(1,128)S(1)} %copy-done.3, f32[384,128]{1,0:T(8,128)S(1)} %bitcast.12, s32[32,128]{1,0:T(8,128)S(1)} %get-tuple-element.10.high_ref, bf16[256,4096]{1,0:T(8,128)(2,1)S(1)} %get-tuple-element.11.hot_ref), custom_call_target="tpu_custom_call" | custom-call | tf_op jit(solution)/shard_map/owner_sums/pallas_call | solution.py:639
  58.4 10.0 %all_to_all.17 = f32[4,1,7168]{2,1,0:T(1,128)S(1)} all-to-all(f32[4,1,7168]{2,1,0:T(1,128)S(1)} %bitcast.17), channel_id=1, replica_groups=mesh['cell'=128,'img'=4] {'img'}, dimensions={0} | all-to-all | bytes 229376 | tf_op jit(solution)/shard_map/all_to_all | solution.py:664
  68.4 0.0 copy-done
  68.4 1.3 %coeff_grads.1 = (f32[48,2048]{1,0:T(8,128)}, f32[384,128]{1,0:T(8,128)}) custom-call(f32[224,128]{1,0:T(8,128)S(1)} %bitcast.15, f32[3,8192]{1,0:T(4,128)S(1)} %copy-done, f32[384,128]{1,0:T(8,128)S(1)} %get-tuple-element.13.rows_ref), custom_call_target="tpu_custom_call" | custom-call | tf_op jit(solution)/shard_map/coeff_grads/pallas_call | solution.py:651
Async XLA Ops:
  0.6 56.3 %copy-start.3 = (f32[1,3]{1,0:T(1,128)S(1)}, f32[1,3]{1,0:T(1,128)}, u32[]{:S(2)}) copy-start(f32[1,3]{1,0:T(1,128)} %cam_ref.1) | copy-start | bytes 40
  0.6 34.6 %copy-start.1 = (f32[1,3,1024]{2,0,1:T(1,128)S(1)}, f32[1,3,1024]{2,0,1:T(1,128)}, u32[]{:S(2)}) copy-start(f32[1,3,1024]{2,0,1:T(1,128)} %param.19) | copy-start | bytes 36868
  0.7 34.6 %copy-start.5 = (s32[1,4]{1,0:T(1,128)S(1)}, s32[1,4]{1,0:T(1,128)}, u32[]{:S(2)}) copy-start(s32[1,4]{1,0:T(1,128)} %len_ref.1) | copy-start | bytes 52
  0.7 34.6 %copy-start.2 = (s32[1,4,256]{2,1,0:T(4,128)S(1)}, s32[1,4,256]{2,1,0:T(4,128)}, u32[]{:S(2)}) copy-start(s32[1,4,256]{2,1,0:T(4,128)} %param.17) | copy-start | bytes 12292
  0.7 34.6 %copy-start.4 = (s32[1,2,4]{2,1,0:T(2,128)S(1)}, s32[1,2,4]{2,1,0:T(2,128)}, u32[]{:S(2)}) copy-start(s32[1,2,4]{2,1,0:T(2,128)} %param.16) | copy-start | bytes 100
  4.5 63.8 %copy-start = (f32[3,8192]{1,0:T(4,128)S(1)}, f32[3,8192]{1,0:T(4,128)}, u32[]{:S(2)}) copy-start(f32[3,8192]{1,0:T(4,128)} %pos_ref.1) | copy-start | bytes 294916

commit v6 on v5

--- a/solution.py
+++ b/solution.py
@@ -39,6 +39,7 @@
 NOTHING = -1.0e4
 LOG2E = 1.4426950408889634
 EARLY = 6
+LANED = 2
 ALONE = 3
 
 LINEAR = (
@@ -151,6 +152,26 @@
     ]
 
 
+def column_sums(blocks):
+    rows = iota((8, 128), 0)
+    low = rows < 4
+    blocks = [
+        jnp.where(low, blocks[i], blocks[i + 4])
+        + pltpu.roll(jnp.where(low, blocks[i + 4], blocks[i]), 4, 0)
+        for i in range(4)
+    ]
+    for step in (2, 1):
+        low = (rows & step) == 0
+        blocks = [
+            jnp.where(low, blocks[i], blocks[i + step])
+            + jnp.where(
+                low, pltpu.roll(blocks[i], 8 - step, 0), pltpu.roll(blocks[i + step], step, 0)
+            )
+            for i in range(step)
+        ]
+    return blocks[0]
+
+
 def slot_index(idx_ref, cnt_ref, low_scr, high_scr):
     turned = jnp.transpose(idx_ref[...].astype(F32)).astype(jnp.int32)
     slots = jnp.concatenate([turned[32 * i : 32 * i + 32] for i in range(4)], axis=1)
@@ -224,14 +245,20 @@
             [ref[pl.ds(par, 32 * comps, stride=2), :] for par in range(2)], axis=1
         )
 
+    partial = {}
+
     def pick(wide, mask, base, comps, pair):
-        for comp in range(comps):
-            row = jnp.sum(
-                jnp.where(mask, wide[32 * comp : 32 * comp + 32], 0.0), axis=0, keepdims=True
-            )
-            at = 32 * (base + comp) + 2 * pair
-            rows_scr[at : at + 1, :] = row[:, :128]
-            rows_scr[at + 1 : at + 2, :] = row[:, 128:]
+        for comp in range(base, base + comps):
+            at = 32 * (comp - base)
+            kept = jnp.where(mask, wide[at : at + 32], 0.0)
+            kept = (kept[0:8] + kept[8:16]) + (kept[16:24] + kept[24:32])
+            for h in range(2):
+                partial[comp, 2 * pair + h] = kept[:, 128 * h : 128 * h + 128]
+            first = 8 * (pair // 4)
+            if all((comp, first + i) in partial for i in range(8)):
+                rows_scr[32 * comp + first : 32 * comp + first + 8, :] = column_sums(
+                    [partial.pop((comp, first + i)) for i in range(8)]
+                )
 
     def shade(chunk):
         lanes = slice(128 * chunk, 128 * chunk + 128)
@@ -239,10 +266,14 @@
         first, second = basis_halves(consts, *offs)
         for chan in range(3):
             terms = sh_ref[16 * chan : 16 * chan + 8, lanes] * first
-            terms = terms + sh_ref[16 * chan + 8 : 16 * chan + 16, lanes] * second
-            colour = jnp.sum(terms, axis=0, keepdims=True) + 0.5
-            at = 64 * chan + chunk
-            col_scr[at : at + 1, :] = colour
+            partial["shade", chan, chunk] = (
+                terms + sh_ref[16 * chan + 8 : 16 * chan + 16, lanes] * second
+            )
+            if chunk % 8 == 7:
+                at = 64 * chan + chunk - 7
+                col_scr[at : at + 8, :] = 0.5 + column_sums(
+                    [partial.pop(("shade", chan, chunk - 7 + i)) for i in range(8)]
+                )
 
     def hots(pair):
         hot = one_hot(low_iota, pair_row(low_scr, 0, pair))
@@ -253,17 +284,37 @@
         return high_iota == pair_row(high_scr, 0, pair)
 
     copies[2].wait()
-    rows = split(table(proj_ref, 6), 3)
-    rows = jnp.concatenate([rows[0], rows[1], rows[2][:160]], axis=0).astype(BF16)
+    rows = split(table(proj_ref, 6)[32 * LANED :], 3)
+    size = 192 - 32 * LANED
+    exact = size - 32
+    rows = jnp.concatenate([rows[0], rows[1], rows[2][:exact]], axis=0).astype(BF16)
+    both = 2 * size + exact
 
     def sum_rows(wide):
-        exact = wide[:160] + wide[192:352] + wide[384:544]
-        return jnp.concatenate([exact, wide[160:192] + wide[352:384]], axis=0)
+        first = wide[:exact] + wide[size : size + exact] + wide[2 * size : both]
+        return jnp.concatenate([first, wide[exact:size] + wide[size + exact : 2 * size]], axis=0)
+
+    lanes_of = [(high_scr[8 * b : 8 * b + 8, :] << 1) | (low_scr[8 * b : 8 * b + 8, :] >> 7) for b in range(4)]
+    dead = [high_scr[8 * b : 8 * b + 8, :] < 0 for b in range(4)]
+    lanes_of = [jnp.where(d, -1, v) for d, v in zip(dead, lanes_of)]
+    within = [low_scr[8 * b : 8 * b + 8, :] & 127 for b in range(4)]
+    found = [[jnp.zeros((8, 128), F32) for _ in range(4)] for _ in range(LANED)]
+
+    def lane_gather(block):
+        mine = [v == block for v in lanes_of]
+        for comp in range(LANED):
+            at = 64 * comp + block
+            row = jnp.broadcast_to(proj_ref[at : at + 1, :], (8, 128))
+            for b in range(4):
+                value = jnp.take_along_axis(row, within[b], axis=1)
+                found[comp][b] = jnp.where(mine[b], value, found[comp][b])
 
     cam, chunk = None, 0
     for pair in range(EARLY):
         hot = hots(pair)
-        pick(sum_rows(dot(rows, hot)), mask(pair), 0, 6, pair)
+        pick(sum_rows(dot(rows, hot)), mask(pair), LANED, 6 - LANED, pair)
+        for block in range(4 * pair, 4 * pair + 4):
+            lane_gather(block)
         if pair == ALONE - 1:
             for copy in copies[3:6]:
                 copy.wait()
@@ -279,12 +330,17 @@
     everything = jnp.concatenate([rows, tints], axis=0)
     for pair in range(EARLY, CAP // 2):
         wide = dot(everything, hots(pair))
-        pick(sum_rows(wide), mask(pair), 0, 6, pair)
-        pick(wide[544:640] + wide[640:736], mask(pair), 6, 3, pair)
+        pick(sum_rows(wide), mask(pair), LANED, 6 - LANED, pair)
+        pick(wide[both : both + 96] + wide[both + 96 :], mask(pair), 6, 3, pair)
+        for block in range(4 * pair, 4 * pair + 4):
+            lane_gather(block)
     for pair in range(EARLY):
         wide = dot(tints, hot_ref[:, 256 * pair : 256 * pair + 256])
         pick(wide[:96] + wide[96:], mask(pair), 6, 3, pair)
 
+    for comp in range(LANED):
+        for b in range(4):
+            rows_scr[32 * comp + 8 * b : 32 * comp + 8 * b + 8, :] = found[comp][b]
     rows_scr[32 * COMPS :, :] = jnp.zeros((96, 128), F32)
     for k in range(3):
         turned = jnp.transpose(rows_scr[128 * k : 128 * k + 128, :])

time: 69.9 us -> 69.5 us (level)
  no operation moved by 1% of the time
where the time goes in v6:
time: 69.5 us; the launch traced here: 69.2 us
  blocking collectives  59.9 us (86%)
  Pallas kernels  8.55 us (12%)
  between operations  0.72 us (1%)
    all_to_all x3, blocking collectives, exchange(): got = lax.all_to_all(sent, axis, split_axis=0, concat_axis=0, tiled=True)  59.9 us
    pallas_call x1, Pallas kernels, owner(): pl.pallas_call(owner_kernel, out_shape=(shape(384, 128), jax.ShapeDtypeSt...  3.37 us
    pallas_call x1, Pallas kernels, render(): pl.pallas_call(render_kernel, out_shape=shape(384, 128), in_specs=[VMEM]...  2.41 us
    pallas_call x1, Pallas kernels, sum_returned(): pl.pallas_call(sum_kernel, out_shape=(shape(384, 128), shape(4 * PACK, 12...  1.46 us

profile of v6, /device:TPU:8, one launch (start us, length us, event | category | flops | bytes accessed | tf_op | source)
XLA Modules:
  0.0 69.2 jit_solution(9976381989540504219)
XLA Ops:
  0.6 0.0 copy-start.3
  0.6 0.0 copy-start.1
  0.7 0.0 copy-start.5
  0.7 0.0 copy-start.2
  0.7 0.0 copy-start.4
  0.7 3.4 %owner_rows.1 = (f32[384,128]{1,0:T(8,128)S(1)}, s32[32,128]{1,0:T(8,128)S(1)}, bf16[256,4096]{1,0:T(8,128)(2,1)S(1)}) custom-call(f32[1,3]{1,0:T(1,128)} %cam_ref.1, f32[384,128]{1,0:T(8,128)} %bitcast.21, f32[48,8192]{1,0:T(8,128)} %sh_hbm.1, f32[3,8192]{1,0:T(4,128)} %pos_ref.1, s32[32,128]{1,0:T(8,128)} %bitcast.22, s32[1,128]{1,0:T(1,128)} %cnt_hbm.1), custom_call_target="tpu_custom_call" | custom-call | tf_op jit(solution)/shard_map/owner_rows/pallas_call | solution.py:651
  4.1 0.0 copy-start
  4.1 30.7 %all_to_all.15 = f32[128,1,384]{2,1,0:T(1,128)S(1)} all-to-all(f32[128,1,384]{2,1,0:T(1,128)S(1)} %bitcast.16), channel_id=1, replica_groups=mesh['cell'=128,'img'=4] {'cell'}, dimensions={0} | all-to-all | bytes 393216 | tf_op jit(solution)/shard_map/all_to_all | solution.py:720
  34.7 0.0 copy-done.1
  34.7 0.0 copy-done.5
  34.7 0.0 copy-done.2
  34.8 0.0 copy-done.4
  34.8 2.4 %render_tiles.1 = f32[384,128]{1,0:T(8,128)S(1)} custom-call(s32[2,4]{1,0:T(2,128)S(1)} %bitcast.20, s32[1,4]{1,0:T(1,128)S(1)} %copy-done.5, f32[384,128]{1,0:T(8,128)S(1)} %bitcast.13, s32[4,256]{1,0:T(4,128)S(1)} %bitcast.19, f32[24,128]{1,0:T(8,128)S(1)} %bitcast.18), custom_call_target="tpu_custom_call" | custom-call | tf_op jit(solution)/shard_map/render_tiles/pallas_call | solution.py:678
  37.2 19.3 %all_to_all.16 = f32[128,1,384]{2,1,0:T(1,128)S(1)} all-to-all(f32[128,1,384]{2,1,0:T(1,128)S(1)} %bitcast.14), channel_id=1, replica_groups=mesh['cell'=128,'img'=4] {'cell'}, dimensions={0} | all-to-all | bytes 393216 | tf_op jit(solution)/shard_map/all_to_all | solution.py:720
  56.4 0.0 copy-done.3
  56.4 1.5 %owner_sums.1 = (f32[384,128]{1,0:T(8,128)S(1)}, f32[224,128]{1,0:T(8,128)S(1)}) custom-call(f32[1,3]{1,0:T(1,128)S(1)} %copy-done.3, f32[384,128]{1,0:T(8,128)S(1)} %bitcast.12, s32[32,128]{1,0:T(8,128)S(1)} %get-tuple-element.10.high_ref, bf16[256,4096]{1,0:T(8,128)(2,1)S(1)} %get-tuple-element.11.hot_ref), custom_call_target="tpu_custom_call" | custom-call | tf_op jit(solution)/shard_map/owner_sums/pallas_call | solution.py:695
  57.9 10.0 %all_to_all.17 = f32[4,1,7168]{2,1,0:T(1,128)S(1)} all-to-all(f32[4,1,7168]{2,1,0:T(1,128)S(1)} %bitcast.17), channel_id=1, replica_groups=mesh['cell'=128,'img'=4] {'img'}, dimensions={0} | all-to-all | bytes 229376 | tf_op jit(solution)/shard_map/all_to_all | solution.py:720
  67.9 0.0 copy-done
  67.9 1.3 %coeff_grads.1 = (f32[48,2048]{1,0:T(8,128)}, f32[384,128]{1,0:T(8,128)}) custom-call(f32[224,128]{1,0:T(8,128)S(1)} %bitcast.15, f32[3,8192]{1,0:T(4,128)S(1)} %copy-done, f32[384,128]{1,0:T(8,128)S(1)} %get-tuple-element.13.rows_ref), custom_call_target="tpu_custom_call" | custom-call | tf_op jit(solution)/shard_map/coeff_grads/pallas_call | solution.py:707
Async XLA Ops:
  0.6 55.8 %copy-start.3 = (f32[1,3]{1,0:T(1,128)S(1)}, f32[1,3]{1,0:T(1,128)}, u32[]{:S(2)}) copy-start(f32[1,3]{1,0:T(1,128)} %cam_ref.1) | copy-start | bytes 40
  0.6 34.1 %copy-start.1 = (f32[1,3,1024]{2,0,1:T(1,128)S(1)}, f32[1,3,1024]{2,0,1:T(1,128)}, u32[]{:S(2)}) copy-start(f32[1,3,1024]{2,0,1:T(1,128)} %param.19) | copy-start | bytes 36868
  0.7 34.1 %copy-start.5 = (s32[1,4]{1,0:T(1,128)S(1)}, s32[1,4]{1,0:T(1,128)}, u32[]{:S(2)}) copy-start(s32[1,4]{1,0:T(1,128)} %len_ref.1) | copy-start | bytes 52
  0.7 34.1 %copy-start.2 = (s32[1,4,256]{2,1,0:T(4,128)S(1)}, s32[1,4,256]{2,1,0:T(4,128)}, u32[]{:S(2)}) copy-start(s32[1,4,256]{2,1,0:T(4,128)} %param.17) | copy-start | bytes 12292
  0.7 34.1 %copy-start.4 = (s32[1,2,4]{2,1,0:T(2,128)S(1)}, s32[1,2,4]{2,1,0:T(2,128)}, u32[]{:S(2)}) copy-start(s32[1,2,4]{2,1,0:T(2,128)} %param.16) | copy-start | bytes 100
  4.1 63.8 %copy-start = (f32[3,8192]{1,0:T(4,128)S(1)}, f32[3,8192]{1,0:T(4,128)}, u32[]{:S(2)}) copy-start(f32[3,8192]{1,0:T(4,128)} %pos_ref.1) | copy-start | bytes 294916

commit v7 on v6

--- a/solution.py
+++ b/solution.py
@@ -142,14 +142,23 @@
     return [(column_consts(LINEAR, half), column_consts(QUADRATIC, half)) for half in range(2)]
 
 
-def basis_halves(consts, xoff, yoff, zoff):
-    inv = lax.rsqrt(xoff * xoff + yoff * yoff + zoff * zoff)
-    xpos, ypos, zpos = xoff * inv, yoff * inv, zoff * inv
-    xsq, ysq, zsq, yz = xpos * xpos, ypos * ypos, zpos * zpos, ypos * zpos
+def unit_terms(place, cam):
+    offs = [at - centre for at, centre in zip(place, cam)]
+    inv = lax.rsqrt(offs[0] * offs[0] + offs[1] * offs[1] + offs[2] * offs[2])
+    xpos, ypos, zpos = [off * inv for off in offs]
+    return xpos, ypos, zpos, xpos * xpos, ypos * ypos, zpos * zpos, ypos * zpos
+
+
+def basis_halves(consts, terms):
+    xpos, ypos, zpos, xsq, ysq, zsq, yz = terms
     return [
         form(lin, (None, xpos, ypos, zpos)) * form(quad, (None, ypos, zpos, xsq, ysq, zsq, yz))
         for lin, quad in consts
     ]
+
+
+def repeated(ref, row):
+    return jnp.broadcast_to(ref[row : row + 1, :], (8, 128))
 
 
 def column_sums(blocks):
@@ -262,8 +271,8 @@
 
     def shade(chunk):
         lanes = slice(128 * chunk, 128 * chunk + 128)
-        offs = [jnp.broadcast_to(pos_ref[i : i + 1, lanes], (8, 128)) - cam[i] for i in range(3)]
-        first, second = basis_halves(consts, *offs)
+        place = [jnp.broadcast_to(pos_ref[i : i + 1, lanes], (8, 128)) for i in range(3)]
+        first, second = basis_halves(consts, unit_terms(place, cam))
         for chan in range(3):
             terms = sh_ref[16 * chan : 16 * chan + 8, lanes] * first
             partial["shade", chan, chunk] = (
@@ -451,16 +460,16 @@
         alpha = jnp.exp2(exponents(tile))
         logs = jnp.log(1.0 - alpha)
         l0 = logs.astype(BF16)
-        return alpha, logs, l0, (logs - l0.astype(F32)).astype(BF16)
-
-    def middle(tile, alpha, logs, l0, l1):
+        return alpha, l0, (logs - l0.astype(F32)).astype(BF16)
+
+    def middle(tile, alpha, l0, l1):
         weight = alpha * jnp.exp(stacked(l0, l1, before))
         flow = dot(turned[:, 32 * tile : 32 * tile + 32], both(right_scr, tile)) * weight
         s0 = flow.astype(BF16)
         return weight, flow, s0, (flow - s0.astype(F32)).astype(BF16)
 
-    def back(tile, alpha, logs, weight, flow, s0, s1):
-        power = flow - stacked(s0, s1, after) * (alpha * jnp.exp(-logs))
+    def back(tile, alpha, weight, flow, s0, s1):
+        power = flow - stacked(s0, s1, after) * (alpha / (1.0 - alpha))
         w0 = weight.astype(BF16)
         w1 = (weight - w0.astype(F32)).astype(BF16)
         colours = dot(sides[tile], w0)
@@ -496,7 +505,7 @@
         fronts = [front(tile) for tile in group]
         middles = [middle(tile, *fronts[tile - first]) for tile in group]
         for tile in group:
-            back(tile, *fronts[tile - first][:2], *middles[tile - first])
+            back(tile, fronts[tile - first][0], *middles[tile - first])
 
     m0, mu, mv, muu, mvv, muv, red, green, blue = [sums_scr[8 * i : 8 * i + 8, :] for i in range(9)]
     grads = [
@@ -589,28 +598,31 @@
         )
 
 
-def coeff_kernel(col_ref, pos_ref, rows_ref, out_hbm, rows_hbm, out_scr, sems):
-    keep = pltpu.make_async_copy(rows_ref, rows_hbm, sems.at[2])
+def coeff_kernel(col_ref, pos_ref, rows_ref, out_hbm, rows_hbm, out_scr, unit_scr, sems):
+    keep = pltpu.make_async_copy(rows_ref, rows_hbm, sems.at[4])
     keep.start()
     consts = basis_consts()
     share = jnp.max(col_ref[48:49, 3:4]).astype(jnp.int32)
-    cams = []
+    for i in range(3):
+        for at in range(16):
+            lanes = pl.ds(pl.multiple_of(share * 2048 + at * 128, 128), 128)
+            unit_scr[16 * i + at : 16 * i + at + 1, :] = pos_ref[i : i + 1, lanes]
+    place = [unit_scr[16 * i : 16 * i + 16, :] for i in range(3)]
     for image in range(4):
-        row = col_ref[PACK * image + 48 : PACK * image + 56, :]
-        cams.append([jnp.broadcast_to(row[:, i : i + 1], (8, 128)) for i in range(3)])
+        row = col_ref[PACK * image + 48 : PACK * image + 49, :]
+        cam = [jnp.broadcast_to(row[:, i : i + 1], (16, 128)) for i in range(3)]
+        for i, term in enumerate(unit_terms(place, cam)):
+            at = 112 * image + 16 * i
+            unit_scr[at : at + 16, :] = term
 
     def chunk(step):
-        lanes = pl.ds(pl.multiple_of(share * 2048 + step * 128, 128), 128)
-        place = [jnp.broadcast_to(pos_ref[i : i + 1, lanes], (8, 128)) for i in range(3)]
         totals = [[None, None] for _ in range(3)]
         for image in range(4):
-            cam = cams[image]
             halves = basis_halves(
-                consts, place[0] - cam[0], place[1] - cam[1], place[2] - cam[2]
+                consts, [repeated(unit_scr, 112 * image + 16 * i + step) for i in range(7)]
             )
             for chan in range(3):
-                at = PACK * image + 16 * chan + step
-                grad = jnp.broadcast_to(col_ref[at : at + 1, :], (8, 128))
+                grad = repeated(col_ref, PACK * image + 16 * chan + step)
                 for half in range(2):
                     term = grad * halves[half]
                     old = totals[chan][half]
@@ -621,12 +633,12 @@
                 out_scr[at : at + 8, 128 * step : 128 * step + 128] = totals[chan][half]
 
     copies = []
-    for half in range(2):
-        for step in range(8 * half, 8 * half + 8):
+    for piece in range(4):
+        for step in range(4 * piece, 4 * piece + 4):
             chunk(step)
-        lanes = pl.ds(1024 * half, 1024)
+        lanes = pl.ds(512 * piece, 512)
         copies.append(
-            pltpu.make_async_copy(out_scr.at[:, lanes], out_hbm.at[:, lanes], sems.at[half])
+            pltpu.make_async_copy(out_scr.at[:, lanes], out_hbm.at[:, lanes], sems.at[piece])
         )
         copies[-1].start()
     keep.wait()
@@ -709,7 +721,11 @@
         out_shape=(shape(48, 2048), shape(384, 128)),
         in_specs=[VMEM] * 3,
         out_specs=[HBM] * 2,
-        scratch_shapes=[pltpu.VMEM((48, 2048), F32), pltpu.SemaphoreType.DMA((3,))],
+        scratch_shapes=[
+            pltpu.VMEM((48, 2048), F32),
+            pltpu.VMEM((448, 128), F32),
+            pltpu.SemaphoreType.DMA((5,)),
+        ],
         compiler_params=PARAMS,
         name="coeff_grads",
     )(colours, positions, rows)

time: 69.5 us -> 69.3 us (level)
  no operation moved by 1% of the time
where the time goes in v7:
time: 69.3 us; the launch traced here: 69 us
  blocking collectives  59.9 us (86%)
  Pallas kernels  8.35 us (12%)
  between operations  0.72 us (1%)
    all_to_all x3, blocking collectives, exchange(): got = lax.all_to_all(sent, axis, split_axis=0, concat_axis=0, tiled=True)  59.9 us
    pallas_call x1, Pallas kernels, owner(): pl.pallas_call(owner_kernel, out_shape=(shape(384, 128), jax.ShapeDtypeSt...  3.37 us
    pallas_call x1, Pallas kernels, render(): pl.pallas_call(render_kernel, out_shape=shape(384, 128), in_specs=[VMEM]...  2.32 us
    pallas_call x1, Pallas kernels, sum_returned(): pl.pallas_call(sum_kernel, out_shape=(shape(384, 128), shape(4 * PACK, 12...  1.46 us

profile of v7, /device:TPU:8, one launch (start us, length us, event | category | flops | bytes accessed | tf_op | source)
XLA Modules:
  0.0 69.0 jit_solution(4106877378475061383)
XLA Ops:
  0.6 0.0 copy-start.3
  0.6 0.0 copy-start.1
  0.7 0.0 copy-start.5
  0.7 0.0 copy-start.2
  0.7 0.0 copy-start.4
  0.7 3.4 %owner_rows.1 = (f32[384,128]{1,0:T(8,128)S(1)}, s32[32,128]{1,0:T(8,128)S(1)}, bf16[256,4096]{1,0:T(8,128)(2,1)S(1)}) custom-call(f32[1,3]{1,0:T(1,128)} %cam_ref.1, f32[384,128]{1,0:T(8,128)} %bitcast.21, f32[48,8192]{1,0:T(8,128)} %sh_hbm.1, f32[3,8192]{1,0:T(4,128)} %pos_ref.1, s32[32,128]{1,0:T(8,128)} %bitcast.22, s32[1,128]{1,0:T(1,128)} %cnt_hbm.1), custom_call_target="tpu_custom_call" | custom-call | tf_op jit(solution)/shard_map/owner_rows/pallas_call | solution.py:663
  4.1 0.0 copy-start
  4.1 30.7 %all_to_all.15 = f32[128,1,384]{2,1,0:T(1,128)S(1)} all-to-all(f32[128,1,384]{2,1,0:T(1,128)S(1)} %bitcast.16), channel_id=1, replica_groups=mesh['cell'=128,'img'=4] {'cell'}, dimensions={0} | all-to-all | bytes 393216 | tf_op jit(solution)/shard_map/all_to_all | solution.py:736
  34.7 0.0 copy-done.1
  34.7 0.0 copy-done.5
  34.7 0.0 copy-done.2
  34.8 0.0 copy-done.4
  34.8 2.3 %render_tiles.1 = f32[384,128]{1,0:T(8,128)S(1)} custom-call(s32[2,4]{1,0:T(2,128)S(1)} %bitcast.20, s32[1,4]{1,0:T(1,128)S(1)} %copy-done.5, f32[384,128]{1,0:T(8,128)S(1)} %bitcast.13, s32[4,256]{1,0:T(4,128)S(1)} %bitcast.19, f32[24,128]{1,0:T(8,128)S(1)} %bitcast.18), custom_call_target="tpu_custom_call" | custom-call | tf_op jit(solution)/shard_map/render_tiles/pallas_call | solution.py:690
  37.1 19.3 %all_to_all.16 = f32[128,1,384]{2,1,0:T(1,128)S(1)} all-to-all(f32[128,1,384]{2,1,0:T(1,128)S(1)} %bitcast.14), channel_id=1, replica_groups=mesh['cell'=128,'img'=4] {'cell'}, dimensions={0} | all-to-all | bytes 393216 | tf_op jit(solution)/shard_map/all_to_all | solution.py:736
  56.4 0.0 copy-done.3
  56.4 1.5 %owner_sums.1 = (f32[384,128]{1,0:T(8,128)S(1)}, f32[224,128]{1,0:T(8,128)S(1)}) custom-call(f32[1,3]{1,0:T(1,128)S(1)} %copy-done.3, f32[384,128]{1,0:T(8,128)S(1)} %bitcast.12, s32[32,128]{1,0:T(8,128)S(1)} %get-tuple-element.10.high_ref, bf16[256,4096]{1,0:T(8,128)(2,1)S(1)} %get-tuple-element.11.hot_ref), custom_call_target="tpu_custom_call" | custom-call | tf_op jit(solution)/shard_map/owner_sums/pallas_call | solution.py:707
  57.8 10.0 %all_to_all.17 = f32[4,1,7168]{2,1,0:T(1,128)S(1)} all-to-all(f32[4,1,7168]{2,1,0:T(1,128)S(1)} %bitcast.17), channel_id=1, replica_groups=mesh['cell'=128,'img'=4] {'img'}, dimensions={0} | all-to-all | bytes 229376 | tf_op jit(solution)/shard_map/all_to_all | solution.py:736
  67.8 0.0 copy-done
  67.8 1.2 %coeff_grads.1 = (f32[48,2048]{1,0:T(8,128)}, f32[384,128]{1,0:T(8,128)}) custom-call(f32[224,128]{1,0:T(8,128)S(1)} %bitcast.15, f32[3,8192]{1,0:T(4,128)S(1)} %copy-done, f32[384,128]{1,0:T(8,128)S(1)} %get-tuple-element.13.rows_ref), custom_call_target="tpu_custom_call" | custom-call | tf_op jit(solution)/shard_map/coeff_grads/pallas_call | solution.py:719
Async XLA Ops:
  0.6 55.7 %copy-start.3 = (f32[1,3]{1,0:T(1,128)S(1)}, f32[1,3]{1,0:T(1,128)}, u32[]{:S(2)}) copy-start(f32[1,3]{1,0:T(1,128)} %cam_ref.1) | copy-start | bytes 40
  0.6 34.1 %copy-start.1 = (f32[1,3,1024]{2,0,1:T(1,128)S(1)}, f32[1,3,1024]{2,0,1:T(1,128)}, u32[]{:S(2)}) copy-start(f32[1,3,1024]{2,0,1:T(1,128)} %param.19) | copy-start | bytes 36868
  0.7 34.1 %copy-start.5 = (s32[1,4]{1,0:T(1,128)S(1)}, s32[1,4]{1,0:T(1,128)}, u32[]{:S(2)}) copy-start(s32[1,4]{1,0:T(1,128)} %len_ref.1) | copy-start | bytes 52
  0.7 34.1 %copy-start.2 = (s32[1,4,256]{2,1,0:T(4,128)S(1)}, s32[1,4,256]{2,1,0:T(4,128)}, u32[]{:S(2)}) copy-start(s32[1,4,256]{2,1,0:T(4,128)} %param.17) | copy-start | bytes 12292
  0.7 34.1 %copy-start.4 = (s32[1,2,4]{2,1,0:T(2,128)S(1)}, s32[1,2,4]{2,1,0:T(2,128)}, u32[]{:S(2)}) copy-start(s32[1,2,4]{2,1,0:T(2,128)} %param.16) | copy-start | bytes 100
  4.1 63.8 %copy-start = (f32[3,8192]{1,0:T(4,128)S(1)}, f32[3,8192]{1,0:T(4,128)}, u32[]{:S(2)}) copy-start(f32[3,8192]{1,0:T(4,128)} %pos_ref.1) | copy-start | bytes 294916

commit v8 on v7

--- a/solution.py
+++ b/solution.py
@@ -37,6 +37,8 @@
 HIGH = 32
 PACK = 56
 NOTHING = -1.0e4
+CELL = ("y2", "y1", "y0", "z2", "z1", "z0", "core")
+ORDER = ("y0", "y1", "y2", "z0", "z1", "z2", "core")
 LOG2E = 1.4426950408889634
 EARLY = 6
 LANED = 2
@@ -181,16 +183,36 @@
     return blocks[0]
 
 
+def flipped(value, bits):
+    out = jnp.zeros_like(value)
+    for i in range(bits):
+        out = out | (((value >> i) & 1) << (bits - 1 - i))
+    return out
+
+
+def rank_of(peer):
+    return (flipped(peer >> 4, 3) << 4) | (flipped((peer >> 1) & 7, 3) << 1) | (peer & 1)
+
+
 def slot_index(idx_ref, cnt_ref, low_scr, high_scr):
-    turned = jnp.transpose(idx_ref[...].astype(F32)).astype(jnp.int32)
+    order = [int(f"{row:05b}"[::-1], 2) for row in range(32)]
+    turned = jnp.concatenate([idx_ref[row : row + 1, :] for row in order], axis=0)
+    turned = jnp.transpose(turned.astype(F32)).astype(jnp.int32)
     slots = jnp.concatenate([turned[32 * i : 32 * i + 32] for i in range(4)], axis=1)
     rows, cols = iota((PEERS, PEERS), 0), iota((PEERS, PEERS), 1)
-    perm = (rows == 4 * (cols & 31) + (cols >> 5)).astype(F32).astype(BF16)
+    perm = (rows == 4 * flipped(cols & 31, 5) + (cols >> 5)).astype(F32).astype(BF16)
     counts = jnp.broadcast_to(cnt_ref[...], (8, PEERS)).astype(F32).astype(BF16)
     counts = dot(counts, perm)[0:1].astype(jnp.int32)
     live = iota((CAP, PEERS), 0) < counts
     low_scr[...] = slots & (LOW - 1)
     high_scr[...] = jnp.where(live, slots >> 8, -1)
+
+
+def peer_blocks(k):
+    for part in range(4):
+        for group in range(4):
+            rank = ((part >> 1) << 3) | (group << 1) | (part & 1)
+            yield 32 * part + 8 * group, pl.ds(3 * rank + k, 8, stride=48)
 
 
 def pair_row(ref, base, pair):
@@ -353,8 +375,8 @@
     rows_scr[32 * COMPS :, :] = jnp.zeros((96, 128), F32)
     for k in range(3):
         turned = jnp.transpose(rows_scr[128 * k : 128 * k + 128, :])
-        for i in range(4):
-            out_ref[pl.ds(3 * i + k, 32, stride=12), :] = turned[32 * i : 32 * i + 32]
+        for at, rows in peer_blocks(k):
+            out_ref[rows, :] = turned[at : at + 8]
 
 
 def render_kernel(
@@ -369,7 +391,7 @@
         [list_ref[t : t + 1, 128 * h : 128 * h + 128] for t in range(TILES) for h in range(2)],
         axis=0,
     )
-    peer, place = slots >> 5, slots & (CAP - 1)
+    peer, place = rank_of(slots >> 5), slots & (CAP - 1)
     row_iota = iota((8, 128), 0)
 
     def by_tile(ref, row):
@@ -554,9 +576,7 @@
 
 def sum_slots(comps, back_ref, high_ref, hot_ref, rows_scr):
     for k in sorted({comp // 4 for comp in comps}):
-        block = jnp.concatenate(
-            [back_ref[pl.ds(3 * i + k, 32, stride=12), :] for i in range(4)], axis=0
-        )
+        block = jnp.concatenate([back_ref[rows, :] for _, rows in peer_blocks(k)], axis=0)
         rows_scr[128 * k : 128 * k + 128, :] = jnp.transpose(block)
     high_iota = iota((HIGH, 256), 0)
     total = None
@@ -753,11 +773,11 @@
     outgoing, high, low_hot = owner(
         camera, proj.reshape(384, 128), sh_coeffs, positions, index, send_count
     )
-    received = exchange(outgoing, "cell", PEERS)
+    received = exchange(outgoing, ORDER, PEERS)
     slot_grads = render(
         tile_xy[0], tile_len, received, tile_list[0], pixel_grad.reshape(24, 128)
     )
-    returned = exchange(slot_grads, "cell", PEERS)
+    returned = exchange(slot_grads, ORDER, PEERS)
     grad_rows, colours = sum_returned(camera, returned, high, low_hot)
     colours = exchange(colours, "img", 4)
     grad_sh, grad_rows = coefficients(colours, positions, grad_rows)
@@ -765,21 +785,22 @@
 
 
 def solution(mesh):
+    bits = jax.sharding.Mesh(mesh.devices.reshape((2,) * len(CELL) + (-1,)), CELL + ("img",))
     return jax.shard_map(
         on_device,
-        mesh=mesh,
+        mesh=bits,
         in_specs=(
-            P("img", None, "cell"),
-            P(None, "cell"),
-            P(None, "cell"),
+            P("img", None, CELL),
+            P(None, CELL),
+            P(None, CELL),
             P("img", None),
-            P("img", "cell"),
-            P("img", "cell"),
-            P("img", None, "cell"),
-            P("img", "cell", None),
-            P("img", "cell"),
-            P("img", None, "cell"),
+            P("img", CELL),
+            P("img", CELL),
+            P("img", None, CELL),
+            P("img", CELL, None),
+            P("img", CELL),
+            P("img", None, CELL),
         ),
-        out_specs=(P("img", None, "cell"), P(None, ("cell", "img"))),
+        out_specs=(P("img", None, CELL), P(None, CELL + ("img",))),
         check_vma=False,
     )

time: 69.3 us -> 68.3 us (0.986)
  blocking collectives: 59.9 us -> 59 us
    all_to_all x3, blocking collectives: 59.9 us -> 59 us  [exchange(): got = lax.all_to_all(sent, axis, split_axis=0, concat_axis=0, tiled=True)]
where the time goes in v8:
time: 68.3 us; the launch traced here: 68.1 us
  blocking collectives  59 us (86%)
  Pallas kernels  8.36 us (12%)
  between operations  0.72 us (1%)
    all_to_all x3, blocking collectives, exchange(): got = lax.all_to_all(sent, axis, split_axis=0, concat_axis=0, tiled=True)  59 us
    pallas_call x1, Pallas kernels, owner(): pl.pallas_call(owner_kernel, out_shape=(shape(384, 128), jax.ShapeDtypeSt...  3.37 us
    pallas_call x1, Pallas kernels, render(): pl.pallas_call(render_kernel, out_shape=shape(384, 128), in_specs=[VMEM]...  2.32 us
    pallas_call x1, Pallas kernels, sum_returned(): pl.pallas_call(sum_kernel, out_shape=(shape(384, 128), shape(4 * PACK, 12...  1.46 us

profile of v8, /device:TPU:8, one launch (start us, length us, event | category | flops | bytes accessed | tf_op | source)
XLA Modules:
  0.0 68.1 jit_solution(5571556126997449600)
XLA Ops:
  0.6 0.0 copy-start.3
  0.6 0.0 copy-start.1
  0.7 0.0 copy-start.5
  0.7 0.0 copy-start.2
  0.7 0.0 copy-start.4
  0.7 3.4 %owner_rows.1 = (f32[384,128]{1,0:T(8,128)S(1)}, s32[32,128]{1,0:T(8,128)S(1)}, bf16[256,4096]{1,0:T(8,128)(2,1)S(1)}) custom-call(f32[1,3]{1,0:T(1,128)} %cam_ref.1, f32[384,128]{1,0:T(8,128)} %bitcast.21, f32[48,8192]{1,0:T(8,128)} %sh_hbm.1, f32[3,8192]{1,0:T(4,128)} %pos_ref.1, s32[32,128]{1,0:T(8,128)} %bitcast.22, s32[1,128]{1,0:T(1,128)} %cnt_hbm.1), custom_call_target="tpu_custom_call" | custom-call | tf_op jit(solution)/shard_map/owner_rows/pallas_call | solution.py:683
  4.1 0.0 copy-start
  4.1 30.3 %all_to_all.15 = f32[128,1,384]{2,1,0:T(1,128)S(1)} all-to-all(f32[128,1,384]{2,1,0:T(1,128)S(1)} %bitcast.16), channel_id=1, replica_groups=mesh['y2'=2,'y1'=2,'y0'=2,'z2'=2,'z1'=2,'z0'=2,'core'=2,'img'=4] {'y0','..., dimensions={0} | all-to-all | bytes 393216 | tf_op jit(solution)/shard_map/all_to_all | solution.py:756
  34.4 0.0 copy-done.1
  34.4 0.0 copy-done.5
  34.4 0.0 copy-done.2
  34.4 0.0 copy-done.4
  34.4 2.3 %render_tiles.1 = f32[384,128]{1,0:T(8,128)S(1)} custom-call(s32[2,4]{1,0:T(2,128)S(1)} %bitcast.20, s32[1,4]{1,0:T(1,128)S(1)} %copy-done.5, f32[384,128]{1,0:T(8,128)S(1)} %bitcast.13, s32[4,256]{1,0:T(4,128)S(1)} %bitcast.19, f32[24,128]{1,0:T(8,128)S(1)} %bitcast.18), custom_call_target="tpu_custom_call" | custom-call | tf_op jit(solution)/shard_map/render_tiles/pallas_call | solution.py:710
  36.7 18.7 %all_to_all.16 = f32[128,1,384]{2,1,0:T(1,128)S(1)} all-to-all(f32[128,1,384]{2,1,0:T(1,128)S(1)} %bitcast.14), channel_id=1, replica_groups=mesh['y2'=2,'y1'=2,'y0'=2,'z2'=2,'z1'=2,'z0'=2,'core'=2,'img'=4] {'y0','..., dimensions={0} | all-to-all | bytes 393216 | tf_op jit(solution)/shard_map/all_to_all | solution.py:756
  55.4 0.0 copy-done.3
  55.4 1.5 %owner_sums.1 = (f32[384,128]{1,0:T(8,128)S(1)}, f32[224,128]{1,0:T(8,128)S(1)}) custom-call(f32[1,3]{1,0:T(1,128)S(1)} %copy-done.3, f32[384,128]{1,0:T(8,128)S(1)} %bitcast.12, s32[32,128]{1,0:T(8,128)S(1)} %get-tuple-element.10.high_ref, bf16[256,4096]{1,0:T(8,128)(2,1)S(1)} %get-tuple-element.11.hot_ref), custom_call_target="tpu_custom_call" | custom-call | tf_op jit(solution)/shard_map/owner_sums/pallas_call | solution.py:727
  56.9 10.0 %all_to_all.17 = f32[4,1,7168]{2,1,0:T(1,128)S(1)} all-to-all(f32[4,1,7168]{2,1,0:T(1,128)S(1)} %bitcast.17), channel_id=1, replica_groups=mesh['y2'=2,'y1'=2,'y0'=2,'z2'=2,'z1'=2,'z0'=2,'core'=2,'img'=4] {'img'}, dimensions={0} | all-to-all | bytes 229376 | tf_op jit(solution)/shard_map/all_to_all | solution.py:756
  66.9 0.0 copy-done
  66.9 1.2 %coeff_grads.1 = (f32[48,2048]{1,0:T(8,128)}, f32[384,128]{1,0:T(8,128)}) custom-call(f32[224,128]{1,0:T(8,128)S(1)} %bitcast.15, f32[3,8192]{1,0:T(4,128)S(1)} %copy-done, f32[384,128]{1,0:T(8,128)S(1)} %get-tuple-element.13.rows_ref), custom_call_target="tpu_custom_call" | custom-call | tf_op jit(solution)/shard_map/coeff_grads/pallas_call | solution.py:739
Async XLA Ops:
  0.6 54.8 %copy-start.3 = (f32[1,3]{1,0:T(1,128)S(1)}, f32[1,3]{1,0:T(1,128)}, u32[]{:S(2)}) copy-start(f32[1,3]{1,0:T(1,128)} %cam_ref.1) | copy-start | bytes 40
  0.6 33.7 %copy-start.1 = (f32[1,3,1024]{2,0,1:T(1,128)S(1)}, f32[1,3,1024]{2,0,1:T(1,128)}, u32[]{:S(2)}) copy-start(f32[1,3,1024]{2,0,1:T(1,128)} %param.19) | copy-start | bytes 36868
  0.7 33.7 %copy-start.5 = (s32[1,4]{1,0:T(1,128)S(1)}, s32[1,4]{1,0:T(1,128)}, u32[]{:S(2)}) copy-start(s32[1,4]{1,0:T(1,128)} %len_ref.1) | copy-start | bytes 52
  0.7 33.7 %copy-start.2 = (s32[1,4,256]{2,1,0:T(4,128)S(1)}, s32[1,4,256]{2,1,0:T(4,128)}, u32[]{:S(2)}) copy-start(s32[1,4,256]{2,1,0:T(4,128)} %param.17) | copy-start | bytes 12292
  0.7 33.7 %copy-start.4 = (s32[1,2,4]{2,1,0:T(2,128)S(1)}, s32[1,2,4]{2,1,0:T(2,128)}, u32[]{:S(2)}) copy-start(s32[1,2,4]{2,1,0:T(2,128)} %param.16) | copy-start | bytes 100
  4.1 62.8 %copy-start = (f32[3,8192]{1,0:T(4,128)S(1)}, f32[3,8192]{1,0:T(4,128)}, u32[]{:S(2)}) copy-start(f32[3,8192]{1,0:T(4,128)} %pos_ref.1) | copy-start | bytes 294916

commit v9 on v8

--- a/solution.py
+++ b/solution.py
@@ -38,7 +38,11 @@
 PACK = 56
 NOTHING = -1.0e4
 CELL = ("y2", "y1", "y0", "z2", "z1", "z0", "core")
-ORDER = ("y0", "y1", "y2", "z0", "z1", "z2", "core")
+ORDER = ("y0", "y1", "z0", "y2", "z1", "z2", "core")
+PEER_ROWS = tuple(
+    ((n >> 4) & 1) << 2 | ((n >> 3) & 1) << 3 | ((n >> 2) & 1) << 4 | ((n >> 1) & 1) | (n & 1) << 1
+    for n in range(32)
+)
 LOG2E = 1.4426950408889634
 EARLY = 6
 LANED = 2
@@ -191,16 +195,24 @@
 
 
 def rank_of(peer):
-    return (flipped(peer >> 4, 3) << 4) | (flipped((peer >> 1) & 7, 3) << 1) | (peer & 1)
+    out = jnp.zeros_like(peer)
+    for place, name in enumerate(ORDER):
+        bit = len(CELL) - 1 - CELL.index(name)
+        out = out | (((peer >> bit) & 1) << (len(ORDER) - 1 - place))
+    return out
+
+
+def peer_of(place):
+    return (flipped(place >> 2, 3) << 2) | flipped(place & 3, 2)
 
 
 def slot_index(idx_ref, cnt_ref, low_scr, high_scr):
-    order = [int(f"{row:05b}"[::-1], 2) for row in range(32)]
-    turned = jnp.concatenate([idx_ref[row : row + 1, :] for row in order], axis=0)
+    rows = [idx_ref[row : row + 1, :] for row in PEER_ROWS]
+    turned = jnp.concatenate(rows, axis=0)
     turned = jnp.transpose(turned.astype(F32)).astype(jnp.int32)
     slots = jnp.concatenate([turned[32 * i : 32 * i + 32] for i in range(4)], axis=1)
     rows, cols = iota((PEERS, PEERS), 0), iota((PEERS, PEERS), 1)
-    perm = (rows == 4 * flipped(cols & 31, 5) + (cols >> 5)).astype(F32).astype(BF16)
+    perm = (rows == 4 * peer_of(cols & 31) + (cols >> 5)).astype(F32).astype(BF16)
     counts = jnp.broadcast_to(cnt_ref[...], (8, PEERS)).astype(F32).astype(BF16)
     counts = dot(counts, perm)[0:1].astype(jnp.int32)
     live = iota((CAP, PEERS), 0) < counts
@@ -211,8 +223,8 @@
 def peer_blocks(k):
     for part in range(4):
         for group in range(4):
-            rank = ((part >> 1) << 3) | (group << 1) | (part & 1)
-            yield 32 * part + 8 * group, pl.ds(3 * rank + k, 8, stride=48)
+            rank = (group << 5) | ((part >> 1) << 4) | (part & 1)
+            yield 32 * part + 8 * group, pl.ds(3 * rank + k, 8, stride=6)
 
 
 def pair_row(ref, base, pair):

time: 68.3 us -> 70 us (1.025)
  blocking collectives: 59 us -> 60.7 us
    all_to_all x3, blocking collectives: 59 us -> 60.7 us  [exchange(): got = lax.all_to_all(sent, axis, split_axis=0, concat_axis=0, tiled=True)]
where the time goes in v9:
time: 70 us; the launch traced here: 69.8 us
  blocking collectives  60.7 us (87%)
  Pallas kernels  8.36 us (12%)
  between operations  0.72 us (1%)
    all_to_all x3, blocking collectives, exchange(): got = lax.all_to_all(sent, axis, split_axis=0, concat_axis=0, tiled=True)  60.7 us
    pallas_call x1, Pallas kernels, owner(): pl.pallas_call(owner_kernel, out_shape=(shape(384, 128), jax.ShapeDtypeSt...  3.37 us
    pallas_call x1, Pallas kernels, render(): pl.pallas_call(render_kernel, out_shape=shape(384, 128), in_specs=[VMEM]...  2.33 us
    pallas_call x1, Pallas kernels, sum_returned(): pl.pallas_call(sum_kernel, out_shape=(shape(384, 128), shape(4 * PACK, 12...  1.46 us

profile of v9, /device:TPU:8, one launch (start us, length us, event | category | flops | bytes accessed | tf_op | source)
XLA Modules:
  0.0 69.8 jit_solution(16487414697990213636)
XLA Ops:
  0.6 0.0 copy-start.3
  0.6 0.0 copy-start.1
  0.7 0.0 copy-start.5
  0.7 0.0 copy-start.2
  0.7 0.0 copy-start.4
  0.7 3.4 %owner_rows.1 = (f32[384,128]{1,0:T(8,128)S(1)}, s32[32,128]{1,0:T(8,128)S(1)}, bf16[256,4096]{1,0:T(8,128)(2,1)S(1)}) custom-call(f32[1,3]{1,0:T(1,128)} %cam_ref.1, f32[384,128]{1,0:T(8,128)} %bitcast.21, f32[48,8192]{1,0:T(8,128)} %sh_hbm.1, f32[3,8192]{1,0:T(4,128)} %pos_ref.1, s32[32,128]{1,0:T(8,128)} %bitcast.22, s32[1,128]{1,0:T(1,128)} %cnt_hbm.1), custom_call_target="tpu_custom_call" | custom-call | tf_op jit(solution)/shard_map/owner_rows/pallas_call | solution.py:695
  4.1 0.0 copy-start
  4.1 31.4 %all_to_all.15 = f32[128,1,384]{2,1,0:T(1,128)S(1)} all-to-all(f32[128,1,384]{2,1,0:T(1,128)S(1)} %bitcast.16), channel_id=1, replica_groups=mesh['y2'=2,'y1'=2,'y0'=2,'z2'=2,'z1'=2,'z0'=2,'core'=2,'img'=4] {'y0','..., dimensions={0} | all-to-all | bytes 393216 | tf_op jit(solution)/shard_map/all_to_all | solution.py:768
  35.4 0.0 copy-done.1
  35.4 0.0 copy-done.5
  35.4 0.0 copy-done.2
  35.4 0.0 copy-done.4
  35.5 2.3 %render_tiles.1 = f32[384,128]{1,0:T(8,128)S(1)} custom-call(s32[2,4]{1,0:T(2,128)S(1)} %bitcast.20, s32[1,4]{1,0:T(1,128)S(1)} %copy-done.5, f32[384,128]{1,0:T(8,128)S(1)} %bitcast.13, s32[4,256]{1,0:T(4,128)S(1)} %bitcast.19, f32[24,128]{1,0:T(8,128)S(1)} %bitcast.18), custom_call_target="tpu_custom_call" | custom-call | tf_op jit(solution)/shard_map/render_tiles/pallas_call | solution.py:722
  37.8 19.3 %all_to_all.16 = f32[128,1,384]{2,1,0:T(1,128)S(1)} all-to-all(f32[128,1,384]{2,1,0:T(1,128)S(1)} %bitcast.14), channel_id=1, replica_groups=mesh['y2'=2,'y1'=2,'y0'=2,'z2'=2,'z1'=2,'z0'=2,'core'=2,'img'=4] {'y0','..., dimensions={0} | all-to-all | bytes 393216 | tf_op jit(solution)/shard_map/all_to_all | solution.py:768
  57.1 0.0 copy-done.3
  57.1 1.5 %owner_sums.1 = (f32[384,128]{1,0:T(8,128)S(1)}, f32[224,128]{1,0:T(8,128)S(1)}) custom-call(f32[1,3]{1,0:T(1,128)S(1)} %copy-done.3, f32[384,128]{1,0:T(8,128)S(1)} %bitcast.12, s32[32,128]{1,0:T(8,128)S(1)} %get-tuple-element.10.high_ref, bf16[256,4096]{1,0:T(8,128)(2,1)S(1)} %get-tuple-element.11.hot_ref), custom_call_target="tpu_custom_call" | custom-call | tf_op jit(solution)/shard_map/owner_sums/pallas_call | solution.py:739
  58.6 10.0 %all_to_all.17 = f32[4,1,7168]{2,1,0:T(1,128)S(1)} all-to-all(f32[4,1,7168]{2,1,0:T(1,128)S(1)} %bitcast.17), channel_id=1, replica_groups=mesh['y2'=2,'y1'=2,'y0'=2,'z2'=2,'z1'=2,'z0'=2,'core'=2,'img'=4] {'img'}, dimensions={0} | all-to-all | bytes 229376 | tf_op jit(solution)/shard_map/all_to_all | solution.py:768
  68.6 0.0 copy-done
  68.6 1.2 %coeff_grads.1 = (f32[48,2048]{1,0:T(8,128)}, f32[384,128]{1,0:T(8,128)}) custom-call(f32[224,128]{1,0:T(8,128)S(1)} %bitcast.15, f32[3,8192]{1,0:T(4,128)S(1)} %copy-done, f32[384,128]{1,0:T(8,128)S(1)} %get-tuple-element.13.rows_ref), custom_call_target="tpu_custom_call" | custom-call | tf_op jit(solution)/shard_map/coeff_grads/pallas_call | solution.py:751
Async XLA Ops:
  0.6 56.5 %copy-start.3 = (f32[1,3]{1,0:T(1,128)S(1)}, f32[1,3]{1,0:T(1,128)}, u32[]{:S(2)}) copy-start(f32[1,3]{1,0:T(1,128)} %cam_ref.1) | copy-start | bytes 40
  0.6 34.8 %copy-start.1 = (f32[1,3,1024]{2,0,1:T(1,128)S(1)}, f32[1,3,1024]{2,0,1:T(1,128)}, u32[]{:S(2)}) copy-start(f32[1,3,1024]{2,0,1:T(1,128)} %param.19) | copy-start | bytes 36868
  0.7 34.8 %copy-start.5 = (s32[1,4]{1,0:T(1,128)S(1)}, s32[1,4]{1,0:T(1,128)}, u32[]{:S(2)}) copy-start(s32[1,4]{1,0:T(1,128)} %len_ref.1) | copy-start | bytes 52
  0.7 34.8 %copy-start.2 = (s32[1,4,256]{2,1,0:T(4,128)S(1)}, s32[1,4,256]{2,1,0:T(4,128)}, u32[]{:S(2)}) copy-start(s32[1,4,256]{2,1,0:T(4,128)} %param.17) | copy-start | bytes 12292
  0.7 34.8 %copy-start.4 = (s32[1,2,4]{2,1,0:T(2,128)S(1)}, s32[1,2,4]{2,1,0:T(2,128)}, u32[]{:S(2)}) copy-start(s32[1,2,4]{2,1,0:T(2,128)} %param.16) | copy-start | bytes 100
  4.1 64.5 %copy-start = (f32[3,8192]{1,0:T(4,128)S(1)}, f32[3,8192]{1,0:T(4,128)}, u32[]{:S(2)}) copy-start(f32[3,8192]{1,0:T(4,128)} %pos_ref.1) | copy-start | bytes 294916

commit v10 on v8

--- a/solution.py
+++ b/solution.py
@@ -38,7 +38,7 @@
 PACK = 56
 NOTHING = -1.0e4
 CELL = ("y2", "y1", "y0", "z2", "z1", "z0", "core")
-ORDER = ("y0", "y1", "y2", "z0", "z1", "z2", "core")
+ORDER = ("y0", "y1", "y2", "z0", "z2", "z1", "core")
 LOG2E = 1.4426950408889634
 EARLY = 6
 LANED = 2
@@ -191,7 +191,8 @@
 
 
 def rank_of(peer):
-    return (flipped(peer >> 4, 3) << 4) | (flipped((peer >> 1) & 7, 3) << 1) | (peer & 1)
+    low = ((peer >> 1) & 1) << 3 | ((peer >> 3) & 1) << 2 | ((peer >> 2) & 1) << 1 | (peer & 1)
+    return (flipped(peer >> 4, 3) << 4) | low
 
 
 def slot_index(idx_ref, cnt_ref, low_scr, high_scr):
@@ -211,7 +212,7 @@
 def peer_blocks(k):
     for part in range(4):
         for group in range(4):
-            rank = ((part >> 1) << 3) | (group << 1) | (part & 1)
+            rank = ((part >> 1) << 3) | ((group & 1) << 2) | ((group >> 1) << 1) | (part & 1)
             yield 32 * part + 8 * group, pl.ds(3 * rank + k, 8, stride=48)
 
 

time: 68.3 us -> 67.9 us (level)
  the two profiles are of different devices: /device:TPU:8 before, /device:TPU:16 now
where the time goes in v10:
time: 67.9 us; the launch traced here: 67.6 us
  blocking collectives  58.5 us (86%)
  Pallas kernels  8.37 us (12%)
  between operations  0.72 us (1%)
    all_to_all x3, blocking collectives, exchange(): got = lax.all_to_all(sent, axis, split_axis=0, concat_axis=0, tiled=True)  58.5 us
    pallas_call x1, Pallas kernels, owner(): pl.pallas_call(owner_kernel, out_shape=(shape(384, 128), jax.ShapeDtypeSt...  3.39 us
    pallas_call x1, Pallas kernels, render(): pl.pallas_call(render_kernel, out_shape=shape(384, 128), in_specs=[VMEM]...  2.33 us
    pallas_call x1, Pallas kernels, sum_returned(): pl.pallas_call(sum_kernel, out_shape=(shape(384, 128), shape(4 * PACK, 12...  1.46 us

profile of v10, /device:TPU:16, one launch (start us, length us, event | category | flops | bytes accessed | tf_op | source)
XLA Modules:
  0.0 67.6 jit_solution(18117060213469004195)
XLA Ops:
  0.6 0.0 copy-start.3
  0.6 0.0 copy-start.1
  0.7 0.0 copy-start.5
  0.7 0.0 copy-start.2
  0.7 0.0 copy-start.4
  0.7 3.4 %owner_rows.1 = (f32[384,128]{1,0:T(8,128)S(1)}, s32[32,128]{1,0:T(8,128)S(1)}, bf16[256,4096]{1,0:T(8,128)(2,1)S(1)}) custom-call(f32[1,3]{1,0:T(1,128)} %cam_ref.1, f32[384,128]{1,0:T(8,128)} %bitcast.21, f32[48,8192]{1,0:T(8,128)} %sh_hbm.1, f32[3,8192]{1,0:T(4,128)} %pos_ref.1, s32[32,128]{1,0:T(8,128)} %bitcast.22, s32[1,128]{1,0:T(1,128)} %cnt_hbm.1), custom_call_target="tpu_custom_call" | custom-call | tf_op jit(solution)/shard_map/owner_rows/pallas_call | solution.py:684
  4.1 0.0 copy-start
  4.1 29.9 %all_to_all.15 = f32[128,1,384]{2,1,0:T(1,128)S(1)} all-to-all(f32[128,1,384]{2,1,0:T(1,128)S(1)} %bitcast.16), channel_id=1, replica_groups=mesh['y2'=2,'y1'=2,'y0'=2,'z2'=2,'z1'=2,'z0'=2,'core'=2,'img'=4] {'y0','..., dimensions={0} | all-to-all | bytes 393216 | tf_op jit(solution)/shard_map/all_to_all | solution.py:757
  34.0 0.0 copy-done.1
  34.0 0.0 copy-done.5
  34.0 0.0 copy-done.2
  34.0 0.0 copy-done.4
  34.0 2.3 %render_tiles.1 = f32[384,128]{1,0:T(8,128)S(1)} custom-call(s32[2,4]{1,0:T(2,128)S(1)} %bitcast.20, s32[1,4]{1,0:T(1,128)S(1)} %copy-done.5, f32[384,128]{1,0:T(8,128)S(1)} %bitcast.13, s32[4,256]{1,0:T(4,128)S(1)} %bitcast.19, f32[24,128]{1,0:T(8,128)S(1)} %bitcast.18), custom_call_target="tpu_custom_call" | custom-call | tf_op jit(solution)/shard_map/render_tiles/pallas_call | solution.py:711
  36.4 18.6 %all_to_all.16 = f32[128,1,384]{2,1,0:T(1,128)S(1)} all-to-all(f32[128,1,384]{2,1,0:T(1,128)S(1)} %bitcast.14), channel_id=1, replica_groups=mesh['y2'=2,'y1'=2,'y0'=2,'z2'=2,'z1'=2,'z0'=2,'core'=2,'img'=4] {'y0','..., dimensions={0} | all-to-all | bytes 393216 | tf_op jit(solution)/shard_map/all_to_all | solution.py:757
  55.0 0.0 copy-done.3
  55.0 1.5 %owner_sums.1 = (f32[384,128]{1,0:T(8,128)S(1)}, f32[224,128]{1,0:T(8,128)S(1)}) custom-call(f32[1,3]{1,0:T(1,128)S(1)} %copy-done.3, f32[384,128]{1,0:T(8,128)S(1)} %bitcast.12, s32[32,128]{1,0:T(8,128)S(1)} %get-tuple-element.10.high_ref, bf16[256,4096]{1,0:T(8,128)(2,1)S(1)} %get-tuple-element.11.hot_ref), custom_call_target="tpu_custom_call" | custom-call | tf_op jit(solution)/shard_map/owner_sums/pallas_call | solution.py:728
  56.4 10.0 %all_to_all.17 = f32[4,1,7168]{2,1,0:T(1,128)S(1)} all-to-all(f32[4,1,7168]{2,1,0:T(1,128)S(1)} %bitcast.17), channel_id=1, replica_groups=mesh['y2'=2,'y1'=2,'y0'=2,'z2'=2,'z1'=2,'z0'=2,'core'=2,'img'=4] {'img'}, dimensions={0} | all-to-all | bytes 229376 | tf_op jit(solution)/shard_map/all_to_all | solution.py:757
  66.4 0.0 copy-done
  66.4 1.2 %coeff_grads.1 = (f32[48,2048]{1,0:T(8,128)}, f32[384,128]{1,0:T(8,128)}) custom-call(f32[224,128]{1,0:T(8,128)S(1)} %bitcast.15, f32[3,8192]{1,0:T(4,128)S(1)} %copy-done, f32[384,128]{1,0:T(8,128)S(1)} %get-tuple-element.13.rows_ref), custom_call_target="tpu_custom_call" | custom-call | tf_op jit(solution)/shard_map/coeff_grads/pallas_call | solution.py:740
Async XLA Ops:
  0.6 54.3 %copy-start.3 = (f32[1,3]{1,0:T(1,128)S(1)}, f32[1,3]{1,0:T(1,128)}, u32[]{:S(2)}) copy-start(f32[1,3]{1,0:T(1,128)} %cam_ref.1) | copy-start | bytes 40
  0.6 33.4 %copy-start.1 = (f32[1,3,1024]{2,0,1:T(1,128)S(1)}, f32[1,3,1024]{2,0,1:T(1,128)}, u32[]{:S(2)}) copy-start(f32[1,3,1024]{2,0,1:T(1,128)} %param.19) | copy-start | bytes 36868
  0.7 33.4 %copy-start.5 = (s32[1,4]{1,0:T(1,128)S(1)}, s32[1,4]{1,0:T(1,128)}, u32[]{:S(2)}) copy-start(s32[1,4]{1,0:T(1,128)} %len_ref.1) | copy-start | bytes 52
  0.7 33.4 %copy-start.2 = (s32[1,4,256]{2,1,0:T(4,128)S(1)}, s32[1,4,256]{2,1,0:T(4,128)}, u32[]{:S(2)}) copy-start(s32[1,4,256]{2,1,0:T(4,128)} %param.17) | copy-start | bytes 12292
  0.7 33.4 %copy-start.4 = (s32[1,2,4]{2,1,0:T(2,128)S(1)}, s32[1,2,4]{2,1,0:T(2,128)}, u32[]{:S(2)}) copy-start(s32[1,2,4]{2,1,0:T(2,128)} %param.16) | copy-start | bytes 100
  4.1 62.3 %copy-start = (f32[3,8192]{1,0:T(4,128)S(1)}, f32[3,8192]{1,0:T(4,128)}, u32[]{:S(2)}) copy-start(f32[3,8192]{1,0:T(4,128)} %pos_ref.1) | copy-start | bytes 294916
